TPU v7x, 32 devices: a whole 2x2x4 slice. The times are simulated.
32 devices in a mesh: group: 2 (over y), state: 8 (over z, x), sample: 2 (over core).
Axes of the slice: x: 2, y: 2, z: 4, core: 2. Of those that a mesh axis runs over, the one named last changes fastest.
Arguments:
- energies: float32 [512, 65536], P(('group', 'state'), 'sample'), parts along dimension 0, may hold values from -300 to 8
- counts: int32 [512], P(('group', 'state')), parts along dimension 0, may hold values from 1 to 256
- labels: int32 [131072], P(('group', 'sample')), parts along dimension 0, may hold values from 0 to 255
- free_energy: float32 [512], P(('group', 'state')), parts along dimension 0, may hold values from -6 to 6
- directions: float32 [2, 512], P(None, ('group', 'state')), parts along dimension 1, may hold values from -6 to 6
Outputs:
- log_norm: float32 [131072], P(('group', 'sample')), parts along dimension 0
- anchor_logp: float32 [131072], P(('group', 'sample')), parts along dimension 0
- gradient: float32 [512], P(('group', 'state')), parts along dimension 0
- hessian_products: float32 [2, 512], P(None, ('group', 'state')), parts along dimension 1
There are 2 independent parts, one for each index of `group`. A program takes and returns all parts, laid end to end along the dimension named above; each array names one. Nothing has to cross between parts.
All inputs are finite; a program needn't handle non-finite values.
Results may differ from a plain program's by a relative error of at most 0.0003.
Values sent between devices are 32-bit elements; how exact they have to be, the bound alone decides.
No kernel may reach another device: no remote copies, remote signals or barrier semaphores. Data moves between devices by JAX's collectives and lax.ppermute only.
A program may use at most 64 MiB of HBM per device.

v0:
```python
import jax
import jax.numpy as jnp
from jax import lax
from jax.sharding import PartitionSpec as P


def mix_states(directions, weights):
    mixed_part = jnp.dot(directions, weights, precision=lax.Precision.HIGHEST)
    return lax.psum(mixed_part, "state")


def local(energies, counts, labels, free_energy, directions):
    state_dev = energies.shape[0]
    samp_dev = energies.shape[1]
    width = lax.axis_size("state")
    base = jnp.log(counts.astype(jnp.float32)) + free_energy
    first_state = lax.axis_index("state") * state_dev
    state_ids = first_state + jnp.arange(state_dev, dtype=jnp.int32)
    matches = state_ids[:, None] == labels[None, :]
    tally = jnp.sum(matches.astype(jnp.float32), axis=1)
    shifted = base[:, None] - energies
    local_max = jnp.max(shifted, axis=0)
    anchor_part = jnp.sum(jnp.where(matches, shifted, 0.0), axis=0)
    peak = lax.pmax(local_max, "state")
    local_total = jnp.sum(jnp.exp(shifted - peak[None, :]), axis=0)
    total, anchor_term = lax.psum((local_total, anchor_part), "state")
    log_norm = peak + jnp.log(total)
    weights = jnp.exp(shifted - log_norm[None, :])
    mixed = mix_states(directions, weights)
    occupancy = jnp.sum(weights, axis=1)
    curvature = directions * occupancy[None, :] - jnp.einsum(
        "jn,kn->jk", mixed, weights, precision=lax.Precision.HIGHEST
    )
    summed = lax.psum(jnp.concatenate([(occupancy - tally)[None, :], curvature], axis=0), "sample")
    scale = state_dev * width / (samp_dev * lax.axis_size("sample"))
    anchor_logp = anchor_term - log_norm
    return (log_norm, anchor_logp, scale * summed[0], scale * summed[1:3])


def solution(mesh):
    return jax.shard_map(
        local,
        mesh=mesh,
        in_specs=(
            P(("group", "state"), "sample"),
            P(("group", "state")),
            P(("group", "sample")),
            P(("group", "state")),
            P(None, ("group", "state")),
        ),
        out_specs=(
            P(("group", "sample")),
            P(("group", "sample")),
            P(("group", "state")),
            P(None, ("group", "state")),
        ),
        check_vma=False,
    )
```

profile of v0, /device:TPU:0, one launch (start us, length us, event | category | flops | bytes accessed | tf_op | source)
XLA Modules:
  0.0 255.5 jit_solution(8633727544877507309)
XLA Ops:
  7.2 0.0 all-reduce.5.cloned.1.call-start
  7.2 0.7 log_add_fusion.1
  7.9 0.0 copy-start.5
  7.9 3.4 %subtract_reduce_fusion = f32[32768]{0:T(1024)} fusion(f32[32,32768]{1,0:T(8,128)} %param.5, f32[32]{0:T(128)S(1)} %log_add_fusion.1), kind=kLoop, calls=%fused_computation.7 | loop fusion | flops 2064384 | bytes 4325504 | tf_op jit(solution)/shard_map/reduce_max | solution.py:22
  11.3 0.0 all-reduce.5.cloned.1.call-update
  11.3 0.0 copy-start.3
  11.3 0.0 all-reduce.7.cloned.1.call-start
  11.4 73.1 %all-reduce.5.cloned.1.call-done = f32[32768]{0:T(1024)} async-done(((f32[32768]{0:T(1024)}), f32[32768]{0:T(1024)}) %all-reduce.5.cloned.1.call-update) | async-done | bytes 131088 | tf_op jit(solution)/shard_map/pmax | solution.py:24
  84.5 0.0 copy-start.2
  84.5 3.8 %exponential_reduce_fusion = f32[32768]{0:T(1024)} fusion(f32[32,32768]{1,0:T(8,128)} %param.5, f32[32768]{0:T(1024)} %all-reduce.5.cloned.1.call-done, f32[32]{0:T(128)S(1)} %log_add_fusion.1), kind=kLoop, calls=%fused_computation.6 | loop fusion | flops 3112960 | bytes 4456576 | tf_op jit(solution)/shard_map/reduce_sum | solution.py:25
  88.3 0.0 all-reduce.7.cloned.1.call-update
  88.3 0.0 all-reduce.9.cloned.1.call-start
  88.4 69.4 %all-reduce.7.cloned.1.call-done = f32[32768]{0:T(1024)} async-done(((f32[32768]{0:T(1024)}), f32[32768]{0:T(1024)}) %all-reduce.7.cloned.1.call-update) | async-done | bytes 131088 | tf_op jit(solution)/shard_map/psum | solution.py:26
  157.8 0.0 copy-done.2
  157.8 0.0 copy-start
  157.8 1.1 log_add_fusion
  158.9 0.0 copy-done.5
  158.9 0.0 copy-start.1
  158.9 6.0 %convolution_bitcast_fusion = f32[2,32768]{1,0:T(2,128)} fusion(f32[2,32]{1,0:T(2,128)S(1)} %copy-done.5, f32[32,32768]{1,0:T(8,128)} %param.5, f32[32768]{0:T(1024)S(1)} %log_add_fusion, f32[32]{0:T(128)S(1)} %log_add_fusion.1), kind=kOutput, calls=%fused_computation | convolution fusion | flops 27262976 | bytes 4587904 | tf_op jit(solution)/shard_map/dot_general | solution.py:8
  164.9 0.0 copy-done.3
  164.9 0.0 copy-done
  164.9 3.1 %fusion.3 = (f32[32]{0:T(128)S(1)}, f32[32768]{0:T(1024)}, f32[32]{0:T(128)S(1)}) fusion(f32[32,32768]{1,0:T(8,128)S(1)} %copy-done, f32[32768]{0:T(1024)S(1)} %log_add_fusion, f32[32]{0:T(128)S(1)} %log_add_fusion.1, s32[32768]{0:T(1024)S(1)} %copy-done.3, s32[32]{0:T(128)S(1)} %iota_add_fusion), kind=kLoop, calls=%fused_computation.9 | loop fusion | flops 8355776 | bytes 4588032 | tf_op jit(solution)/shard_map/reduce_sum | solution.py:30
  168.0 0.0 all-reduce.9.cloned.1.call-update
  168.0 70.9 %all-reduce.9.cloned.1.call-done = (f32[32768]{0:T(1024)}, f32[2,32768]{1,0:T(2,128)}) async-done(((f32[32768]{0:T(1024)}, f32[2,32768]{1,0:T(2,128)}), (f32[32768]{0:T(1024)}, f32[2,32768]{1,0:T(2,128)})) %all-reduce.9.cloned.1.call-update) | async-done | bytes 393232 | tf_op jit(solution)/shard_map/psum | solution.py:26
  238.9 0.0 copy-start.4
  238.9 5.8 %fusion.8 = f32[2,32]{1,0:T(2,128)S(1)} fusion(f32[2,32768]{1,0:T(2,128)} %get-tuple-element.8, f32[32,32768]{1,0:T(8,128)} %param.5, f32[32768]{0:T(1024)S(1)} %log_add_fusion, f32[32]{0:T(128)S(1)} %log_add_fusion.1, f32[2,32]{1,0:T(2,128)S(1)} %copy-done.5, f32[32]{0:T(128)S(1)} %get-tuple-element.4), kind=kOutput, calls=%fused_computation.14 | convolution fusion | flops 27263104 | bytes 4588288 | tf_op jit(solution)/shard_map/jn,kn->jk/dot_general | solution.py:31
  244.7 2.5 psum.31
  247.2 0.5 multiply_bitcast_fusion
  247.7 0.6 slice_multiply_fusion
  248.3 0.0 copy-done.1
  248.3 0.0 copy-done.4
  248.3 0.7 sub.47
  (3 shorter events, 0.0 us)
Async XLA Ops:
  7.2 77.3 %all-reduce.5.cloned.1.call-start = ((), (), s32[]{:S(2)}) async-start(), calls=%async_computation | async-start | bytes 262144 | tf_op jit(solution)/shard_map/pmax | solution.py:24
  7.9 151.0 %copy-start.5 = (f32[2,32]{1,0:T(2,128)S(1)}, f32[2,32]{1,0:T(2,128)}, u32[]{:S(2)}) copy-start(f32[2,32]{1,0:T(2,128)} %param.9) | copy-start | bytes 772
  11.3 153.6 %copy-start.3 = (s32[32768]{0:T(1024)S(1)}, s32[32768]{0:T(1024)}, u32[]{:S(2)}) copy-start(s32[32768]{0:T(1024)} %param.7) | copy-start | bytes 393220
  11.3 146.4 %all-reduce.7.cloned.1.call-start = ((), (), s32[]{:S(2)}) async-start(), calls=%async_computation.1 | async-start | bytes 262144 | tf_op jit(solution)/shard_map/psum | solution.py:26
  84.5 73.3 %copy-start.2 = (f32[32768]{0:T(1024)S(1)}, f32[32768]{0:T(1024)}, u32[]{:S(2)}) copy-start(f32[32768]{0:T(1024)} %all-reduce.5.cloned.1.call-done) | copy-start | bytes 393220
  88.3 150.6 %all-reduce.9.cloned.1.call-start = ((), (), s32[]{:S(2)}) async-start(), calls=%async_computation.2 | async-start | bytes 786432 | tf_op jit(solution)/shard_map/psum | solution.py:26
  157.8 7.1 %copy-start = (f32[32,32768]{1,0:T(8,128)S(1)}, f32[32,32768]{1,0:T(8,128)}, u32[]{:S(2)}) copy-start(f32[32,32768]{1,0:T(8,128)} %param.5) | copy-start | bytes 12582916
  158.9 89.4 %copy-start.1 = (f32[32768]{0:T(1024)}, f32[32768]{0:T(1024)S(1)}, u32[]{:S(2)}) copy-start(f32[32768]{0:T(1024)S(1)} %log_add_fusion) | copy-start | bytes 393220
  238.9 9.4 %copy-start.4 = (f32[32768]{0:T(1024)S(1)}, f32[32768]{0:T(1024)}, u32[]{:S(2)}) copy-start(f32[32768]{0:T(1024)} %get-tuple-element.7) | copy-start | bytes 393220
Sparse Core Ops, SparseCore 0:
  11.9 72.4 all-reduce.4
  88.8 68.9 all-reduce.6
  168.1 70.7 all-reduce.8
where the time goes:
time: 256 us; the launch traced here: 255 us
  waiting for transfers between devices  213 us (83%)
  other arithmetic  13.9 us (5%)
  between operations  13.8 us (5%)
  matrix products  11.8 us (5%)
    psum x2, waiting for transfers between devices, local(): total, anchor_term = lax.psum((local_total, anchor_part), 'state')  140 us
    pmax x1, waiting for transfers between devices, local(): peak = lax.pmax(local_max, 'state')  73.1 us
    dot_general x1, matrix products, mix_states(): mixed_part = jnp.dot(directions, weights, precision=lax.Precision.HIGHEST)  5.99 us
    dot_general x1, matrix products, local(): jnp.einsum('jn,kn->jk', mixed, weights, precision=lax.Precision.HIGHEST)  5.79 us
  transfers between devices with their start and end apart: 3, of which 3 were waited for; matrix products, arithmetic and copies ran while one was open for 0% of the time, Pallas kernels for 0%

commit v1 on v0

v1 whole, which is shorter than its diff:
```python
import functools
import math

import jax
import jax.numpy as jnp
from jax import lax
from jax.experimental import pallas as pl
from jax.experimental.pallas import tpu as pltpu
from jax.sharding import PartitionSpec as P

LANES = 128
ROWS = 8
TILE = LANES * ROWS


def plan(level, shift):
    if level == 0:
        return [0] * ROWS, 1
    half = ROWS >> level
    first, count = plan(level - 1, shift)
    second, _ = plan(level - 1, shift - half)
    owner = []
    for row in range(ROWS):
        keep = ((row - shift) // half) % 2 == 1
        owner.append(first[row] if keep else second[row] + count)
    return owner, 2 * count


PLACE, _ = plan(3, 0)


def fold(leaf, combine, rows, level=3, shift=0, first=0):
    if level == 0:
        return leaf(PLACE.index(first))
    half = ROWS >> level
    count = 1 << (level - 1)
    a = fold(leaf, combine, rows, level - 1, shift, first)
    b = fold(leaf, combine, rows, level - 1, shift - half, first + count)
    keep = (((rows - shift + 2 * ROWS) // half) % 2) == 1
    out = []
    for one, two, how in zip(a, b, combine, strict=True):
        mine = jnp.where(keep, one, two)
        other = jnp.where(keep, two, one)
        out.append(how(mine, pltpu.roll(other, half, 0)))
    return tuple(out)


def column(row, states):
    spread = jnp.broadcast_to(row, (states, states))
    eye = lax.broadcasted_iota(jnp.int32, (states, states), 0) == lax.broadcasted_iota(jnp.int32, (states, states), 1)
    picked = jnp.sum(jnp.where(eye, spread, 0.0), axis=1, keepdims=True)
    return jnp.broadcast_to(picked, (states, LANES))


def bases(counts_ref, free_ref, states):
    return column(jnp.log(counts_ref[...].astype(jnp.float32)) + free_ref[...], states)


def over_tiles(x, how):
    parts = [x[i * ROWS : (i + 1) * ROWS] for i in range(x.shape[0] // ROWS)]
    return functools.reduce(how, parts)


def local_body(spots_ref, counts_ref, free_ref, dirs_ref, labels_ref, energies_ref, *refs):
    *out_refs, tally_ref, base_s, dir_s = refs
    states = energies_ref.shape[0]
    steps = energies_ref.shape[1] // TILE
    number = pl.program_id(0)

    @pl.when(number == 0)
    def _():
        base_s[...] = bases(counts_ref, free_ref, states)
        dir_s[0] = column(dirs_ref[0:1, :], states)
        dir_s[1] = column(dirs_ref[1:2, :], states)
        tally_ref[...] = jnp.zeros_like(tally_ref)

    rows = lax.broadcasted_iota(jnp.int32, (ROWS, LANES), 0)
    ids = lax.broadcasted_iota(jnp.int32, (states, LANES), 0)
    first_state = spots_ref[4]

    def step(out_ref, j, tally):
        at = pl.multiple_of(j * ROWS, ROWS)
        labels = labels_ref[pl.ds(at, ROWS), :] - first_state
        base = base_s[...]

        def shifted(g):
            cols = pl.ds(pl.multiple_of(j * TILE + g * LANES, LANES), LANES)
            return base - energies_ref[:, cols]

        (peak,) = fold(lambda g: (over_tiles(shifted(g), jnp.maximum),), (jnp.maximum,), rows)
        matched = []

        def leaf(g):
            s = shifted(g)
            e = jnp.exp(s - jnp.broadcast_to(peak[g : g + 1, :], (states, LANES)))
            match = ids == jnp.broadcast_to(labels[g : g + 1, :], (states, LANES))
            matched.append(match.astype(jnp.float32))
            return (
                over_tiles(e, jnp.add),
                over_tiles(e * dir_s[0], jnp.add),
                over_tiles(e * dir_s[1], jnp.add),
                over_tiles(jnp.where(match, s, 0.0), jnp.add),
            )

        total, mix0, mix1, anchor = fold(leaf, (jnp.add,) * 4, rows)
        inverse = 1.0 / total
        out_ref[0, pl.ds(at, ROWS), :] = peak + jnp.log(total)
        out_ref[1, pl.ds(at, ROWS), :] = mix0 * inverse
        out_ref[2, pl.ds(at, ROWS), :] = mix1 * inverse
        out_ref[3, pl.ds(at, ROWS), :] = anchor
        return tally + functools.reduce(jnp.add, matched)

    for k, out_ref in enumerate(out_refs):

        @pl.when(number == k)
        def _():
            tally_ref[...] += lax.fori_loop(
                0, steps, functools.partial(step, out_ref), jnp.zeros((states, LANES), jnp.float32)
            )


def local_sums(spots, which, counts, free_energy, directions, labels, energies):
    states, samples = energies.shape
    width = samples // 4
    n = len(which)
    lo = which[0]
    whole = pl.BlockSpec(memory_space=pltpu.VMEM)
    part = jax.ShapeDtypeStruct((4, width // LANES, LANES), jnp.float32)
    fixed = pl.BlockSpec((4, width // LANES, LANES), lambda i, s: (0, 0, 0))
    return pl.pallas_call(
        local_body,
        grid_spec=pltpu.PrefetchScalarGridSpec(
            num_scalar_prefetch=1,
            grid=(n,),
            in_specs=[
                pl.BlockSpec((1, states), lambda i, s: (0, 0)),
                pl.BlockSpec((1, states), lambda i, s: (0, 0)),
                pl.BlockSpec((2, states), lambda i, s: (0, 0)),
                pl.BlockSpec((width // LANES, LANES), lambda i, s: (s[lo + i], 0)),
                pl.BlockSpec((states, width), lambda i, s: (0, s[lo + i])),
            ],
            out_specs=[fixed] * n + [pl.BlockSpec((states, LANES), lambda i, s: (0, 0))],
            scratch_shapes=[pltpu.VMEM((states, LANES), jnp.float32), pltpu.VMEM((2, states, LANES), jnp.float32)],
        ),
        out_shape=[part] * n + [jax.ShapeDtypeStruct((states, LANES), jnp.float32)],
        compiler_params=pltpu.CompilerParams(vmem_limit_bytes=24 * 1024 * 1024),
        cost_estimate=pl.CostEstimate(
            flops=20 * n * states * width, bytes_accessed=4 * n * states * width, transcendentals=n * states * width
        ),
        name="local_sums",
    )(
        spots,
        counts.reshape(1, states),
        free_energy.reshape(1, states),
        directions,
        labels.reshape(samples // LANES, LANES),
        energies,
    )


def curve_body(spots_ref, counts_ref, free_ref, dirs_ref, energies_ref, *refs):
    n = len(refs) - 5
    part_refs = refs[:n]
    norm_ref, anchor_ref, sums_ref, base_s, acc_s = refs[n:]
    states = energies_ref.shape[0]
    steps = energies_ref.shape[1] // TILE
    number = pl.program_id(0)

    @pl.when(number == 0)
    def _():
        base_s[...] = bases(counts_ref, free_ref, states)
        acc_s[...] = jnp.zeros_like(acc_s)

    def step(part_ref, j, carry):
        occupancy, mix0, mix1 = carry
        at = pl.multiple_of(j * ROWS, ROWS)
        norm = part_ref[0, pl.ds(at, ROWS), :]
        norm_ref[pl.ds(at, ROWS), :] = norm
        anchor_ref[pl.ds(at, ROWS), :] = part_ref[3, pl.ds(at, ROWS), :] - norm
        first = part_ref[1, pl.ds(at, ROWS), :]
        second = part_ref[2, pl.ds(at, ROWS), :]
        base = base_s[...]
        for g in range(ROWS):
            cols = pl.ds(pl.multiple_of(j * TILE + g * LANES, LANES), LANES)
            spread = lambda x: jnp.broadcast_to(x[g : g + 1, :], (states, LANES))
            w = jnp.exp((base - energies_ref[:, cols]) - spread(norm))
            occupancy += w
            mix0 += w * spread(first)
            mix1 += w * spread(second)
        return occupancy, mix0, mix1

    for k, part_ref in enumerate(part_refs):

        @pl.when(number == k)
        def _():
            zero = jnp.zeros((states, LANES), jnp.float32)
            occupancy, mix0, mix1 = lax.fori_loop(0, steps, functools.partial(step, part_ref), (zero, zero, zero))
            acc_s[0] += occupancy
            acc_s[1] += mix0
            acc_s[2] += mix1

    @pl.when(number == n - 1)
    def _():
        sums_ref[...] = acc_s[...]


def curve_sums(spots, which, parts, counts, free_energy, directions, energies, outs):
    states, samples = energies.shape
    width = samples // 4
    n = len(which)
    lo = which[0]
    body = curve_body
    whole = pl.BlockSpec((4, width // LANES, LANES), lambda i, s: (0, 0, 0))
    quarter = pl.BlockSpec((width // LANES, LANES), lambda i, s: (s[lo + i], 0))
    in_specs = [
        pl.BlockSpec((1, states), lambda i, s: (0, 0)),
        pl.BlockSpec((1, states), lambda i, s: (0, 0)),
        pl.BlockSpec((2, states), lambda i, s: (0, 0)),
        pl.BlockSpec((states, width), lambda i, s: (0, s[lo + i])),
    ] + [whole] * n
    args = [
        spots,
        counts.reshape(1, states),
        free_energy.reshape(1, states),
        directions,
        energies,
        *parts,
    ]
    aliases = {}
    if outs is not None:
        in_specs = in_specs + [pl.BlockSpec(memory_space=pl.ANY)] * 2
        aliases = {len(args): 0, len(args) + 1: 1}
        args += list(outs)

        def body(*refs):
            head = 5 + n
            return curve_body(*refs[:head], *refs[head + 2 :])

    long = jax.ShapeDtypeStruct((samples // LANES, LANES), jnp.float32)
    return pl.pallas_call(
        body,
        grid_spec=pltpu.PrefetchScalarGridSpec(
            num_scalar_prefetch=1,
            grid=(n,),
            in_specs=in_specs,
            out_specs=[quarter, quarter, pl.BlockSpec((3, states, LANES), lambda i, s: (0, 0, 0))],
            scratch_shapes=[pltpu.VMEM((states, LANES), jnp.float32), pltpu.VMEM((3, states, LANES), jnp.float32)],
        ),
        out_shape=[long, long, jax.ShapeDtypeStruct((3, states, LANES), jnp.float32)],
        input_output_aliases=aliases,
        compiler_params=pltpu.CompilerParams(vmem_limit_bytes=24 * 1024 * 1024),
        cost_estimate=pl.CostEstimate(
            flops=9 * n * states * width, bytes_accessed=4 * n * states * width, transcendentals=n * states * width
        ),
        name="curve_sums",
    )(*args)


def merge(parts):
    norms = [part[0:1] for part in parts]
    peak = functools.reduce(jnp.maximum, norms)
    scales = [jnp.exp(norm - peak) for norm in norms]
    total = functools.reduce(jnp.add, scales)
    mixed = functools.reduce(jnp.add, [s * part for s, part in zip(scales, parts, strict=True)]) / total
    anchor = functools.reduce(jnp.add, parts)
    kind = lax.broadcasted_iota(jnp.int32, parts[0].shape, 0)
    return jnp.where(kind == 0, peak + jnp.log(total), jnp.where(kind == 3, anchor, mixed))


def swap(x, width, cores, flips):
    pairs = []
    for place in range(width):
        for core in range(cores):
            pairs.append((place * cores + core, (place ^ flips[core]) * cores + core))
    return lax.ppermute(x, ("state", "sample"), pairs)


def local(energies, counts, labels, free_energy, directions):
    states, samples = energies.shape
    width, cores = lax.axis_size("state"), lax.axis_size("sample")
    place, core = lax.axis_index("state"), lax.axis_index("sample")
    rounds = [[3] * cores, [1 + c % 2 for c in range(cores)], [2 - c % 2 for c in range(cores)]]
    mine = place % 4
    turn = core % 2
    spots = jnp.stack([mine ^ 3, mine ^ (1 + turn), mine ^ (2 - turn), mine, place * states]).astype(jnp.int32)

    *sent, tally_a = local_sums(spots, (0, 1, 2), counts, free_energy, directions, labels, energies)
    got = [swap(x, width, cores, flips) for x, flips in zip(sent, rounds, strict=True)]
    own, tally_b = local_sums(spots, (3,), counts, free_energy, directions, labels, energies)
    part = merge([own, *got])
    for far in range(2, int(math.log2(width))):
        part = merge([part, swap(part, width, cores, [1 << far] * cores)])
    others = [swap(part, width, cores, flips) for flips in rounds]
    *outs, sums_a = curve_sums(spots, (3,), [part], counts, free_energy, directions, energies, None)
    log_norm, anchor_logp, sums_b = curve_sums(
        spots, (0, 1, 2), others, counts, free_energy, directions, energies, outs
    )
    sums = jnp.sum(sums_a + sums_b, axis=2)
    tally = jnp.sum(tally_a + tally_b, axis=1)
    summed = jnp.concatenate([(sums[0] - tally)[None, :], directions * sums[0][None, :] - sums[1:3]], axis=0)
    summed = lax.psum(summed, "sample")
    scale = states * width / (samples * cores)
    return (log_norm.reshape(samples), anchor_logp.reshape(samples), scale * summed[0], scale * summed[1:3])


def solution(mesh):
    return jax.shard_map(
        local,
        mesh=mesh,
        in_specs=(
            P(("group", "state"), "sample"),
            P(("group", "state")),
            P(("group", "sample")),
            P(("group", "state")),
            P(None, ("group", "state")),
        ),
        out_specs=(
            P(("group", "sample")),
            P(("group", "sample")),
            P(("group", "state")),
            P(None, ("group", "state")),
        ),
        check_vma=False,
    )
```

time: 256 us -> 44.8 us (0.17)
  waiting for transfers between devices: 213 us -> 14.3 us
  between operations: 13.8 us -> 0.75 us
  other arithmetic: 13.9 us -> 1.61 us
  matrix products: 11.8 us -> 0 us
  starting transfers between devices: 0.12 us -> 10.9 us
  Pallas kernels: 0 us -> 9.41 us
  local copies, waits for them, and re-layouts: 0.03 us -> 5.17 us
    psum x2 -> x0, waiting for transfers between devices: 140 us -> none  [local(): total, anchor_term = lax.psum((local_total, anchor_part), 'state')]
    pmax x1 -> x0, waiting for transfers between devices: 73.1 us -> none  [local(): peak = lax.pmax(local_max, 'state')]
    ppermute x0 -> x7, waiting for transfers between devices: none -> 14.3 us  [swap(): return lax.ppermute(x, ('state', 'sample'), pairs)]
    dot_general x2 -> x0, matrix products: 11.8 us -> none  [the longest x1 5.99 us: mix_states(): mixed_part = jnp.dot(directions, weights, precision=lax.Precision.HIGHEST)]
    ppermute x0 -> x7, starting transfers between devices: none -> 10.9 us  [swap(): return lax.ppermute(x, ('state', 'sample'), pairs)]
    pallas_call x0 -> x4, Pallas kernels: none -> 9.41 us  [the longest x2 4.93 us: local_sums(): pl.pallas_call(local_body, grid_spec=pltpu.PrefetchScalarGridSpec(num_sca...]
    reduce_sum x2, other arithmetic: 6.97 us -> 0.2 us  [the longest x1 0.11 us: local(): tally = jnp.sum(tally_a + tally_b, axis=1)]
    unnamed x12, local copies, waits for them, and re-layouts: 0.03 us -> 5.09 us
  transfers between devices with their start and end apart: 3 -> 7, of which waited for: 3 -> 6; matrix products, arithmetic and copies ran while one was open for 0% -> 0% of each run, Pallas kernels for 0% -> 7%
where the time goes in v1:
time: 44.8 us; the launch traced here: 44.6 us
  waiting for transfers between devices  14.3 us (32%)
  starting transfers between devices  10.9 us (24%)
  Pallas kernels  9.41 us (21%)
  local copies, waits for them, and re-layouts  5.17 us (12%)
  blocking collectives  2.47 us (6%)
  other arithmetic  1.61 us (4%)
  between operations  0.75 us (2%)
    ppermute x7, waiting for transfers between devices, swap(): return lax.ppermute(x, ('state', 'sample'), pairs)  14.3 us
    ppermute x7, starting transfers between devices, swap(): return lax.ppermute(x, ('state', 'sample'), pairs)  10.9 us
    unnamed x12, local copies, waits for them, and re-layouts  5.09 us
    pallas_call x2, Pallas kernels, local_sums(): pl.pallas_call(local_body, grid_spec=pltpu.PrefetchScalarGridSpec(num_sca...  4.93 us
    pallas_call x2, Pallas kernels, curve_sums(): pl.pallas_call(body, grid_spec=pltpu.PrefetchScalarGridSpec(num_scalar_pr...  4.48 us
    psum x1, blocking collectives, local(): summed = lax.psum(summed, 'sample')  2.47 us
  transfers between devices with their start and end apart: 7, of which 6 were waited for; matrix products, arithmetic and copies ran while one was open for 0% of the time, Pallas kernels for 7%

profile of v1, /device:TPU:0, one launch (start us, length us, event | category | flops | bytes accessed | tf_op | source)
XLA Modules:
  0.0 44.6 jit_solution(2449748212095163554)
XLA Ops:
  0.7 0.1 stack.23.spots_ref.refs_0_
  0.7 0.0 copy-start
  0.7 2.2 %copy-done = f32[32,32768]{1,0:T(8,128)S(1)} copy-done((f32[32,32768]{1,0:T(8,128)S(1)}, f32[32,32768]{1,0:T(8,128)}, u32[]{:S(2)}) %copy-start) | copy-done | bytes 4194328
  2.9 0.0 copy-start.2
  2.9 0.9 %copy-done.2 = s32[32768]{0:T(1024)S(1)} copy-done((s32[32768]{0:T(1024)S(1)}, s32[32768]{0:T(1024)}, u32[]{:S(2)}) %copy-start.2) | copy-done | bytes 131096
  3.8 0.0 copy-start.3
  3.8 0.7 %copy-done.3 = f32[2,32]{1,0:T(2,128)S(1)} copy-done((f32[2,32]{1,0:T(2,128)S(1)}, f32[2,32]{1,0:T(2,128)}, u32[]{:S(2)}) %copy-start.3) | copy-done | bytes 280
  4.5 0.0 copy-start.4
  4.5 0.7 %copy-done.4 = s32[32]{0:T(128)S(1)} copy-done((s32[32]{0:T(128)S(1)}, s32[32]{0:T(128)}, u32[]{:S(2)}) %copy-start.4) | copy-done | bytes 152
  5.2 0.0 copy-start.5
  5.2 0.7 %copy-done.5 = f32[32]{0:T(128)S(1)} copy-done((f32[32]{0:T(128)S(1)}, f32[32]{0:T(128)}, u32[]{:S(2)}) %copy-start.5) | copy-done | bytes 152
  5.8 3.5 %local_sums.3 = (f32[4,64,128]{2,1,0:T(8,128)S(1)}, f32[4,64,128]{2,1,0:T(8,128)S(1)}, f32[4,64,128]{2,1,0:T(8,128)S(1)}, f32[32,128]{1,0:T(8,128)S(1)}) custom-call(s32[5]{0:T(128)S(1)} %stack.23.spots_ref.refs_0_, s32[1,32]{1,0:T(1,128)S(1)} %bitcast.37, f32[1,32]{1,0:T(1,128)S(1)} %bitcast.41, f32[2,32]{1,0:T(2,128)S(1)} %copy-done.3, ...), custom_call_target="tpu_custom_call" | custom-call | flops 15728640 | bytes 3145728 | tf_op jit(solution)/shard_map/local_sums/pallas_call | solution.py:130
  9.3 0.0 copy-start.1
  9.3 4.0 %collective-permute-start = (f32[4,64,128]{2,1,0:T(8,128)S(1)}, f32[4,64,128]{2,1,0:T(8,128)S(1)}, u32[]{:S(2)}, u32[]{:S(2)}) collective-permute-start(f32[4,64,128]{2,1,0:T(8,128)S(1)} %get-tuple-element.17), channel_id=1, source_target_pairs={{0,6},{1,7},{2,4},{3,5},{4,2},{5,3},{6,0},{7,1},{8,14},{9,15},{10,... | collective-permute-start | bytes 393224 | tf_op jit(solution)/shard_map/ppermute | solution.py:275
  13.3 0.5 %collective-permute-start.1 = (f32[4,64,128]{2,1,0:T(8,128)S(1)}, f32[4,64,128]{2,1,0:T(8,128)S(1)}, u32[]{:S(2)}, u32[]{:S(2)}) collective-permute-start(f32[4,64,128]{2,1,0:T(8,128)S(1)} %get-tuple-element.18), channel_id=1, source_target_pairs={{0,2},{1,5},{2,0},{3,7},{4,6},{5,1},{6,4},{7,3},{8,10},{9,13},{10,... | collective-permute-start | bytes 393224 | tf_op jit(solution)/shard_map/ppermute | solution.py:275
  13.9 0.1 collective-permute-start.2
  14.0 1.5 %local_sums.2 = (f32[4,64,128]{2,1,0:T(8,128)S(1)}, f32[32,128]{1,0:T(8,128)S(1)}) custom-call(s32[5]{0:T(128)S(1)} %stack.23.spots_ref.refs_0_, s32[1,32]{1,0:T(1,128)S(1)} %bitcast.38, f32[1,32]{1,0:T(1,128)S(1)} %bitcast.42, f32[2,32]{1,0:T(2,128)S(1)} %copy-done.3, s32[256,128]{1,0:T(8,128)S(1)} %bitcast.36, f32[32,32768]{1,0:T(8,128)S(1)} %copy-done), custom_call_target="tpu_custom_call" | custom-call | flops 5242880 | bytes 1048576 | tf_op jit(solution)/shard_map/local_sums/pallas_call | solution.py:130
  15.4 2.2 %collective-permute-done = f32[4,64,128]{2,1,0:T(8,128)S(1)} collective-permute-done((f32[4,64,128]{2,1,0:T(8,128)S(1)}, f32[4,64,128]{2,1,0:T(8,128)S(1)}, u32[]{:S(2)}, u32[]{:S(2)}) %collective-permute-start) | collective-permute-done | bytes 131104 | tf_op jit(solution)/shard_map/ppermute | solution.py:275
  17.6 2.0 %collective-permute-done.1 = f32[4,64,128]{2,1,0:T(8,128)S(1)} collective-permute-done((f32[4,64,128]{2,1,0:T(8,128)S(1)}, f32[4,64,128]{2,1,0:T(8,128)S(1)}, u32[]{:S(2)}, u32[]{:S(2)}) %collective-permute-start.1) | collective-permute-done | bytes 131104 | tf_op jit(solution)/shard_map/ppermute | solution.py:275
  19.6 0.2 collective-permute-done.2
  19.9 0.1 select_select_fusion.1
  20.0 2.7 %collective-permute-start.3 = (f32[4,64,128]{2,1,0:T(8,128)S(1)}, f32[4,64,128]{2,1,0:T(8,128)S(1)}, u32[]{:S(2)}, u32[]{:S(2)}) collective-permute-start(f32[4,64,128]{2,1,0:T(8,128)S(1)} %select_select_fusion.1), channel_id=1, source_target_pairs={{0,8},{1,9},{2,10},{3,11},{4,12},{5,13},{6,14},{7,15},{8,0},{9,1},... | collective-permute-start | bytes 393224 | tf_op jit(solution)/shard_map/ppermute | solution.py:275
  22.6 6.1 %collective-permute-done.3 = f32[4,64,128]{2,1,0:T(8,128)S(1)} collective-permute-done((f32[4,64,128]{2,1,0:T(8,128)S(1)}, f32[4,64,128]{2,1,0:T(8,128)S(1)}, u32[]{:S(2)}, u32[]{:S(2)}) %collective-permute-start.3) | collective-permute-done | bytes 131104 | tf_op jit(solution)/shard_map/ppermute | solution.py:275
  28.8 0.1 select_select_fusion.refs_0_
  28.9 0.7 %collective-permute-start.6 = (f32[4,64,128]{2,1,0:T(8,128)S(1)}, f32[4,64,128]{2,1,0:T(8,128)S(1)}, u32[]{:S(2)}, u32[]{:S(2)}) collective-permute-start(f32[4,64,128]{2,1,0:T(8,128)S(1)} %select_select_fusion.refs_0_), channel_id=1, source_target_pairs={{0,4},{1,3},{2,6},{3,1},{4,0},{5,7},{6,2},{7,5},{8,12},{9,11},{10,... | collective-permute-start | bytes 393224 | tf_op jit(solution)/shard_map/ppermute | solution.py:275
  29.5 2.0 %collective-permute-start.5 = (f32[4,64,128]{2,1,0:T(8,128)S(1)}, f32[4,64,128]{2,1,0:T(8,128)S(1)}, u32[]{:S(2)}, u32[]{:S(2)}) collective-permute-start(f32[4,64,128]{2,1,0:T(8,128)S(1)} %select_select_fusion.refs_0_), channel_id=1, source_target_pairs={{0,2},{1,5},{2,0},{3,7},{4,6},{5,1},{6,4},{7,3},{8,10},{9,13},{10,... | collective-permute-start | bytes 393224 | tf_op jit(solution)/shard_map/ppermute | solution.py:275
  31.5 0.9 %collective-permute-start.4 = (f32[4,64,128]{2,1,0:T(8,128)S(1)}, f32[4,64,128]{2,1,0:T(8,128)S(1)}, u32[]{:S(2)}, u32[]{:S(2)}) collective-permute-start(f32[4,64,128]{2,1,0:T(8,128)S(1)} %select_select_fusion.refs_0_), channel_id=1, source_target_pairs={{0,6},{1,7},{2,4},{3,5},{4,2},{5,3},{6,0},{7,1},{8,14},{9,15},{10,... | collective-permute-start | bytes 393224 | tf_op jit(solution)/shard_map/ppermute | solution.py:275
  32.4 0.1 add_reduce_fusion.1
  32.5 0.0 copy-done.1
  32.5 1.6 %curve_sums.2 = (f32[256,128]{1,0:T(8,128)}, f32[256,128]{1,0:T(8,128)}, f32[3,32,128]{2,1,0:T(8,128)S(1)}) custom-call(s32[5]{0:T(128)S(1)} %stack.23.spots_ref.refs_0_, s32[1,32]{1,0:T(1,128)S(1)} %bitcast.39, f32[1,32]{1,0:T(1,128)S(1)} %bitcast.43, f32[2,32]{1,0:T(2,128)S(1)} %copy-done.3, f32[32,32768]{1,0:T(8,128)S(1)} %copy-done.1, ...), custom_call_target="tpu_custom_call" | custom-call | flops 2359296 | bytes 1048576 | tf_op jit(solution)/shard_map/curve_sums/pallas_call | solution.py:240
  34.1 1.1 %collective-permute-done.6.refs_7_ = f32[4,64,128]{2,1,0:T(8,128)S(1)} collective-permute-done((f32[4,64,128]{2,1,0:T(8,128)S(1)}, f32[4,64,128]{2,1,0:T(8,128)S(1)}, u32[]{:S(2)}, u32[]{:S(2)}) %collective-permute-start.6) | collective-permute-done | bytes 131104 | tf_op jit(solution)/shard_map/ppermute | solution.py:275
  35.3 0.0 collective-permute-done.5.refs_6_
  35.3 2.8 %collective-permute-done.4.refs_5_ = f32[4,64,128]{2,1,0:T(8,128)S(1)} collective-permute-done((f32[4,64,128]{2,1,0:T(8,128)S(1)}, f32[4,64,128]{2,1,0:T(8,128)S(1)}, u32[]{:S(2)}, u32[]{:S(2)}) %collective-permute-start.4) | collective-permute-done | bytes 131104 | tf_op jit(solution)/shard_map/ppermute | solution.py:275
  38.0 2.9 %curve_sums.3 = (f32[256,128]{1,0:T(8,128)}, f32[256,128]{1,0:T(8,128)}, f32[3,32,128]{2,1,0:T(8,128)S(1)}) custom-call(s32[5]{0:T(128)S(1)} %stack.23.spots_ref.refs_0_, s32[1,32]{1,0:T(1,128)S(1)} %bitcast.40, f32[1,32]{1,0:T(1,128)S(1)} %bitcast.44, f32[2,32]{1,0:T(2,128)S(1)} %copy-done.3, ...), custom_call_target="tpu_custom_call", output_to_operand_aliasing={{0}: (8, {}), {1}: (9, {})} | custom-call | flops 7077888 | bytes 3145728 | tf_op jit(solution)/shard_map/curve_sums/pallas_call | solution.py:240
  40.9 0.1 add_reduce_fusion
  41.0 2.5 %psum.7 = f32[3,32]{1,0:T(4,128)S(1)} all-reduce(f32[3,32]{1,0:T(4,128)S(1)} %pad_maximum_fusion), channel_id=1, replica_groups=mesh['group'=2,'state'=8,'sample'=2] {'sample'}, use_global_device_ids=true, to_apply=%region_2.3 | all-reduce | flops 96 | bytes 768 | tf_op jit(solution)/shard_map/psum | solution.py:301
  43.5 0.5 %multiply_bitcast_fusion = f32[32]{0:T(128)} fusion(f32[3,32]{1,0:T(4,128)S(1)} %psum.7), kind=kLoop, calls=%fused_computation.26 | loop fusion | flops 32 | bytes 256 | tf_op jit(solution)/shard_map/mul | solution.py:303
  44.0 0.6 %slice_multiply_fusion = f32[2,32]{1,0:T(2,128)} fusion(f32[3,32]{1,0:T(4,128)S(1)} %psum.7), kind=kLoop, calls=%fused_computation.23 | loop fusion | flops 64 | bytes 512 | tf_op jit(solution)/shard_map/mul | solution.py:303
  (8 shorter events, 0.1 us)
Async XLA Ops:
  0.7 2.2 %copy-start = (f32[32,32768]{1,0:T(8,128)S(1)}, f32[32,32768]{1,0:T(8,128)}, u32[]{:S(2)}) copy-start(f32[32,32768]{1,0:T(8,128)} %refs_4_.1) | copy-start | bytes 12582916
  2.9 0.9 %copy-start.2 = (s32[32768]{0:T(1024)S(1)}, s32[32768]{0:T(1024)}, u32[]{:S(2)}) copy-start(s32[32768]{0:T(1024)} %param.7) | copy-start | bytes 393220
  3.8 0.7 %copy-start.3 = (f32[2,32]{1,0:T(2,128)S(1)}, f32[2,32]{1,0:T(2,128)}, u32[]{:S(2)}) copy-start(f32[2,32]{1,0:T(2,128)} %refs_3_.1) | copy-start | bytes 772
  4.5 0.7 %copy-start.4 = (s32[32]{0:T(128)S(1)}, s32[32]{0:T(128)}, u32[]{:S(2)}) copy-start(s32[32]{0:T(128)} %param.6) | copy-start | bytes 388
  5.2 0.7 %copy-start.5 = (f32[32]{0:T(128)S(1)}, f32[32]{0:T(128)}, u32[]{:S(2)}) copy-start(f32[32]{0:T(128)} %param.8) | copy-start | bytes 388
  9.3 23.2 %copy-start.1 = (f32[32,32768]{1,0:T(8,128)S(1)}, f32[32,32768]{1,0:T(8,128)}, u32[]{:S(2)}) copy-start(f32[32,32768]{1,0:T(8,128)} %refs_4_.1) | copy-start | bytes 12582916
  9.3 8.3 %collective-permute-start = (f32[4,64,128]{2,1,0:T(8,128)S(1)}, f32[4,64,128]{2,1,0:T(8,128)S(1)}, u32[]{:S(2)}, u32[]{:S(2)}) collective-permute-start(f32[4,64,128]{2,1,0:T(8,128)S(1)} %get-tuple-element.17), channel_id=1, source_target_pairs={{0,6},{1,7},{2,4},{3,5},{4,2},{5,3},{6,0},{7,1},{8,14},{9,15},{10,... | collective-permute-start | bytes 393224 | tf_op jit(solution)/shard_map/ppermute | solution.py:275
  13.3 6.3 %collective-permute-start.1 = (f32[4,64,128]{2,1,0:T(8,128)S(1)}, f32[4,64,128]{2,1,0:T(8,128)S(1)}, u32[]{:S(2)}, u32[]{:S(2)}) collective-permute-start(f32[4,64,128]{2,1,0:T(8,128)S(1)} %get-tuple-element.18), channel_id=1, source_target_pairs={{0,2},{1,5},{2,0},{3,7},{4,6},{5,1},{6,4},{7,3},{8,10},{9,13},{10,... | collective-permute-start | bytes 393224 | tf_op jit(solution)/shard_map/ppermute | solution.py:275
  13.9 5.9 %collective-permute-start.2 = (f32[4,64,128]{2,1,0:T(8,128)S(1)}, f32[4,64,128]{2,1,0:T(8,128)S(1)}, u32[]{:S(2)}, u32[]{:S(2)}) collective-permute-start(f32[4,64,128]{2,1,0:T(8,128)S(1)} %get-tuple-element.19), channel_id=1, source_target_pairs={{0,4},{1,3},{2,6},{3,1},{4,0},{5,7},{6,2},{7,5},{8,12},{9,11},{10,... | collective-permute-start | bytes 393224 | tf_op jit(solution)/shard_map/ppermute | solution.py:275
  20.0 8.7 %collective-permute-start.3 = (f32[4,64,128]{2,1,0:T(8,128)S(1)}, f32[4,64,128]{2,1,0:T(8,128)S(1)}, u32[]{:S(2)}, u32[]{:S(2)}) collective-permute-start(f32[4,64,128]{2,1,0:T(8,128)S(1)} %select_select_fusion.1), channel_id=1, source_target_pairs={{0,8},{1,9},{2,10},{3,11},{4,12},{5,13},{6,14},{7,15},{8,0},{9,1},... | collective-permute-start | bytes 393224 | tf_op jit(solution)/shard_map/ppermute | solution.py:275
  28.9 6.4 %collective-permute-start.6 = (f32[4,64,128]{2,1,0:T(8,128)S(1)}, f32[4,64,128]{2,1,0:T(8,128)S(1)}, u32[]{:S(2)}, u32[]{:S(2)}) collective-permute-start(f32[4,64,128]{2,1,0:T(8,128)S(1)} %select_select_fusion.refs_0_), channel_id=1, source_target_pairs={{0,4},{1,3},{2,6},{3,1},{4,0},{5,7},{6,2},{7,5},{8,12},{9,11},{10,... | collective-permute-start | bytes 393224 | tf_op jit(solution)/shard_map/ppermute | solution.py:275
  29.5 5.8 %collective-permute-start.5 = (f32[4,64,128]{2,1,0:T(8,128)S(1)}, f32[4,64,128]{2,1,0:T(8,128)S(1)}, u32[]{:S(2)}, u32[]{:S(2)}) collective-permute-start(f32[4,64,128]{2,1,0:T(8,128)S(1)} %select_select_fusion.refs_0_), channel_id=1, source_target_pairs={{0,2},{1,5},{2,0},{3,7},{4,6},{5,1},{6,4},{7,3},{8,10},{9,13},{10,... | collective-permute-start | bytes 393224 | tf_op jit(solution)/shard_map/ppermute | solution.py:275
  31.5 6.5 %collective-permute-start.4 = (f32[4,64,128]{2,1,0:T(8,128)S(1)}, f32[4,64,128]{2,1,0:T(8,128)S(1)}, u32[]{:S(2)}, u32[]{:S(2)}) collective-permute-start(f32[4,64,128]{2,1,0:T(8,128)S(1)} %select_select_fusion.refs_0_), channel_id=1, source_target_pairs={{0,6},{1,7},{2,4},{3,5},{4,2},{5,3},{6,0},{7,1},{8,14},{9,15},{10,... | collective-permute-start | bytes 393224 | tf_op jit(solution)/shard_map/ppermute | solution.py:275

commit v2 on v0

v2 whole, which is shorter than its diff:
```python
import functools
import math

import jax
import jax.numpy as jnp
from jax import lax
from jax.experimental import pallas as pl
from jax.experimental.pallas import tpu as pltpu
from jax.sharding import PartitionSpec as P

LANES = 128
ROWS = 8
TILE = LANES * ROWS


def plan(level, shift):
    if level == 0:
        return [0] * ROWS, 1
    half = ROWS >> level
    first, count = plan(level - 1, shift)
    second, _ = plan(level - 1, shift - half)
    owner = []
    for row in range(ROWS):
        keep = ((row - shift) // half) % 2 == 1
        owner.append(first[row] if keep else second[row] + count)
    return owner, 2 * count


PLACE, _ = plan(3, 0)


def fold(leaf, combine, rows, level=3, shift=0, first=0):
    if level == 0:
        return leaf(PLACE.index(first))
    half = ROWS >> level
    count = 1 << (level - 1)
    a = fold(leaf, combine, rows, level - 1, shift, first)
    b = fold(leaf, combine, rows, level - 1, shift - half, first + count)
    keep = (((rows - shift + 2 * ROWS) // half) % 2) == 1
    out = []
    for one, two, how in zip(a, b, combine, strict=True):
        mine = jnp.where(keep, one, two)
        other = jnp.where(keep, two, one)
        out.append(how(mine, pltpu.roll(other, half, 0)))
    return tuple(out)


def column(row, states):
    spread = jnp.broadcast_to(row, (states, states))
    eye = lax.broadcasted_iota(jnp.int32, (states, states), 0) == lax.broadcasted_iota(jnp.int32, (states, states), 1)
    picked = jnp.sum(jnp.where(eye, spread, 0.0), axis=1, keepdims=True)
    return jnp.broadcast_to(picked, (states, LANES))


def bases(counts_ref, free_ref, states):
    return column(jnp.log(counts_ref[...].astype(jnp.float32)) + free_ref[...], states)


def spot(flips):
    core = lax.axis_index("sample")
    flip = functools.reduce(lambda rest, c: jnp.where(core == c, flips[c], rest), range(1, len(flips)), flips[0])
    return jnp.bitwise_xor(jnp.bitwise_and(lax.axis_index("state"), 3), flip)


def over_tiles(x, how):
    parts = [x[i * ROWS : (i + 1) * ROWS] for i in range(x.shape[0] // ROWS)]
    return functools.reduce(how, parts)


def spread(x, g, states):
    return jnp.broadcast_to(x[g : g + 1, :], (states, LANES))


def sums_of(out_ref, energies_ref, offset, labels_ref, label_row, base, dirs, first_state, steps):
    states = energies_ref.shape[0]
    rows = lax.broadcasted_iota(jnp.int32, (ROWS, LANES), 0)
    ids = lax.broadcasted_iota(jnp.int32, (states, LANES), 0)

    def step(j, carry):
        at = pl.multiple_of(j * ROWS, ROWS)
        labels = labels_ref[pl.ds(pl.multiple_of(label_row + j * ROWS, ROWS), ROWS), :] - first_state

        def shifted(g):
            cols = pl.ds(pl.multiple_of(offset + j * TILE + g * LANES, LANES), LANES)
            return base[...] - energies_ref[:, cols]

        (peak,) = fold(lambda g: (over_tiles(shifted(g), jnp.maximum),), (jnp.maximum,), rows)

        def leaf(g):
            s = shifted(g)
            e = jnp.exp(s - spread(peak, g, states))
            return (
                over_tiles(e, jnp.add),
                over_tiles(e * dirs[0], jnp.add),
                over_tiles(e * dirs[1], jnp.add),
                over_tiles(jnp.where(ids == spread(labels, g, states), s, 0.0), jnp.add),
            )

        total, mix0, mix1, anchor = fold(leaf, (jnp.add,) * 4, rows)
        inverse = 1.0 / total
        out_ref[0, pl.ds(at, ROWS), :] = peak + jnp.log(total)
        out_ref[1, pl.ds(at, ROWS), :] = mix0 * inverse
        out_ref[2, pl.ds(at, ROWS), :] = mix1 * inverse
        out_ref[3, pl.ds(at, ROWS), :] = anchor
        return carry

    lax.fori_loop(0, steps, step, 0)


def first_body(flips, counts_hbm, free_hbm, dirs_hbm, labels_hbm, energies_hbm, out_ref, base_out, dirs_out, *scratch):
    counts_s, free_s, dirs_s, labels_s, energies_s, sems = scratch
    states, samples = energies_hbm.shape
    width = samples // 4
    chunks = energies_s.shape[0]
    chunk = width // chunks
    quarter = spot(flips)
    rows = width // LANES
    small = [
        pltpu.make_async_copy(counts_hbm, counts_s, sems.at[0]),
        pltpu.make_async_copy(free_hbm, free_s, sems.at[1]),
        pltpu.make_async_copy(dirs_hbm, dirs_s, sems.at[2]),
        pltpu.make_async_copy(labels_hbm.at[pl.ds(pl.multiple_of(quarter * rows, rows), rows), :], labels_s, sems.at[3]),
    ]
    large = [
        pltpu.make_async_copy(
            energies_hbm.at[:, pl.ds(pl.multiple_of(quarter * width + c * chunk, chunk), chunk)],
            energies_s.at[c],
            sems.at[4 + c],
        )
        for c in range(chunks)
    ]
    for copy in small + large:
        copy.start()
    for copy in small:
        copy.wait()
    base_out[...] = bases(counts_s, free_s, states)
    dirs_out[0] = column(dirs_s[0:1, :], states)
    dirs_out[1] = column(dirs_s[1:2, :], states)
    first_state = lax.axis_index("state") * states
    for c, copy in enumerate(large):
        copy.wait()
        part = out_ref.at[:, pl.ds(c * (rows // chunks), rows // chunks), :]
        sums_of(
            part, energies_s.at[c], 0, labels_s, c * (rows // chunks), base_out, dirs_out, first_state, chunk // TILE
        )


def later_body(flips, base_ref, dirs_ref, labels_ref, energies_ref, out_ref):
    states, samples = energies_ref.shape
    width = samples // 4
    quarter = spot(flips)
    first_state = lax.axis_index("state") * states
    offset, row = quarter * width, quarter * (width // LANES)
    sums_of(out_ref, energies_ref, offset, labels_ref, row, base_ref, dirs_ref, first_state, width // TILE)


def tally_body(labels_ref, tally_ref):
    states = tally_ref.shape[0]
    first_state = lax.axis_index("state") * states
    ids = lax.broadcasted_iota(jnp.int32, (states, LANES), 0)

    def step(j, tally):
        labels = labels_ref[pl.ds(pl.multiple_of(j * ROWS, ROWS), ROWS), :] - first_state
        for g in range(ROWS):
            tally += jnp.where(ids == spread(labels, g, states), 1.0, 0.0)
        return tally

    tally_ref[...] = lax.fori_loop(0, labels_ref.shape[0] // ROWS, step, jnp.zeros((states, LANES), jnp.float32))


def weigh(part_ref, energies_ref, quarter, base_ref):
    states, samples = energies_ref.shape
    width = samples // 4

    def step(j, carry):
        occupancy, mix0, mix1 = carry
        at = pl.ds(pl.multiple_of(j * ROWS, ROWS), ROWS)
        norm, first, second = part_ref[0, at, :], part_ref[1, at, :], part_ref[2, at, :]
        for g in range(ROWS):
            cols = pl.ds(pl.multiple_of(quarter * width + j * TILE + g * LANES, LANES), LANES)
            w = jnp.exp((base_ref[...] - energies_ref[:, cols]) - spread(norm, g, states))
            occupancy += w
            mix0 += w * spread(first, g, states)
            mix1 += w * spread(second, g, states)
        return occupancy, mix0, mix1

    zero = jnp.zeros((states, LANES), jnp.float32)
    return lax.fori_loop(0, width // TILE, step, (zero, zero, zero))


def weigh_body(flips, *refs):
    n = len(flips)
    part_refs = refs[:n]
    base_ref, energies_ref, sums_ref = refs[n:]
    for k in range(n):
        for i, x in enumerate(weigh(part_refs[k], energies_ref, spot(flips[k]), base_ref)):
            if k == 0:
                sums_ref[i] = x
            else:
                sums_ref[i] += x


def last_body(flips, *refs):
    part_refs = refs[:4]
    base_ref, dirs_ref, tally_ref, sums_ref, energies_ref, norm_hbm, anchor_hbm, out_ref, sems = refs[4:]
    states, samples = energies_ref.shape
    rows = samples // 4 // LANES
    copies = []
    for k, part_ref in enumerate(part_refs):
        at = pl.ds(pl.multiple_of(spot(flips[k]) * rows, rows), rows)
        copies.append(pltpu.make_async_copy(part_ref.at[0], norm_hbm.at[at, :], sems.at[2 * k]))
        copies.append(pltpu.make_async_copy(part_ref.at[3], anchor_hbm.at[at, :], sems.at[2 * k + 1]))
    for copy in copies:
        copy.start()
    sums = weigh(part_refs[3], energies_ref, spot(flips[3]), base_ref)
    eye = lax.broadcasted_iota(jnp.int32, (states, states), 0) == lax.broadcasted_iota(jnp.int32, (states, states), 1)

    def row(x):
        total = jnp.broadcast_to(jnp.sum(x, axis=1, keepdims=True), (states, states))
        return jnp.sum(jnp.where(eye, total, 0.0), axis=0, keepdims=True)

    occupancy = sums[0] + sums_ref[0]
    out_ref[0:1, :] = row(occupancy - tally_ref[...])
    for j in range(2):
        out_ref[j + 1 : j + 2, :] = row(dirs_ref[j] * occupancy - (sums[j + 1] + sums_ref[j + 1]))
    for copy in copies:
        copy.wait()


def total_body(scale, mine_ref, other_ref, gradient_ref, products_ref):
    total = scale * (mine_ref[...] + other_ref[...])
    gradient_ref[...] = total[0:1]
    products_ref[...] = total[1:3]


VMEM = pl.BlockSpec(memory_space=pltpu.VMEM)
HBM = pl.BlockSpec(memory_space=pltpu.HBM)
LIMIT = 16 * 1024 * 1024


def f32(*shape):
    return jax.ShapeDtypeStruct(shape, jnp.float32)


def kernel(body, in_specs, out_specs, out_shape, name, work, scratch=()):
    return pl.pallas_call(
        body,
        in_specs=in_specs,
        out_specs=out_specs,
        out_shape=out_shape,
        scratch_shapes=list(scratch),
        compiler_params=pltpu.CompilerParams(vmem_limit_bytes=LIMIT),
        cost_estimate=pl.CostEstimate(flops=16 * work, bytes_accessed=4 * work, transcendentals=work),
        name=name,
    )


def merge(parts, last):
    norms = [part[0:1] for part in parts]
    peak = functools.reduce(jnp.maximum, norms)
    scales = [jnp.exp(norm - peak) for norm in norms]
    total = functools.reduce(jnp.add, scales)
    mixed = functools.reduce(jnp.add, [s * part for s, part in zip(scales, parts, strict=True)]) / total
    anchor = functools.reduce(jnp.add, parts)
    norm = peak + jnp.log(total)
    kind = lax.broadcasted_iota(jnp.int32, parts[0].shape, 0)
    return jnp.where(kind == 0, norm, jnp.where(kind == 3, anchor - norm if last else anchor, mixed))


def swap(x, width, cores, flips):
    pairs = []
    for place in range(width):
        for core in range(cores):
            pairs.append((place * cores + core, (place ^ flips[core]) * cores + core))
    return lax.ppermute(x, ("state", "sample"), pairs)


def local(energies, counts, labels, free_energy, directions):
    states, samples = energies.shape
    width, cores = lax.axis_size("state"), lax.axis_size("sample")
    rounds = [(3,) * cores, tuple(1 + c % 2 for c in range(cores)), tuple(2 - c % 2 for c in range(cores))]
    stay = (0,) * cores
    rows = samples // 4 // LANES
    work = states * samples // 4
    labels = labels.reshape(samples // LANES, LANES)
    part = f32(4, rows, LANES)
    chunks = 2 if samples % (8 * TILE) == 0 else 1

    first, base, dirs = kernel(
        functools.partial(first_body, rounds[0]),
        [HBM] * 5,
        [VMEM] * 3,
        [part, f32(states, LANES), f32(2, states, LANES)],
        "first_sums",
        work,
        [
            pltpu.VMEM((1, states), jnp.int32),
            pltpu.VMEM((1, states), jnp.float32),
            pltpu.VMEM((2, states), jnp.float32),
            pltpu.VMEM((rows, LANES), jnp.int32),
            pltpu.VMEM((chunks, states, samples // 4 // chunks), jnp.float32),
            pltpu.SemaphoreType.DMA((4 + chunks,)),
        ],
    )(
        *(
            pltpu.with_memory_space_constraint(x, pltpu.HBM)
            for x in (counts.reshape(1, states), free_energy.reshape(1, states), directions, labels, energies)
        )
    )

    def later(flips, name):
        return kernel(functools.partial(later_body, flips), [VMEM] * 4, VMEM, part, name, work)(
            base, dirs, labels, energies
        )

    sent = [first, later(rounds[1], "second_sums"), later(rounds[2], "third_sums")]
    got = [swap(x, width, cores, flips) for x, flips in zip(sent, rounds, strict=True)]
    own = later(stay, "own_sums")
    tally = kernel(tally_body, [VMEM], VMEM, f32(states, LANES), "tally", work)(labels)
    far = range(2, int(math.log2(width)))
    union = merge([own, *got], not far)
    for bit in far:
        union = merge([union, swap(union, width, cores, (1 << bit,) * cores)], bit == far[-1])
    others = [swap(union, width, cores, flips) for flips in rounds]
    sums = kernel(
        functools.partial(weigh_body, (stay, rounds[0], rounds[1])),
        [VMEM] * 5,
        VMEM,
        f32(3, states, LANES),
        "weigh",
        3 * work,
    )(union, others[0], others[1], base, energies)
    long = f32(samples // LANES, LANES)
    log_norm, anchor_logp, mine = kernel(
        functools.partial(last_body, (stay, *rounds)),
        [VMEM] * 9,
        [HBM, HBM, VMEM],
        [long, long, f32(3, states)],
        "last_sums",
        work,
        [pltpu.SemaphoreType.DMA((8,))],
    )(union, *others, base, dirs, tally, sums, energies)
    other = lax.ppermute(mine, "sample", [(c, cores - 1 - c) for c in range(cores)])
    gradient, products = kernel(
        functools.partial(total_body, states * width / (samples * cores)),
        [VMEM] * 2,
        [VMEM] * 2,
        [f32(1, states), f32(2, states)],
        "totals",
        1024,
    )(mine, other)
    return log_norm.reshape(samples), anchor_logp.reshape(samples), gradient.reshape(states), products


def solution(mesh):
    return jax.shard_map(
        local,
        mesh=mesh,
        in_specs=(
            P(("group", "state"), "sample"),
            P(("group", "state")),
            P(("group", "sample")),
            P(("group", "state")),
            P(None, ("group", "state")),
        ),
        out_specs=(
            P(("group", "sample")),
            P(("group", "sample")),
            P(("group", "state")),
            P(None, ("group", "state")),
        ),
        check_vma=False,
    )
```

time: 256 us -> 36.6 us (0.14)
  waiting for transfers between devices: 213 us -> 16.2 us
  other arithmetic: 13.9 us -> 0.3 us
  between operations: 13.8 us -> 0.74 us
  matrix products: 11.8 us -> 0 us
  starting transfers between devices: 0.12 us -> 11.3 us
  Pallas kernels: 0 us -> 7.44 us
    psum x2 -> x0, waiting for transfers between devices: 140 us -> none  [local(): total, anchor_term = lax.psum((local_total, anchor_part), 'state')]
    pmax x1 -> x0, waiting for transfers between devices: 73.1 us -> none  [local(): peak = lax.pmax(local_max, 'state')]
    ppermute x0 -> x8, waiting for transfers between devices: none -> 16.2 us  [the longest x7 15 us: swap(): return lax.ppermute(x, ('state', 'sample'), pairs)]
    dot_general x2 -> x0, matrix products: 11.8 us -> none  [the longest x1 5.99 us: mix_states(): mixed_part = jnp.dot(directions, weights, precision=lax.Precision.HIGHEST)]
    ppermute x0 -> x8, starting transfers between devices: none -> 11.3 us  [the longest x7 11.2 us: swap(): return lax.ppermute(x, ('state', 'sample'), pairs)]
    pallas_call x0 -> x8, Pallas kernels: none -> 7.44 us  [the longest x3 2.34 us: later(): kernel(functools.partial(later_body, flips), [VMEM] * 4, VMEM, part, name...]
    reduce_sum x2 -> x0, other arithmetic: 6.97 us -> none  [the longest x1 3.84 us: local(): local_total = jnp.sum(jnp.exp(shifted - peak[None, :]), axis=0)]
    reduce_max x1 -> x0, other arithmetic: 3.4 us -> none  [local(): local_max = jnp.max(shifted, axis=0)]
  transfers between devices with their start and end apart: 3 -> 8, of which waited for: 3 -> 5; matrix products, arithmetic and copies ran while one was open for 0% -> 0% of each run, Pallas kernels for 0% -> 9%
where the time goes in v2:
time: 36.6 us; the launch traced here: 36.4 us
  waiting for transfers between devices  16.2 us (44%)
  starting transfers between devices  11.3 us (31%)
  Pallas kernels  7.44 us (20%)
  between operations  0.74 us (2%)
  local copies, waits for them, and re-layouts  0.49 us (1%)
    ppermute x7, waiting for transfers between devices, swap(): return lax.ppermute(x, ('state', 'sample'), pairs)  15 us
    ppermute x7, starting transfers between devices, swap(): return lax.ppermute(x, ('state', 'sample'), pairs)  11.2 us
    pallas_call x3, Pallas kernels, later(): kernel(functools.partial(later_body, flips), [VMEM] * 4, VMEM, part, name...  2.34 us
    pallas_call x1, Pallas kernels, local(): kernel(functools.partial(first_body, rounds[0]), [HBM] * 5, [VMEM] * 3, [...  2.06 us
    ppermute x1, waiting for transfers between devices, local(): lax.ppermute(mine, 'sample', [(c, cores - 1 - c) for c in range(cores)])  1.14 us
    pallas_call x1, Pallas kernels, local(): kernel(functools.partial(weigh_body, (stay, rounds[0], rounds[1])), [VMEM...  1.11 us
    pallas_call x1, Pallas kernels, local(): kernel(functools.partial(last_body, (stay, *rounds)), [VMEM] * 9, [HBM, H...  0.77 us
  transfers between devices with their start and end apart: 8, of which 5 were waited for; matrix products, arithmetic and copies ran while one was open for 0% of the time, Pallas kernels for 9%

profile of v2, /device:TPU:0, one launch (start us, length us, event | category | flops | bytes accessed | tf_op | source)
XLA Modules:
  0.0 36.4 jit_solution(3820879252340043554)
XLA Ops:
  0.6 0.0 copy-start
  0.6 0.0 copy-start.1
  0.7 2.1 %first_sums.1 = (f32[4,64,128]{2,1,0:T(8,128)S(1)}, f32[32,128]{1,0:T(8,128)S(1)}, f32[2,32,128]{2,1,0:T(8,128)S(1)}) custom-call(s32[1,32]{1,0:T(1,128)} %bitcast.31, f32[1,32]{1,0:T(1,128)} %bitcast.32, f32[2,32]{1,0:T(2,128)} %dirs_hbm.1, s32[256,128]{1,0:T(8,128)} %bitcast.25, f32[32,32768]{1,0:T(8,128)} %refs_8_.1), custom_call_target="tpu_custom_call" | custom-call | flops 4194304 | bytes 1048576 | tf_op jit(solution)/shard_map/first_sums/pallas_call | solution.py:289
  2.7 0.5 %copy-done = f32[32,32768]{1,0:T(8,128)S(1)} copy-done((f32[32,32768]{1,0:T(8,128)S(1)}, f32[32,32768]{1,0:T(8,128)}, u32[]{:S(2)}) %copy-start) | copy-done | bytes 4194328
  3.2 0.0 copy-done.1
  3.2 0.8 %second_sums.1 = f32[4,64,128]{2,1,0:T(8,128)S(1)} custom-call(f32[32,128]{1,0:T(8,128)S(1)} %get-tuple-element.12.base_ref.refs_3_.refs_4_, f32[2,32,128]{2,1,0:T(8,128)S(1)} %get-tuple-element.13.dirs_ref.refs_5_, s32[256,128]{1,0:T(8,128)S(1)} %bitcast.26, f32[32,32768]{1,0:T(8,128)S(1)} %copy-done), custom_call_target="tpu_custom_call" | custom-call | flops 4194304 | bytes 1048576 | tf_op jit(solution)/shard_map/second_sums/pallas_call | solution.py:312
  4.0 3.0 %collective-permute-start.1 = (f32[4,64,128]{2,1,0:T(8,128)S(1)}, f32[4,64,128]{2,1,0:T(8,128)S(1)}, u32[]{:S(2)}, u32[]{:S(2)}) collective-permute-start(f32[4,64,128]{2,1,0:T(8,128)S(1)} %second_sums.1), channel_id=1, source_target_pairs={{0,2},{1,5},{2,0},{3,7},{4,6},{5,1},{6,4},{7,3},{8,10},{9,13},{10,... | collective-permute-start | bytes 393224 | tf_op jit(solution)/shard_map/ppermute | solution.py:275
  7.0 0.8 %third_sums.1 = f32[4,64,128]{2,1,0:T(8,128)S(1)} custom-call(f32[32,128]{1,0:T(8,128)S(1)} %get-tuple-element.12.base_ref.refs_3_.refs_4_, f32[2,32,128]{2,1,0:T(8,128)S(1)} %get-tuple-element.13.dirs_ref.refs_5_, s32[256,128]{1,0:T(8,128)S(1)} %bitcast.27, f32[32,32768]{1,0:T(8,128)S(1)} %copy-done), custom_call_target="tpu_custom_call" | custom-call | flops 4194304 | bytes 1048576 | tf_op jit(solution)/shard_map/third_sums/pallas_call | solution.py:312
  7.8 1.6 %collective-permute-start.2 = (f32[4,64,128]{2,1,0:T(8,128)S(1)}, f32[4,64,128]{2,1,0:T(8,128)S(1)}, u32[]{:S(2)}, u32[]{:S(2)}) collective-permute-start(f32[4,64,128]{2,1,0:T(8,128)S(1)} %third_sums.1), channel_id=1, source_target_pairs={{0,4},{1,3},{2,6},{3,1},{4,0},{5,7},{6,2},{7,5},{8,12},{9,11},{10,... | collective-permute-start | bytes 393224 | tf_op jit(solution)/shard_map/ppermute | solution.py:275
  9.4 0.0 collective-permute-start
  9.5 0.8 %own_sums.1 = f32[4,64,128]{2,1,0:T(8,128)S(1)} custom-call(f32[32,128]{1,0:T(8,128)S(1)} %get-tuple-element.12.base_ref.refs_3_.refs_4_, f32[2,32,128]{2,1,0:T(8,128)S(1)} %get-tuple-element.13.dirs_ref.refs_5_, s32[256,128]{1,0:T(8,128)S(1)} %bitcast.28, f32[32,32768]{1,0:T(8,128)S(1)} %copy-done), custom_call_target="tpu_custom_call" | custom-call | flops 4194304 | bytes 1048576 | tf_op jit(solution)/shard_map/own_sums/pallas_call | solution.py:312
  10.3 0.0 collective-permute-done.1
  10.3 3.8 %collective-permute-done.2 = f32[4,64,128]{2,1,0:T(8,128)S(1)} collective-permute-done((f32[4,64,128]{2,1,0:T(8,128)S(1)}, f32[4,64,128]{2,1,0:T(8,128)S(1)}, u32[]{:S(2)}, u32[]{:S(2)}) %collective-permute-start.2) | collective-permute-done | bytes 131104 | tf_op jit(solution)/shard_map/ppermute | solution.py:275
  14.1 1.2 %collective-permute-done = f32[4,64,128]{2,1,0:T(8,128)S(1)} collective-permute-done((f32[4,64,128]{2,1,0:T(8,128)S(1)}, f32[4,64,128]{2,1,0:T(8,128)S(1)}, u32[]{:S(2)}, u32[]{:S(2)}) %collective-permute-start) | collective-permute-done | bytes 131104 | tf_op jit(solution)/shard_map/ppermute | solution.py:275
  15.4 0.1 select_select_fusion.1
  15.5 3.0 %collective-permute-start.3 = (f32[4,64,128]{2,1,0:T(8,128)S(1)}, f32[4,64,128]{2,1,0:T(8,128)S(1)}, u32[]{:S(2)}, u32[]{:S(2)}) collective-permute-start(f32[4,64,128]{2,1,0:T(8,128)S(1)} %select_select_fusion.1), channel_id=1, source_target_pairs={{0,8},{1,9},{2,10},{3,11},{4,12},{5,13},{6,14},{7,15},{8,0},{9,1},... | collective-permute-start | bytes 393224 | tf_op jit(solution)/shard_map/ppermute | solution.py:275
  18.4 5.3 %collective-permute-done.3 = f32[4,64,128]{2,1,0:T(8,128)S(1)} collective-permute-done((f32[4,64,128]{2,1,0:T(8,128)S(1)}, f32[4,64,128]{2,1,0:T(8,128)S(1)}, u32[]{:S(2)}, u32[]{:S(2)}) %collective-permute-start.3) | collective-permute-done | bytes 131104 | tf_op jit(solution)/shard_map/ppermute | solution.py:275
  23.8 0.1 select_select_fusion.refs_0_
  23.9 1.4 %collective-permute-start.5 = (f32[4,64,128]{2,1,0:T(8,128)S(1)}, f32[4,64,128]{2,1,0:T(8,128)S(1)}, u32[]{:S(2)}, u32[]{:S(2)}) collective-permute-start(f32[4,64,128]{2,1,0:T(8,128)S(1)} %select_select_fusion.refs_0_), channel_id=1, source_target_pairs={{0,2},{1,5},{2,0},{3,7},{4,6},{5,1},{6,4},{7,3},{8,10},{9,13},{10,... | collective-permute-start | bytes 393224 | tf_op jit(solution)/shard_map/ppermute | solution.py:275
  25.3 0.0 collective-permute-start.4
  25.3 2.1 %collective-permute-start.6 = (f32[4,64,128]{2,1,0:T(8,128)S(1)}, f32[4,64,128]{2,1,0:T(8,128)S(1)}, u32[]{:S(2)}, u32[]{:S(2)}) collective-permute-start(f32[4,64,128]{2,1,0:T(8,128)S(1)} %select_select_fusion.refs_0_), channel_id=1, source_target_pairs={{0,4},{1,3},{2,6},{3,1},{4,0},{5,7},{6,2},{7,5},{8,12},{9,11},{10,... | collective-permute-start | bytes 393224 | tf_op jit(solution)/shard_map/ppermute | solution.py:275
  27.4 0.6 %tally.1.refs_6_ = f32[32,128]{1,0:T(8,128)S(1)} custom-call(s32[256,128]{1,0:T(8,128)S(1)} %bitcast.29), custom_call_target="tpu_custom_call" | custom-call | flops 4194304 | bytes 1048576 | tf_op jit(solution)/shard_map/tally/pallas_call | solution.py:319
  28.0 4.7 %collective-permute-done.5.refs_2_ = f32[4,64,128]{2,1,0:T(8,128)S(1)} collective-permute-done((f32[4,64,128]{2,1,0:T(8,128)S(1)}, f32[4,64,128]{2,1,0:T(8,128)S(1)}, u32[]{:S(2)}, u32[]{:S(2)}) %collective-permute-start.5) | collective-permute-done | bytes 131104 | tf_op jit(solution)/shard_map/ppermute | solution.py:275
  32.7 0.0 collective-permute-done.4.refs_1_
  32.7 1.1 %weigh.1.refs_7_ = f32[3,32,128]{2,1,0:T(8,128)S(1)} custom-call(f32[4,64,128]{2,1,0:T(8,128)S(1)} %select_select_fusion.refs_0_, f32[4,64,128]{2,1,0:T(8,128)S(1)} %collective-permute-done.4.refs_1_, f32[4,64,128]{2,1,0:T(8,128)S(1)} %collective-permute-done.5.refs_2_, f32[32,128]{1,0:T(8,128)S(1)} %get-tuple-element.12.base_ref.refs_3_.refs_4_, ...), custom_call_target="tpu_custom_call" | custom-call | flops 12582912 | bytes 3145728 | tf_op jit(solution)/shard_map/weigh/pallas_call | solution.py:325
  33.8 0.0 collective-permute-done.6.refs_3_
  33.8 0.8 %last_sums.1 = (f32[256,128]{1,0:T(8,128)}, f32[256,128]{1,0:T(8,128)}, f32[3,32]{1,0:T(4,128)S(1)}) custom-call(f32[4,64,128]{2,1,0:T(8,128)S(1)} %select_select_fusion.refs_0_, f32[4,64,128]{2,1,0:T(8,128)S(1)} %collective-permute-done.4.refs_1_, f32[4,64,128]{2,1,0:T(8,128)S(1)} %collective-permute-done.5.refs_2_, ...), custom_call_target="tpu_custom_call" | custom-call | flops 4194304 | bytes 1048576 | tf_op jit(solution)/shard_map/last_sums/pallas_call | solution.py:334
  34.6 0.1 collective-permute-start.7
  34.7 1.1 %collective-permute-done.7.other_ref = f32[3,32]{1,0:T(4,128)S(1)} collective-permute-done((f32[3,32]{1,0:T(4,128)S(1)}, f32[3,32]{1,0:T(4,128)S(1)}, u32[]{:S(2)}, u32[]{:S(2)}) %collective-permute-start.7) | collective-permute-done | bytes 416 | tf_op jit(solution)/shard_map/ppermute | solution.py:343
  35.8 0.6 %totals.1 = (f32[1,32]{1,0:T(1,128)}, f32[2,32]{1,0:T(2,128)}) custom-call(f32[3,32]{1,0:T(4,128)S(1)} %get-tuple-element.17.mine_ref, f32[3,32]{1,0:T(4,128)S(1)} %collective-permute-done.7.other_ref), custom_call_target="tpu_custom_call" | custom-call | flops 16384 | bytes 4096 | tf_op jit(solution)/shard_map/totals/pallas_call | solution.py:344
  (5 shorter events, 0.1 us)
Async XLA Ops:
  0.6 2.6 %copy-start = (f32[32,32768]{1,0:T(8,128)S(1)}, f32[32,32768]{1,0:T(8,128)}, u32[]{:S(2)}) copy-start(f32[32,32768]{1,0:T(8,128)} %refs_8_.1) | copy-start | bytes 12582916
  0.6 2.6 %copy-start.1 = (s32[32768]{0:T(1024)S(1)}, s32[32768]{0:T(1024)}, u32[]{:S(2)}) copy-start(s32[32768]{0:T(1024)} %param.7) | copy-start | bytes 393220
  4.0 6.3 %collective-permute-start.1 = (f32[4,64,128]{2,1,0:T(8,128)S(1)}, f32[4,64,128]{2,1,0:T(8,128)S(1)}, u32[]{:S(2)}, u32[]{:S(2)}) collective-permute-start(f32[4,64,128]{2,1,0:T(8,128)S(1)} %second_sums.1), channel_id=1, source_target_pairs={{0,2},{1,5},{2,0},{3,7},{4,6},{5,1},{6,4},{7,3},{8,10},{9,13},{10,... | collective-permute-start | bytes 393224 | tf_op jit(solution)/shard_map/ppermute | solution.py:275
  7.8 6.3 %collective-permute-start.2 = (f32[4,64,128]{2,1,0:T(8,128)S(1)}, f32[4,64,128]{2,1,0:T(8,128)S(1)}, u32[]{:S(2)}, u32[]{:S(2)}) collective-permute-start(f32[4,64,128]{2,1,0:T(8,128)S(1)} %third_sums.1), channel_id=1, source_target_pairs={{0,4},{1,3},{2,6},{3,1},{4,0},{5,7},{6,2},{7,5},{8,12},{9,11},{10,... | collective-permute-start | bytes 393224 | tf_op jit(solution)/shard_map/ppermute | solution.py:275
  9.4 5.9 %collective-permute-start = (f32[4,64,128]{2,1,0:T(8,128)S(1)}, f32[4,64,128]{2,1,0:T(8,128)S(1)}, u32[]{:S(2)}, u32[]{:S(2)}) collective-permute-start(f32[4,64,128]{2,1,0:T(8,128)S(1)} %get-tuple-element.14), channel_id=1, source_target_pairs={{0,6},{1,7},{2,4},{3,5},{4,2},{5,3},{6,0},{7,1},{8,14},{9,15},{10,... | collective-permute-start | bytes 393224 | tf_op jit(solution)/shard_map/ppermute | solution.py:275
  15.5 8.3 %collective-permute-start.3 = (f32[4,64,128]{2,1,0:T(8,128)S(1)}, f32[4,64,128]{2,1,0:T(8,128)S(1)}, u32[]{:S(2)}, u32[]{:S(2)}) collective-permute-start(f32[4,64,128]{2,1,0:T(8,128)S(1)} %select_select_fusion.1), channel_id=1, source_target_pairs={{0,8},{1,9},{2,10},{3,11},{4,12},{5,13},{6,14},{7,15},{8,0},{9,1},... | collective-permute-start | bytes 393224 | tf_op jit(solution)/shard_map/ppermute | solution.py:275
  23.9 8.8 %collective-permute-start.5 = (f32[4,64,128]{2,1,0:T(8,128)S(1)}, f32[4,64,128]{2,1,0:T(8,128)S(1)}, u32[]{:S(2)}, u32[]{:S(2)}) collective-permute-start(f32[4,64,128]{2,1,0:T(8,128)S(1)} %select_select_fusion.refs_0_), channel_id=1, source_target_pairs={{0,2},{1,5},{2,0},{3,7},{4,6},{5,1},{6,4},{7,3},{8,10},{9,13},{10,... | collective-permute-start | bytes 393224 | tf_op jit(solution)/shard_map/ppermute | solution.py:275
  25.3 7.4 %collective-permute-start.4 = (f32[4,64,128]{2,1,0:T(8,128)S(1)}, f32[4,64,128]{2,1,0:T(8,128)S(1)}, u32[]{:S(2)}, u32[]{:S(2)}) collective-permute-start(f32[4,64,128]{2,1,0:T(8,128)S(1)} %select_select_fusion.refs_0_), channel_id=1, source_target_pairs={{0,6},{1,7},{2,4},{3,5},{4,2},{5,3},{6,0},{7,1},{8,14},{9,15},{10,... | collective-permute-start | bytes 393224 | tf_op jit(solution)/shard_map/ppermute | solution.py:275
  25.3 8.5 %collective-permute-start.6 = (f32[4,64,128]{2,1,0:T(8,128)S(1)}, f32[4,64,128]{2,1,0:T(8,128)S(1)}, u32[]{:S(2)}, u32[]{:S(2)}) collective-permute-start(f32[4,64,128]{2,1,0:T(8,128)S(1)} %select_select_fusion.refs_0_), channel_id=1, source_target_pairs={{0,4},{1,3},{2,6},{3,1},{4,0},{5,7},{6,2},{7,5},{8,12},{9,11},{10,... | collective-permute-start | bytes 393224 | tf_op jit(solution)/shard_map/ppermute | solution.py:275
  34.6 1.2 %collective-permute-start.7 = (f32[3,32]{1,0:T(4,128)S(1)}, f32[3,32]{1,0:T(4,128)S(1)}, u32[]{:S(2)}, u32[]{:S(2)}) collective-permute-start(f32[3,32]{1,0:T(4,128)S(1)} %get-tuple-element.17.mine_ref), channel_id=1, source_target_pairs={{0,1},{1,0},{2,3},{3,2},{4,5},{5,4},{6,7},{7,6},{8,9},{9,8},{10,11... | collective-permute-start | bytes 1160 | tf_op jit(solution)/shard_map/ppermute | solution.py:343

commit v3 on v2

--- a/solution.py
+++ b/solution.py
@@ -107,42 +107,50 @@
     lax.fori_loop(0, steps, step, 0)
 
 
-def first_body(flips, counts_hbm, free_hbm, dirs_hbm, labels_hbm, energies_hbm, out_ref, base_out, dirs_out, *scratch):
-    counts_s, free_s, dirs_s, labels_s, energies_s, sems = scratch
+def first_body(flips, counts_hbm, free_hbm, dirs_hbm, labels_hbm, energies_hbm, *refs):
+    out_ref, base_ref, dirs_ref, labels_ref, energies_ref, counts_s, free_s, dirs_s, sems = refs
     states, samples = energies_hbm.shape
     width = samples // 4
-    chunks = energies_s.shape[0]
-    chunk = width // chunks
+    pieces = sems.shape[0] - 7
+    piece = width // pieces
     quarter = spot(flips)
-    rows = width // LANES
+    first_state = lax.axis_index("state") * states
+
+    def energy_copy(start, size, sem):
+        at = pl.ds(pl.multiple_of(start, size), size)
+        return pltpu.make_async_copy(energies_hbm.at[:, at], energies_ref.at[:, at], sems.at[sem])
+
     small = [
         pltpu.make_async_copy(counts_hbm, counts_s, sems.at[0]),
         pltpu.make_async_copy(free_hbm, free_s, sems.at[1]),
         pltpu.make_async_copy(dirs_hbm, dirs_s, sems.at[2]),
-        pltpu.make_async_copy(labels_hbm.at[pl.ds(pl.multiple_of(quarter * rows, rows), rows), :], labels_s, sems.at[3]),
+        pltpu.make_async_copy(labels_hbm, labels_ref, sems.at[3]),
     ]
-    large = [
-        pltpu.make_async_copy(
-            energies_hbm.at[:, pl.ds(pl.multiple_of(quarter * width + c * chunk, chunk), chunk)],
-            energies_s.at[c],
-            sems.at[4 + c],
-        )
-        for c in range(chunks)
-    ]
-    for copy in small + large:
+    near = [energy_copy(quarter * width + i * piece, piece, 7 + i) for i in range(pieces)]
+    rest = [energy_copy(jnp.bitwise_xor(quarter, i) * width, width, 3 + i) for i in range(1, 4)]
+    for copy in small + near + rest:
         copy.start()
     for copy in small:
         copy.wait()
-    base_out[...] = bases(counts_s, free_s, states)
-    dirs_out[0] = column(dirs_s[0:1, :], states)
-    dirs_out[1] = column(dirs_s[1:2, :], states)
-    first_state = lax.axis_index("state") * states
-    for c, copy in enumerate(large):
+    base_ref[...] = bases(counts_s, free_s, states)
+    dirs_ref[0] = column(dirs_s[0:1, :], states)
+    dirs_ref[1] = column(dirs_s[1:2, :], states)
+    rows = piece // LANES
+    for i, copy in enumerate(near):
         copy.wait()
-        part = out_ref.at[:, pl.ds(c * (rows // chunks), rows // chunks), :]
         sums_of(
-            part, energies_s.at[c], 0, labels_s, c * (rows // chunks), base_out, dirs_out, first_state, chunk // TILE
+            out_ref.at[:, pl.ds(i * rows, rows), :],
+            energies_ref,
+            quarter * width + i * piece,
+            labels_ref,
+            quarter * (width // LANES) + i * rows,
+            base_ref,
+            dirs_ref,
+            first_state,
+            piece // TILE,
         )
+    for copy in rest:
+        copy.wait()
 
 
 def later_body(flips, base_ref, dirs_ref, labels_ref, energies_ref, out_ref):
@@ -188,49 +196,62 @@
     return lax.fori_loop(0, width // TILE, step, (zero, zero, zero))
 
 
-def weigh_body(flips, *refs):
-    n = len(flips)
-    part_refs = refs[:n]
-    base_ref, energies_ref, sums_ref = refs[n:]
-    for k in range(n):
-        for i, x in enumerate(weigh(part_refs[k], energies_ref, spot(flips[k]), base_ref)):
-            if k == 0:
-                sums_ref[i] = x
-            else:
-                sums_ref[i] += x
-
-
-def last_body(flips, *refs):
+def weigh_body(flips, part_ref, base_ref, energies_ref, *refs):
+    *before, sums_ref = refs
+    for i, x in enumerate(weigh(part_ref, energies_ref, spot(flips), base_ref)):
+        sums_ref[i] = x + before[0][i] if before else x
+
+
+def last_body(flips, part_ref, base_ref, energies_ref, before_ref, dirs_ref, tally_ref, out_ref):
+    sums = weigh(part_ref, energies_ref, spot(flips), base_ref)
+    states = energies_ref.shape[0]
+    eye = lax.broadcasted_iota(jnp.int32, (states, states), 0) == lax.broadcasted_iota(jnp.int32, (states, states), 1)
+
+    def row(x):
+        total = jnp.broadcast_to(jnp.sum(x, axis=1, keepdims=True), (states, states))
+        return jnp.sum(jnp.where(eye, total, 0.0), axis=0, keepdims=True)
+
+    occupancy = sums[0] + before_ref[0]
+    out_ref[0:1, :] = row(occupancy - tally_ref[...])
+    for j in range(2):
+        out_ref[j + 1 : j + 2, :] = row(dirs_ref[j] * occupancy - (sums[j + 1] + before_ref[j + 1]))
+
+
+def total_body(flips, scale, *refs):
     part_refs = refs[:4]
-    base_ref, dirs_ref, tally_ref, sums_ref, energies_ref, norm_hbm, anchor_hbm, out_ref, sems = refs[4:]
-    states, samples = energies_ref.shape
-    rows = samples // 4 // LANES
+    mine_ref, other_ref, norm_hbm, anchor_hbm, gradient_hbm, products_hbm, gradient_s, products_s, sems = refs[4:]
+    rows = norm_hbm.shape[0] // 4
     copies = []
     for k, part_ref in enumerate(part_refs):
         at = pl.ds(pl.multiple_of(spot(flips[k]) * rows, rows), rows)
         copies.append(pltpu.make_async_copy(part_ref.at[0], norm_hbm.at[at, :], sems.at[2 * k]))
         copies.append(pltpu.make_async_copy(part_ref.at[3], anchor_hbm.at[at, :], sems.at[2 * k + 1]))
-    for copy in copies:
+    copies.append(pltpu.make_async_copy(gradient_s, gradient_hbm, sems.at[8]))
+    copies.append(pltpu.make_async_copy(products_s, products_hbm, sems.at[9]))
+    for copy in copies[:8]:
         copy.start()
-    sums = weigh(part_refs[3], energies_ref, spot(flips[3]), base_ref)
-    eye = lax.broadcasted_iota(jnp.int32, (states, states), 0) == lax.broadcasted_iota(jnp.int32, (states, states), 1)
-
-    def row(x):
-        total = jnp.broadcast_to(jnp.sum(x, axis=1, keepdims=True), (states, states))
-        return jnp.sum(jnp.where(eye, total, 0.0), axis=0, keepdims=True)
-
-    occupancy = sums[0] + sums_ref[0]
-    out_ref[0:1, :] = row(occupancy - tally_ref[...])
-    for j in range(2):
-        out_ref[j + 1 : j + 2, :] = row(dirs_ref[j] * occupancy - (sums[j + 1] + sums_ref[j + 1]))
+    total = scale * (mine_ref[...] + other_ref[...])
+    gradient_s[...] = total[0:1]
+    products_s[...] = total[1:3]
+    for copy in copies[8:]:
+        copy.start()
     for copy in copies:
         copy.wait()
 
 
-def total_body(scale, mine_ref, other_ref, gradient_ref, products_ref):
-    total = scale * (mine_ref[...] + other_ref[...])
-    gradient_ref[...] = total[0:1]
-    products_ref[...] = total[1:3]
+def merge_body(last, *refs):
+    *parts, out_ref = refs
+    norms = [part[0] for part in parts]
+    peak = functools.reduce(jnp.maximum, norms)
+    scales = [jnp.exp(norm - peak) for norm in norms]
+    total = functools.reduce(jnp.add, scales)
+    inverse = 1.0 / total
+    norm = peak + jnp.log(total)
+    anchor = functools.reduce(jnp.add, [part[3] for part in parts])
+    out_ref[0] = norm
+    for j in (1, 2):
+        out_ref[j] = functools.reduce(jnp.add, [s * part[j] for s, part in zip(scales, parts, strict=True)]) * inverse
+    out_ref[3] = anchor - norm if last else anchor
 
 
 VMEM = pl.BlockSpec(memory_space=pltpu.VMEM)
@@ -250,21 +271,9 @@
         out_shape=out_shape,
         scratch_shapes=list(scratch),
         compiler_params=pltpu.CompilerParams(vmem_limit_bytes=LIMIT),
-        cost_estimate=pl.CostEstimate(flops=16 * work, bytes_accessed=4 * work, transcendentals=work),
+        cost_estimate=pl.CostEstimate(flops=work // 1024, bytes_accessed=1024, transcendentals=0),
         name=name,
     )
-
-
-def merge(parts, last):
-    norms = [part[0:1] for part in parts]
-    peak = functools.reduce(jnp.maximum, norms)
-    scales = [jnp.exp(norm - peak) for norm in norms]
-    total = functools.reduce(jnp.add, scales)
-    mixed = functools.reduce(jnp.add, [s * part for s, part in zip(scales, parts, strict=True)]) / total
-    anchor = functools.reduce(jnp.add, parts)
-    norm = peak + jnp.log(total)
-    kind = lax.broadcasted_iota(jnp.int32, parts[0].shape, 0)
-    return jnp.where(kind == 0, norm, jnp.where(kind == 3, anchor - norm if last else anchor, mixed))
 
 
 def swap(x, width, cores, flips):
@@ -284,22 +293,26 @@
     work = states * samples // 4
     labels = labels.reshape(samples // LANES, LANES)
     part = f32(4, rows, LANES)
-    chunks = 2 if samples % (8 * TILE) == 0 else 1
-
-    first, base, dirs = kernel(
+    pieces = 2 if samples % (8 * TILE) == 0 else 1
+
+    first, base, dirs, labels, energies = kernel(
         functools.partial(first_body, rounds[0]),
         [HBM] * 5,
-        [VMEM] * 3,
-        [part, f32(states, LANES), f32(2, states, LANES)],
+        [VMEM] * 5,
+        [
+            part,
+            f32(states, LANES),
+            f32(2, states, LANES),
+            jax.ShapeDtypeStruct(labels.shape, labels.dtype),
+            f32(states, samples),
+        ],
         "first_sums",
         work,
         [
             pltpu.VMEM((1, states), jnp.int32),
             pltpu.VMEM((1, states), jnp.float32),
             pltpu.VMEM((2, states), jnp.float32),
-            pltpu.VMEM((rows, LANES), jnp.int32),
-            pltpu.VMEM((chunks, states, samples // 4 // chunks), jnp.float32),
-            pltpu.SemaphoreType.DMA((4 + chunks,)),
+            pltpu.SemaphoreType.DMA((7 + pieces,)),
         ],
     )(
         *(
@@ -313,42 +326,44 @@
             base, dirs, labels, energies
         )
 
+    def merge(parts, last, name):
+        return kernel(functools.partial(merge_body, last), [VMEM] * len(parts), VMEM, part, name, 4 * rows * LANES)(
+            *parts
+        )
+
+    def weigh_quarter(flips, x, before, name):
+        args = [x, base, energies, *before]
+        return kernel(
+            functools.partial(weigh_body, flips), [VMEM] * len(args), VMEM, f32(3, states, LANES), name, work
+        )(*args)
+
     sent = [first, later(rounds[1], "second_sums"), later(rounds[2], "third_sums")]
     got = [swap(x, width, cores, flips) for x, flips in zip(sent, rounds, strict=True)]
     own = later(stay, "own_sums")
     tally = kernel(tally_body, [VMEM], VMEM, f32(states, LANES), "tally", work)(labels)
     far = range(2, int(math.log2(width)))
-    union = merge([own, *got], not far)
+    union = merge([own, got[0]], False, "merge_first")
+    union = merge([union, got[1], got[2]], not far, "merge_square")
     for bit in far:
-        union = merge([union, swap(union, width, cores, (1 << bit,) * cores)], bit == far[-1])
+        union = merge([union, swap(union, width, cores, (1 << bit,) * cores)], bit == far[-1], "merge_far")
     others = [swap(union, width, cores, flips) for flips in rounds]
-    sums = kernel(
-        functools.partial(weigh_body, (stay, rounds[0], rounds[1])),
-        [VMEM] * 5,
-        VMEM,
-        f32(3, states, LANES),
-        "weigh",
-        3 * work,
-    )(union, others[0], others[1], base, energies)
+    sums = weigh_quarter(stay, union, [], "weigh_own")
+    sums = weigh_quarter(rounds[0], others[0], [sums], "weigh_first")
+    sums = weigh_quarter(rounds[1], others[1], [sums], "weigh_second")
+    mine = kernel(
+        functools.partial(last_body, rounds[2]), [VMEM] * 6, VMEM, f32(3, states), "last_sums", work
+    )(others[2], base, energies, sums, dirs, tally)
+    other = lax.ppermute(mine, "sample", [(c, cores - 1 - c) for c in range(cores)])
     long = f32(samples // LANES, LANES)
-    log_norm, anchor_logp, mine = kernel(
-        functools.partial(last_body, (stay, *rounds)),
-        [VMEM] * 9,
-        [HBM, HBM, VMEM],
-        [long, long, f32(3, states)],
-        "last_sums",
-        work,
-        [pltpu.SemaphoreType.DMA((8,))],
-    )(union, *others, base, dirs, tally, sums, energies)
-    other = lax.ppermute(mine, "sample", [(c, cores - 1 - c) for c in range(cores)])
-    gradient, products = kernel(
-        functools.partial(total_body, states * width / (samples * cores)),
-        [VMEM] * 2,
-        [VMEM] * 2,
-        [f32(1, states), f32(2, states)],
+    log_norm, anchor_logp, gradient, products = kernel(
+        functools.partial(total_body, (stay, *rounds), states * width / (samples * cores)),
+        [VMEM] * 6,
+        [HBM] * 4,
+        [long, long, f32(1, states), f32(2, states)],
         "totals",
         1024,
-    )(mine, other)
+        [pltpu.VMEM((1, states), jnp.float32), pltpu.VMEM((2, states), jnp.float32), pltpu.SemaphoreType.DMA((10,))],
+    )(union, *others, mine, other)
     return log_norm.reshape(samples), anchor_logp.reshape(samples), gradient.reshape(states), products
 
 

time: 36.6 us -> 34.3 us (0.937)
  waiting for transfers between devices: 16.2 us -> 14.7 us
  local copies, waits for them, and re-layouts: 0.49 us -> 0 us
    ppermute x7, waiting for transfers between devices: 15 us -> 13.5 us  [swap(): return lax.ppermute(x, ('state', 'sample'), pairs)]
    unnamed x4 -> x0, local copies, waits for them, and re-layouts: 0.49 us -> none
    pallas_call x4 -> x9, Pallas kernels: 4.51 us -> 4.85 us  [the longest x1 2.37 us: local(): kernel(functools.partial(first_body, rounds[0]), [HBM] * 5, [VMEM] * 5, [...]
  transfers between devices with their start and end apart: 8 -> 8, of which waited for: 5 -> 7; matrix products, arithmetic and copies ran while one was open for 0% -> 0% of each run, Pallas kernels for 9% -> 12%
where the time goes in v3:
time: 34.3 us; the launch traced here: 34.1 us
  waiting for transfers between devices  14.7 us (43%)
  starting transfers between devices  11 us (32%)
  Pallas kernels  7.77 us (23%)
  between operations  0.71 us (2%)
    ppermute x7, waiting for transfers between devices, swap(): return lax.ppermute(x, ('state', 'sample'), pairs)  13.5 us
    ppermute x7, starting transfers between devices, swap(): return lax.ppermute(x, ('state', 'sample'), pairs)  10.9 us
    pallas_call x1, Pallas kernels, local(): kernel(functools.partial(first_body, rounds[0]), [HBM] * 5, [VMEM] * 5, [...  2.37 us
    pallas_call x3, Pallas kernels, later(): kernel(functools.partial(later_body, flips), [VMEM] * 4, VMEM, part, name...  2.34 us
    ppermute x1, waiting for transfers between devices, local(): lax.ppermute(mine, 'sample', [(c, cores - 1 - c) for c in range(cores)])  1.14 us
    pallas_call x3, Pallas kernels, weigh_quarter(): kernel(functools.partial(weigh_body, flips), [VMEM] * len(args), VMEM, f3...  1.11 us
    pallas_call x1, Pallas kernels, local(): kernel(functools.partial(total_body, (stay, *rounds), states * width / (s...  0.78 us
  transfers between devices with their start and end apart: 8, of which 7 were waited for; matrix products, arithmetic and copies ran while one was open for 0% of the time, Pallas kernels for 12%

profile of v3, /device:TPU:0, one launch (start us, length us, event | category | flops | bytes accessed | tf_op | source)
XLA Modules:
  0.0 34.1 jit_solution(4550427466085143235)
XLA Ops:
  0.6 2.4 %first_sums.1 = (f32[4,64,128]{2,1,0:T(8,128)S(1)}, f32[32,128]{1,0:T(8,128)S(1)}, f32[2,32,128]{2,1,0:T(8,128)S(1)}, s32[256,128]{1,0:T(8,128)S(1)}, f32[32,32768]{1,0:T(8,128)S(1)}) custom-call(s32[1,32]{1,0:T(1,128)} %bitcast.7, f32[1,32]{1,0:T(1,128)} %bitcast.8, f32[2,32]{1,0:T(2,128)} %dirs_hbm.1, s32[256,128]{1,0:T(8,128)} %bitcast.6, ...), custom_call_target="tpu_custom_call" | custom-call | flops 256 | bytes 1024 | tf_op jit(solution)/shard_map/first_sums/pallas_call | solution.py:298
  3.0 4.0 %collective-permute-start = (f32[4,64,128]{2,1,0:T(8,128)S(1)}, f32[4,64,128]{2,1,0:T(8,128)S(1)}, u32[]{:S(2)}, u32[]{:S(2)}) collective-permute-start(f32[4,64,128]{2,1,0:T(8,128)S(1)} %get-tuple-element.17), channel_id=1, source_target_pairs={{0,6},{1,7},{2,4},{3,5},{4,2},{5,3},{6,0},{7,1},{8,14},{9,15},{10,... | collective-permute-start | bytes 393224 | tf_op jit(solution)/shard_map/ppermute | solution.py:284
  7.0 0.8 %second_sums.1 = f32[4,64,128]{2,1,0:T(8,128)S(1)} custom-call(f32[32,128]{1,0:T(8,128)S(1)} %get-tuple-element.13.base_ref, f32[2,32,128]{2,1,0:T(8,128)S(1)} %get-tuple-element.14.dirs_ref, s32[256,128]{1,0:T(8,128)S(1)} %get-tuple-element.15.labels_ref, f32[32,32768]{1,0:T(8,128)S(1)} %get-tuple-element.16.energies_ref), custom_call_target="tpu_custom_call" | custom-call | flops 256 | bytes 1024 | tf_op jit(solution)/shard_map/second_sums/pallas_call | solution.py:325
  7.8 0.6 %collective-permute-start.1 = (f32[4,64,128]{2,1,0:T(8,128)S(1)}, f32[4,64,128]{2,1,0:T(8,128)S(1)}, u32[]{:S(2)}, u32[]{:S(2)}) collective-permute-start(f32[4,64,128]{2,1,0:T(8,128)S(1)} %second_sums.1), channel_id=1, source_target_pairs={{0,2},{1,5},{2,0},{3,7},{4,6},{5,1},{6,4},{7,3},{8,10},{9,13},{10,... | collective-permute-start | bytes 393224 | tf_op jit(solution)/shard_map/ppermute | solution.py:284
  8.4 0.8 %third_sums.1 = f32[4,64,128]{2,1,0:T(8,128)S(1)} custom-call(f32[32,128]{1,0:T(8,128)S(1)} %get-tuple-element.13.base_ref, f32[2,32,128]{2,1,0:T(8,128)S(1)} %get-tuple-element.14.dirs_ref, s32[256,128]{1,0:T(8,128)S(1)} %get-tuple-element.15.labels_ref, f32[32,32768]{1,0:T(8,128)S(1)} %get-tuple-element.16.energies_ref), custom_call_target="tpu_custom_call" | custom-call | flops 256 | bytes 1024 | tf_op jit(solution)/shard_map/third_sums/pallas_call | solution.py:325
  9.2 0.1 collective-permute-start.2
  9.3 0.8 %own_sums.1.refs_0_ = f32[4,64,128]{2,1,0:T(8,128)S(1)} custom-call(f32[32,128]{1,0:T(8,128)S(1)} %get-tuple-element.13.base_ref, f32[2,32,128]{2,1,0:T(8,128)S(1)} %get-tuple-element.14.dirs_ref, s32[256,128]{1,0:T(8,128)S(1)} %get-tuple-element.15.labels_ref, f32[32,32768]{1,0:T(8,128)S(1)} %get-tuple-element.16.energies_ref), custom_call_target="tpu_custom_call" | custom-call | flops 256 | bytes 1024 | tf_op jit(solution)/shard_map/own_sums/pallas_call | solution.py:325
  10.1 0.9 %collective-permute-done.refs_1_ = f32[4,64,128]{2,1,0:T(8,128)S(1)} collective-permute-done((f32[4,64,128]{2,1,0:T(8,128)S(1)}, f32[4,64,128]{2,1,0:T(8,128)S(1)}, u32[]{:S(2)}, u32[]{:S(2)}) %collective-permute-start) | collective-permute-done | bytes 131104 | tf_op jit(solution)/shard_map/ppermute | solution.py:284
  11.0 2.8 %collective-permute-done.1.refs_1_ = f32[4,64,128]{2,1,0:T(8,128)S(1)} collective-permute-done((f32[4,64,128]{2,1,0:T(8,128)S(1)}, f32[4,64,128]{2,1,0:T(8,128)S(1)}, u32[]{:S(2)}, u32[]{:S(2)}) %collective-permute-start.1) | collective-permute-done | bytes 131104 | tf_op jit(solution)/shard_map/ppermute | solution.py:284
  13.9 0.4 %collective-permute-done.2.refs_2_ = f32[4,64,128]{2,1,0:T(8,128)S(1)} collective-permute-done((f32[4,64,128]{2,1,0:T(8,128)S(1)}, f32[4,64,128]{2,1,0:T(8,128)S(1)}, u32[]{:S(2)}, u32[]{:S(2)}) %collective-permute-start.2) | collective-permute-done | bytes 131104 | tf_op jit(solution)/shard_map/ppermute | solution.py:284
  14.3 2.7 %collective-permute-start.3 = (f32[4,64,128]{2,1,0:T(8,128)S(1)}, f32[4,64,128]{2,1,0:T(8,128)S(1)}, u32[]{:S(2)}, u32[]{:S(2)}) collective-permute-start(f32[4,64,128]{2,1,0:T(8,128)S(1)} %merge_square.1.refs_0_), channel_id=1, source_target_pairs={{0,8},{1,9},{2,10},{3,11},{4,12},{5,13},{6,14},{7,15},{8,0},{9,1},... | collective-permute-start | bytes 393224 | tf_op jit(solution)/shard_map/ppermute | solution.py:284
  16.9 6.1 %collective-permute-done.3.refs_1_ = f32[4,64,128]{2,1,0:T(8,128)S(1)} collective-permute-done((f32[4,64,128]{2,1,0:T(8,128)S(1)}, f32[4,64,128]{2,1,0:T(8,128)S(1)}, u32[]{:S(2)}, u32[]{:S(2)}) %collective-permute-start.3) | collective-permute-done | bytes 131104 | tf_op jit(solution)/shard_map/ppermute | solution.py:284
  23.0 1.3 %collective-permute-start.4 = (f32[4,64,128]{2,1,0:T(8,128)S(1)}, f32[4,64,128]{2,1,0:T(8,128)S(1)}, u32[]{:S(2)}, u32[]{:S(2)}) collective-permute-start(f32[4,64,128]{2,1,0:T(8,128)S(1)} %merge_far.1.part_ref.refs_0_), channel_id=1, source_target_pairs={{0,6},{1,7},{2,4},{3,5},{4,2},{5,3},{6,0},{7,1},{8,14},{9,15},{10,... | collective-permute-start | bytes 393224 | tf_op jit(solution)/shard_map/ppermute | solution.py:284
  24.3 0.9 %collective-permute-start.5 = (f32[4,64,128]{2,1,0:T(8,128)S(1)}, f32[4,64,128]{2,1,0:T(8,128)S(1)}, u32[]{:S(2)}, u32[]{:S(2)}) collective-permute-start(f32[4,64,128]{2,1,0:T(8,128)S(1)} %merge_far.1.part_ref.refs_0_), channel_id=1, source_target_pairs={{0,2},{1,5},{2,0},{3,7},{4,6},{5,1},{6,4},{7,3},{8,10},{9,13},{10,... | collective-permute-start | bytes 393224 | tf_op jit(solution)/shard_map/ppermute | solution.py:284
  25.3 1.3 %collective-permute-start.6 = (f32[4,64,128]{2,1,0:T(8,128)S(1)}, f32[4,64,128]{2,1,0:T(8,128)S(1)}, u32[]{:S(2)}, u32[]{:S(2)}) collective-permute-start(f32[4,64,128]{2,1,0:T(8,128)S(1)} %merge_far.1.part_ref.refs_0_), channel_id=1, source_target_pairs={{0,4},{1,3},{2,6},{3,1},{4,0},{5,7},{6,2},{7,5},{8,12},{9,11},{10,... | collective-permute-start | bytes 393224 | tf_op jit(solution)/shard_map/ppermute | solution.py:284
  26.6 0.6 %tally.1.tally_ref = f32[32,128]{1,0:T(8,128)S(1)} custom-call(s32[256,128]{1,0:T(8,128)S(1)} %get-tuple-element.15.labels_ref), custom_call_target="tpu_custom_call" | custom-call | flops 256 | bytes 1024 | tf_op jit(solution)/shard_map/tally/pallas_call | solution.py:343
  27.2 0.4 %weigh_own.1.refs_0_ = f32[3,32,128]{2,1,0:T(8,128)S(1)} custom-call(f32[4,64,128]{2,1,0:T(8,128)S(1)} %merge_far.1.part_ref.refs_0_, f32[32,128]{1,0:T(8,128)S(1)} %get-tuple-element.13.base_ref, f32[32,32768]{1,0:T(8,128)S(1)} %get-tuple-element.16.energies_ref), custom_call_target="tpu_custom_call" | custom-call | flops 256 | bytes 1024 | tf_op jit(solution)/shard_map/weigh_own/pallas_call | solution.py:336
  27.6 2.4 %collective-permute-done.4.part_ref.refs_1_ = f32[4,64,128]{2,1,0:T(8,128)S(1)} collective-permute-done((f32[4,64,128]{2,1,0:T(8,128)S(1)}, f32[4,64,128]{2,1,0:T(8,128)S(1)}, u32[]{:S(2)}, u32[]{:S(2)}) %collective-permute-start.4) | collective-permute-done | bytes 131104 | tf_op jit(solution)/shard_map/ppermute | solution.py:284
  30.0 0.4 %weigh_first.1.refs_0_ = f32[3,32,128]{2,1,0:T(8,128)S(1)} custom-call(f32[4,64,128]{2,1,0:T(8,128)S(1)} %collective-permute-done.4.part_ref.refs_1_, f32[32,128]{1,0:T(8,128)S(1)} %get-tuple-element.13.base_ref, f32[32,32768]{1,0:T(8,128)S(1)} %get-tuple-element.16.energies_ref, f32[3,32,128]{2,1,0:T(8,128)S(1)} %weigh_own.1.refs_0_), custom_call_target="tpu_custom_call" | custom-call | flops 256 | bytes 1024 | tf_op jit(solution)/shard_map/weigh_first/pallas_call | solution.py:336
  30.3 0.9 %collective-permute-done.5.part_ref.refs_2_ = f32[4,64,128]{2,1,0:T(8,128)S(1)} collective-permute-done((f32[4,64,128]{2,1,0:T(8,128)S(1)}, f32[4,64,128]{2,1,0:T(8,128)S(1)}, u32[]{:S(2)}, u32[]{:S(2)}) %collective-permute-start.5) | collective-permute-done | bytes 131104 | tf_op jit(solution)/shard_map/ppermute | solution.py:284
  31.3 0.4 %weigh_second.1.before_ref = f32[3,32,128]{2,1,0:T(8,128)S(1)} custom-call(f32[4,64,128]{2,1,0:T(8,128)S(1)} %collective-permute-done.5.part_ref.refs_2_, f32[32,128]{1,0:T(8,128)S(1)} %get-tuple-element.13.base_ref, f32[32,32768]{1,0:T(8,128)S(1)} %get-tuple-element.16.energies_ref, f32[3,32,128]{2,1,0:T(8,128)S(1)} %weigh_first.1.refs_0_), custom_call_target="tpu_custom_call" | custom-call | flops 256 | bytes 1024 | tf_op jit(solution)/shard_map/weigh_second/pallas_call | solution.py:336
  31.6 0.0 collective-permute-done.6.part_ref.refs_3_
  31.7 0.5 %last_sums.1.refs_4_ = f32[3,32]{1,0:T(4,128)S(1)} custom-call(f32[4,64,128]{2,1,0:T(8,128)S(1)} %collective-permute-done.6.part_ref.refs_3_, f32[32,128]{1,0:T(8,128)S(1)} %get-tuple-element.13.base_ref, f32[32,32768]{1,0:T(8,128)S(1)} %get-tuple-element.16.energies_ref, f32[3,32,128]{2,1,0:T(8,128)S(1)} %weigh_second.1.before_ref, ...), custom_call_target="tpu_custom_call" | custom-call | flops 256 | bytes 1024 | tf_op jit(solution)/shard_map/last_sums/pallas_call | solution.py:353
  32.1 0.1 collective-permute-start.7
  32.2 1.1 %collective-permute-done.7.refs_5_ = f32[3,32]{1,0:T(4,128)S(1)} collective-permute-done((f32[3,32]{1,0:T(4,128)S(1)}, f32[3,32]{1,0:T(4,128)S(1)}, u32[]{:S(2)}, u32[]{:S(2)}) %collective-permute-start.7) | collective-permute-done | bytes 416 | tf_op jit(solution)/shard_map/ppermute | solution.py:356
  33.4 0.8 %totals.1 = (f32[256,128]{1,0:T(8,128)}, f32[256,128]{1,0:T(8,128)}, f32[1,32]{1,0:T(1,128)}, f32[2,32]{1,0:T(2,128)}) custom-call(f32[4,64,128]{2,1,0:T(8,128)S(1)} %merge_far.1.part_ref.refs_0_, f32[4,64,128]{2,1,0:T(8,128)S(1)} %collective-permute-done.4.part_ref.refs_1_, f32[4,64,128]{2,1,0:T(8,128)S(1)} %collective-permute-done.5.part_ref.refs_2_, ...), custom_call_target="tpu_custom_call" | custom-call | flops 1 | bytes 1024 | tf_op jit(solution)/shard_map/totals/pallas_call | solution.py:358
  (3 shorter events, 0.1 us)
Async XLA Ops:
  3.0 8.0 %collective-permute-start = (f32[4,64,128]{2,1,0:T(8,128)S(1)}, f32[4,64,128]{2,1,0:T(8,128)S(1)}, u32[]{:S(2)}, u32[]{:S(2)}) collective-permute-start(f32[4,64,128]{2,1,0:T(8,128)S(1)} %get-tuple-element.17), channel_id=1, source_target_pairs={{0,6},{1,7},{2,4},{3,5},{4,2},{5,3},{6,0},{7,1},{8,14},{9,15},{10,... | collective-permute-start | bytes 393224 | tf_op jit(solution)/shard_map/ppermute | solution.py:284
  7.8 6.0 %collective-permute-start.1 = (f32[4,64,128]{2,1,0:T(8,128)S(1)}, f32[4,64,128]{2,1,0:T(8,128)S(1)}, u32[]{:S(2)}, u32[]{:S(2)}) collective-permute-start(f32[4,64,128]{2,1,0:T(8,128)S(1)} %second_sums.1), channel_id=1, source_target_pairs={{0,2},{1,5},{2,0},{3,7},{4,6},{5,1},{6,4},{7,3},{8,10},{9,13},{10,... | collective-permute-start | bytes 393224 | tf_op jit(solution)/shard_map/ppermute | solution.py:284
  9.2 5.0 %collective-permute-start.2 = (f32[4,64,128]{2,1,0:T(8,128)S(1)}, f32[4,64,128]{2,1,0:T(8,128)S(1)}, u32[]{:S(2)}, u32[]{:S(2)}) collective-permute-start(f32[4,64,128]{2,1,0:T(8,128)S(1)} %third_sums.1), channel_id=1, source_target_pairs={{0,4},{1,3},{2,6},{3,1},{4,0},{5,7},{6,2},{7,5},{8,12},{9,11},{10,... | collective-permute-start | bytes 393224 | tf_op jit(solution)/shard_map/ppermute | solution.py:284
  14.3 8.7 %collective-permute-start.3 = (f32[4,64,128]{2,1,0:T(8,128)S(1)}, f32[4,64,128]{2,1,0:T(8,128)S(1)}, u32[]{:S(2)}, u32[]{:S(2)}) collective-permute-start(f32[4,64,128]{2,1,0:T(8,128)S(1)} %merge_square.1.refs_0_), channel_id=1, source_target_pairs={{0,8},{1,9},{2,10},{3,11},{4,12},{5,13},{6,14},{7,15},{8,0},{9,1},... | collective-permute-start | bytes 393224 | tf_op jit(solution)/shard_map/ppermute | solution.py:284
  23.0 6.9 %collective-permute-start.4 = (f32[4,64,128]{2,1,0:T(8,128)S(1)}, f32[4,64,128]{2,1,0:T(8,128)S(1)}, u32[]{:S(2)}, u32[]{:S(2)}) collective-permute-start(f32[4,64,128]{2,1,0:T(8,128)S(1)} %merge_far.1.part_ref.refs_0_), channel_id=1, source_target_pairs={{0,6},{1,7},{2,4},{3,5},{4,2},{5,3},{6,0},{7,1},{8,14},{9,15},{10,... | collective-permute-start | bytes 393224 | tf_op jit(solution)/shard_map/ppermute | solution.py:284
  24.3 6.9 %collective-permute-start.5 = (f32[4,64,128]{2,1,0:T(8,128)S(1)}, f32[4,64,128]{2,1,0:T(8,128)S(1)}, u32[]{:S(2)}, u32[]{:S(2)}) collective-permute-start(f32[4,64,128]{2,1,0:T(8,128)S(1)} %merge_far.1.part_ref.refs_0_), channel_id=1, source_target_pairs={{0,2},{1,5},{2,0},{3,7},{4,6},{5,1},{6,4},{7,3},{8,10},{9,13},{10,... | collective-permute-start | bytes 393224 | tf_op jit(solution)/shard_map/ppermute | solution.py:284
  25.3 6.4 %collective-permute-start.6 = (f32[4,64,128]{2,1,0:T(8,128)S(1)}, f32[4,64,128]{2,1,0:T(8,128)S(1)}, u32[]{:S(2)}, u32[]{:S(2)}) collective-permute-start(f32[4,64,128]{2,1,0:T(8,128)S(1)} %merge_far.1.part_ref.refs_0_), channel_id=1, source_target_pairs={{0,4},{1,3},{2,6},{3,1},{4,0},{5,7},{6,2},{7,5},{8,12},{9,11},{10,... | collective-permute-start | bytes 393224 | tf_op jit(solution)/shard_map/ppermute | solution.py:284
  32.1 1.2 %collective-permute-start.7 = (f32[3,32]{1,0:T(4,128)S(1)}, f32[3,32]{1,0:T(4,128)S(1)}, u32[]{:S(2)}, u32[]{:S(2)}) collective-permute-start(f32[3,32]{1,0:T(4,128)S(1)} %last_sums.1.refs_4_), channel_id=1, source_target_pairs={{0,1},{1,0},{2,3},{3,2},{4,5},{5,4},{6,7},{7,6},{8,9},{9,8},{10,11... | collective-permute-start | bytes 1160 | tf_op jit(solution)/shard_map/ppermute | solution.py:356

commit v4 on v3

--- a/solution.py
+++ b/solution.py
@@ -11,6 +11,9 @@
 LANES = 128
 ROWS = 8
 TILE = LANES * ROWS
+CHUNKS = 1
+FORWARD = True
+RELAY = False
 
 
 def plan(level, shift):
@@ -111,13 +114,13 @@
     out_ref, base_ref, dirs_ref, labels_ref, energies_ref, counts_s, free_s, dirs_s, sems = refs
     states, samples = energies_hbm.shape
     width = samples // 4
-    pieces = sems.shape[0] - 7
-    piece = width // pieces
+    size = out_ref.shape[1] * LANES
+    pieces = sems.shape[0] - 8
+    piece = size // pieces
     quarter = spot(flips)
-    first_state = lax.axis_index("state") * states
 
     def energy_copy(start, size, sem):
-        at = pl.ds(pl.multiple_of(start, size), size)
+        at = pl.ds(pl.multiple_of(start, LANES), size)
         return pltpu.make_async_copy(energies_hbm.at[:, at], energies_ref.at[:, at], sems.at[sem])
 
     small = [
@@ -126,8 +129,10 @@
         pltpu.make_async_copy(dirs_hbm, dirs_s, sems.at[2]),
         pltpu.make_async_copy(labels_hbm, labels_ref, sems.at[3]),
     ]
-    near = [energy_copy(quarter * width + i * piece, piece, 7 + i) for i in range(pieces)]
+    near = [energy_copy(quarter * width + i * piece, piece, 8 + i) for i in range(pieces)]
     rest = [energy_copy(jnp.bitwise_xor(quarter, i) * width, width, 3 + i) for i in range(1, 4)]
+    if size < width:
+        rest.append(energy_copy(quarter * width + size, width - size, 7))
     for copy in small + near + rest:
         copy.start()
     for copy in small:
@@ -136,6 +141,7 @@
     dirs_ref[0] = column(dirs_s[0:1, :], states)
     dirs_ref[1] = column(dirs_s[1:2, :], states)
     rows = piece // LANES
+    first_state = lax.axis_index("state") * states
     for i, copy in enumerate(near):
         copy.wait()
         sums_of(
@@ -153,13 +159,14 @@
         copy.wait()
 
 
-def later_body(flips, base_ref, dirs_ref, labels_ref, energies_ref, out_ref):
+def later_body(flips, chunk, base_ref, dirs_ref, labels_ref, energies_ref, out_ref):
     states, samples = energies_ref.shape
-    width = samples // 4
+    width, rows = samples // 4, out_ref.shape[1]
     quarter = spot(flips)
     first_state = lax.axis_index("state") * states
-    offset, row = quarter * width, quarter * (width // LANES)
-    sums_of(out_ref, energies_ref, offset, labels_ref, row, base_ref, dirs_ref, first_state, width // TILE)
+    row = quarter * (width // LANES) + chunk * rows
+    offset = quarter * width + chunk * rows * LANES
+    sums_of(out_ref, energies_ref, offset, labels_ref, row, base_ref, dirs_ref, first_state, rows * LANES // TILE)
 
 
 def tally_body(labels_ref, tally_ref):
@@ -176,16 +183,17 @@
     tally_ref[...] = lax.fori_loop(0, labels_ref.shape[0] // ROWS, step, jnp.zeros((states, LANES), jnp.float32))
 
 
-def weigh(part_ref, energies_ref, quarter, base_ref):
+def weigh(part_ref, energies_ref, quarter, chunk, base_ref):
     states, samples = energies_ref.shape
-    width = samples // 4
+    size = part_ref.shape[1] * LANES
+    offset = quarter * (samples // 4) + chunk * size
 
     def step(j, carry):
         occupancy, mix0, mix1 = carry
         at = pl.ds(pl.multiple_of(j * ROWS, ROWS), ROWS)
         norm, first, second = part_ref[0, at, :], part_ref[1, at, :], part_ref[2, at, :]
         for g in range(ROWS):
-            cols = pl.ds(pl.multiple_of(quarter * width + j * TILE + g * LANES, LANES), LANES)
+            cols = pl.ds(pl.multiple_of(offset + j * TILE + g * LANES, LANES), LANES)
             w = jnp.exp((base_ref[...] - energies_ref[:, cols]) - spread(norm, g, states))
             occupancy += w
             mix0 += w * spread(first, g, states)
@@ -193,17 +201,20 @@
         return occupancy, mix0, mix1
 
     zero = jnp.zeros((states, LANES), jnp.float32)
-    return lax.fori_loop(0, width // TILE, step, (zero, zero, zero))
-
-
-def weigh_body(flips, part_ref, base_ref, energies_ref, *refs):
+    return lax.fori_loop(0, size // TILE, step, (zero, zero, zero))
+
+
+def weigh_body(flips, chunk, part_ref, base_ref, energies_ref, *refs):
     *before, sums_ref = refs
-    for i, x in enumerate(weigh(part_ref, energies_ref, spot(flips), base_ref)):
+    for i, x in enumerate(weigh(part_ref, energies_ref, spot(flips), chunk, base_ref)):
         sums_ref[i] = x + before[0][i] if before else x
 
 
-def last_body(flips, part_ref, base_ref, energies_ref, before_ref, dirs_ref, tally_ref, out_ref):
-    sums = weigh(part_ref, energies_ref, spot(flips), base_ref)
+def last_body(flips, chunk, part_ref, base_ref, energies_ref, dirs_ref, tally_ref, *refs):
+    *before, out_ref = refs
+    sums = list(weigh(part_ref, energies_ref, spot(flips), chunk, base_ref))
+    for ref in before:
+        sums = [x + ref[i] for i, x in enumerate(sums)]
     states = energies_ref.shape[0]
     eye = lax.broadcasted_iota(jnp.int32, (states, states), 0) == lax.broadcasted_iota(jnp.int32, (states, states), 1)
 
@@ -211,29 +222,30 @@
         total = jnp.broadcast_to(jnp.sum(x, axis=1, keepdims=True), (states, states))
         return jnp.sum(jnp.where(eye, total, 0.0), axis=0, keepdims=True)
 
-    occupancy = sums[0] + before_ref[0]
-    out_ref[0:1, :] = row(occupancy - tally_ref[...])
+    out_ref[0:1, :] = row(sums[0] - tally_ref[...])
     for j in range(2):
-        out_ref[j + 1 : j + 2, :] = row(dirs_ref[j] * occupancy - (sums[j + 1] + before_ref[j + 1]))
+        out_ref[j + 1 : j + 2, :] = row(dirs_ref[j] * sums[0] - sums[j + 1])
 
 
 def total_body(flips, scale, *refs):
-    part_refs = refs[:4]
-    mine_ref, other_ref, norm_hbm, anchor_hbm, gradient_hbm, products_hbm, gradient_s, products_s, sems = refs[4:]
-    rows = norm_hbm.shape[0] // 4
+    *part_refs, mine_ref, other_ref, norm_hbm, anchor_hbm, gradient_hbm, products_hbm = refs[:-3]
+    gradient_s, products_s, sems = refs[-3:]
+    n = len(part_refs)
+    rows = part_refs[0].shape[1]
     copies = []
     for k, part_ref in enumerate(part_refs):
-        at = pl.ds(pl.multiple_of(spot(flips[k]) * rows, rows), rows)
+        start = spot(flips[k // CHUNKS]) * (rows * CHUNKS) + (k % CHUNKS) * rows
+        at = pl.ds(pl.multiple_of(start, ROWS), rows)
         copies.append(pltpu.make_async_copy(part_ref.at[0], norm_hbm.at[at, :], sems.at[2 * k]))
         copies.append(pltpu.make_async_copy(part_ref.at[3], anchor_hbm.at[at, :], sems.at[2 * k + 1]))
-    copies.append(pltpu.make_async_copy(gradient_s, gradient_hbm, sems.at[8]))
-    copies.append(pltpu.make_async_copy(products_s, products_hbm, sems.at[9]))
-    for copy in copies[:8]:
+    copies.append(pltpu.make_async_copy(gradient_s, gradient_hbm, sems.at[2 * n]))
+    copies.append(pltpu.make_async_copy(products_s, products_hbm, sems.at[2 * n + 1]))
+    for copy in copies[: 2 * n]:
         copy.start()
     total = scale * (mine_ref[...] + other_ref[...])
     gradient_s[...] = total[0:1]
     products_s[...] = total[1:3]
-    for copy in copies[8:]:
+    for copy in copies[2 * n :]:
         copy.start()
     for copy in copies:
         copy.wait()
@@ -287,16 +299,17 @@
 def local(energies, counts, labels, free_energy, directions):
     states, samples = energies.shape
     width, cores = lax.axis_size("state"), lax.axis_size("sample")
-    rounds = [(3,) * cores, tuple(1 + c % 2 for c in range(cores)), tuple(2 - c % 2 for c in range(cores))]
-    stay = (0,) * cores
-    rows = samples // 4 // LANES
-    work = states * samples // 4
+    near = tuple(1 + c % 2 for c in range(cores))
+    side = tuple(2 - c % 2 for c in range(cores))
+    across, stay = (3,) * cores, (0,) * cores
+    rows = samples // 4 // LANES // CHUNKS
+    work = states * rows * LANES
     labels = labels.reshape(samples // LANES, LANES)
     part = f32(4, rows, LANES)
-    pieces = 2 if samples % (8 * TILE) == 0 else 1
+    pieces = 2 if rows % (2 * ROWS) == 0 else 1
 
     first, base, dirs, labels, energies = kernel(
-        functools.partial(first_body, rounds[0]),
+        functools.partial(first_body, across),
         [HBM] * 5,
         [VMEM] * 5,
         [
@@ -312,7 +325,7 @@
             pltpu.VMEM((1, states), jnp.int32),
             pltpu.VMEM((1, states), jnp.float32),
             pltpu.VMEM((2, states), jnp.float32),
-            pltpu.SemaphoreType.DMA((7 + pieces,)),
+            pltpu.SemaphoreType.DMA((8 + pieces,)),
         ],
     )(
         *(
@@ -321,49 +334,71 @@
         )
     )
 
-    def later(flips, name):
-        return kernel(functools.partial(later_body, flips), [VMEM] * 4, VMEM, part, name, work)(
-            base, dirs, labels, energies
-        )
+    def sums_for(flips, chunk, name):
+        if chunk == 0 and flips == across:
+            return first
+        body = functools.partial(later_body, flips, chunk)
+        return kernel(body, [VMEM] * 4, VMEM, part, f"{name}_{chunk}", work)(base, dirs, labels, energies)
 
     def merge(parts, last, name):
-        return kernel(functools.partial(merge_body, last), [VMEM] * len(parts), VMEM, part, name, 4 * rows * LANES)(
-            *parts
-        )
-
-    def weigh_quarter(flips, x, before, name):
+        return kernel(functools.partial(merge_body, last), [VMEM] * len(parts), VMEM, part, name, work)(*parts)
+
+    def send(x, flips):
+        return swap(x, width, cores, flips)
+
+    def weigh_part(flips, chunk, x, before, name):
         args = [x, base, energies, *before]
-        return kernel(
-            functools.partial(weigh_body, flips), [VMEM] * len(args), VMEM, f32(3, states, LANES), name, work
-        )(*args)
-
-    sent = [first, later(rounds[1], "second_sums"), later(rounds[2], "third_sums")]
-    got = [swap(x, width, cores, flips) for x, flips in zip(sent, rounds, strict=True)]
-    own = later(stay, "own_sums")
+        body = functools.partial(weigh_body, flips, chunk)
+        return kernel(body, [VMEM] * len(args), VMEM, f32(3, states, LANES), f"{name}_{chunk}", work)(*args)
+
+    far = range(2, int(math.log2(width)))
     tally = kernel(tally_body, [VMEM], VMEM, f32(states, LANES), "tally", work)(labels)
-    far = range(2, int(math.log2(width)))
-    union = merge([own, got[0]], False, "merge_first")
-    union = merge([union, got[1], got[2]], not far, "merge_square")
-    for bit in far:
-        union = merge([union, swap(union, width, cores, (1 << bit,) * cores)], bit == far[-1], "merge_far")
-    others = [swap(union, width, cores, flips) for flips in rounds]
-    sums = weigh_quarter(stay, union, [], "weigh_own")
-    sums = weigh_quarter(rounds[0], others[0], [sums], "weigh_first")
-    sums = weigh_quarter(rounds[1], others[1], [sums], "weigh_second")
-    mine = kernel(
-        functools.partial(last_body, rounds[2]), [VMEM] * 6, VMEM, f32(3, states), "last_sums", work
-    )(others[2], base, energies, sums, dirs, tally)
+    found = []
+    for chunk in range(CHUNKS):
+        if FORWARD:
+            got_side = send(sums_for(across, chunk, "across"), near)
+            got = send(sums_for(near, chunk, "near"), near)
+            pair = merge([sums_for(side, chunk, "side"), got_side], False, f"merge_side_{chunk}")
+            union = merge([sums_for(stay, chunk, "own"), got], False, f"merge_near_{chunk}")
+            union = merge([union, send(pair, side)], not far, f"merge_square_{chunk}")
+        else:
+            got = [send(sums_for(flips, chunk, f"sums{k}"), flips) for k, flips in enumerate((across, near, side))]
+            union = merge([sums_for(stay, chunk, "own"), got[0]], False, f"merge_across_{chunk}")
+            union = merge([union, got[1], got[2]], not far, f"merge_square_{chunk}")
+        for bit in far:
+            union = merge([union, send(union, (1 << bit,) * cores)], bit == far[-1], f"merge_far_{chunk}")
+        if RELAY:
+            from_side = send(union, side)
+            found.append([(stay, union), (side, from_side), (near, send(union, near)), (across, send(from_side, near))])
+        else:
+            found.append([(stay, union)] + [(flips, send(union, flips)) for flips in (across, near, side)])
+    sums = []
+    for chunk, parts in enumerate(found):
+        before = []
+        for k, (flips, x) in enumerate(parts[:-1] if chunk == CHUNKS - 1 else parts):
+            before = [weigh_part(flips, chunk, x, before, f"weigh{k}")]
+        sums += before
+    flips, x = found[-1][-1]
+    body = functools.partial(last_body, flips, CHUNKS - 1)
+    mine = kernel(body, [VMEM] * (5 + len(sums)), VMEM, f32(3, states), "last_sums", work)(
+        x, base, energies, dirs, tally, *sums
+    )
     other = lax.ppermute(mine, "sample", [(c, cores - 1 - c) for c in range(cores)])
     long = f32(samples // LANES, LANES)
+    ends = [parts[k][1] for k in range(4) for parts in found]
     log_norm, anchor_logp, gradient, products = kernel(
-        functools.partial(total_body, (stay, *rounds), states * width / (samples * cores)),
-        [VMEM] * 6,
+        functools.partial(total_body, tuple(p[0] for p in found[0]), states * width / (samples * cores)),
+        [VMEM] * (len(ends) + 2),
         [HBM] * 4,
         [long, long, f32(1, states), f32(2, states)],
         "totals",
         1024,
-        [pltpu.VMEM((1, states), jnp.float32), pltpu.VMEM((2, states), jnp.float32), pltpu.SemaphoreType.DMA((10,))],
-    )(union, *others, mine, other)
+        [
+            pltpu.VMEM((1, states), jnp.float32),
+            pltpu.VMEM((2, states), jnp.float32),
+            pltpu.SemaphoreType.DMA((2 * len(ends) + 2,)),
+        ],
+    )(*ends, mine, other)
     return log_norm.reshape(samples), anchor_logp.reshape(samples), gradient.reshape(states), products
 
 

time: 34.3 us -> 33 us (0.962)
  waiting for transfers between devices: 14.7 us -> 12.3 us
  starting transfers between devices: 11 us -> 12 us
    ppermute x7, waiting for transfers between devices: 13.5 us -> 11.2 us  [swap(): return lax.ppermute(x, ('state', 'sample'), pairs)]
    ppermute x7, starting transfers between devices: 10.9 us -> 11.9 us  [swap(): return lax.ppermute(x, ('state', 'sample'), pairs)]
where the time goes in v4:
time: 33 us; the launch traced here: 32.8 us
  waiting for transfers between devices  12.3 us (37%)
  starting transfers between devices  12 us (36%)
  Pallas kernels  7.8 us (24%)
  between operations  0.71 us (2%)
    ppermute x7, starting transfers between devices, swap(): return lax.ppermute(x, ('state', 'sample'), pairs)  11.9 us
    ppermute x7, waiting for transfers between devices, swap(): return lax.ppermute(x, ('state', 'sample'), pairs)  11.2 us
    pallas_call x1, Pallas kernels, local(): kernel(functools.partial(first_body, across), [HBM] * 5, [VMEM] * 5, [par...  2.38 us
    pallas_call x3, Pallas kernels, sums_for(): kernel(body, [VMEM] * 4, VMEM, part, f'{name}_{chunk}', work)  2.34 us
    ppermute x1, waiting for transfers between devices, local(): lax.ppermute(mine, 'sample', [(c, cores - 1 - c) for c in range(cores)])  1.14 us
    pallas_call x3, Pallas kernels, weigh_part(): kernel(body, [VMEM] * len(args), VMEM, f32(3, states, LANES), f'{name}_{c...  1.1 us
    pallas_call x1, Pallas kernels, local(): kernel(functools.partial(total_body, tuple((p[0] for p in found[0])), sta...  0.78 us
  transfers between devices with their start and end apart: 8, of which 7 were waited for; matrix products, arithmetic and copies ran while one was open for 0% of the time, Pallas kernels for 12%

profile of v4, /device:TPU:0, one launch (start us, length us, event | category | flops | bytes accessed | tf_op | source)
XLA Modules:
  0.0 32.8 jit_solution(7473794665010359228)
XLA Ops:
  0.6 2.4 %first_sums.1 = (f32[4,64,128]{2,1,0:T(8,128)S(1)}, f32[32,128]{1,0:T(8,128)S(1)}, f32[2,32,128]{2,1,0:T(8,128)S(1)}, s32[256,128]{1,0:T(8,128)S(1)}, f32[32,32768]{1,0:T(8,128)S(1)}) custom-call(s32[1,32]{1,0:T(1,128)} %bitcast.7, f32[1,32]{1,0:T(1,128)} %bitcast.8, f32[2,32]{1,0:T(2,128)} %dirs_hbm.1, s32[256,128]{1,0:T(8,128)} %bitcast.6, ...), custom_call_target="tpu_custom_call" | custom-call | flops 256 | bytes 1024 | tf_op jit(solution)/shard_map/first_sums/pallas_call | solution.py:311
  3.0 3.0 %collective-permute-start.1 = (f32[4,64,128]{2,1,0:T(8,128)S(1)}, f32[4,64,128]{2,1,0:T(8,128)S(1)}, u32[]{:S(2)}, u32[]{:S(2)}) collective-permute-start(f32[4,64,128]{2,1,0:T(8,128)S(1)} %get-tuple-element.17), channel_id=1, source_target_pairs={{0,2},{1,5},{2,0},{3,7},{4,6},{5,1},{6,4},{7,3},{8,10},{9,13},{10,... | collective-permute-start | bytes 393224 | tf_op jit(solution)/shard_map/ppermute | solution.py:296
  6.0 0.8 %near_0.1 = f32[4,64,128]{2,1,0:T(8,128)S(1)} custom-call(f32[32,128]{1,0:T(8,128)S(1)} %get-tuple-element.13.base_ref, f32[2,32,128]{2,1,0:T(8,128)S(1)} %get-tuple-element.14.dirs_ref, s32[256,128]{1,0:T(8,128)S(1)} %get-tuple-element.15.labels_ref, f32[32,32768]{1,0:T(8,128)S(1)} %get-tuple-element.16.energies_ref), custom_call_target="tpu_custom_call" | custom-call | flops 256 | bytes 1024 | tf_op jit(solution)/shard_map/near_0/pallas_call | solution.py:341
  6.8 0.1 collective-permute-start
  6.9 0.8 %side_0.1.refs_0_ = f32[4,64,128]{2,1,0:T(8,128)S(1)} custom-call(f32[32,128]{1,0:T(8,128)S(1)} %get-tuple-element.13.base_ref, f32[2,32,128]{2,1,0:T(8,128)S(1)} %get-tuple-element.14.dirs_ref, s32[256,128]{1,0:T(8,128)S(1)} %get-tuple-element.15.labels_ref, f32[32,32768]{1,0:T(8,128)S(1)} %get-tuple-element.16.energies_ref), custom_call_target="tpu_custom_call" | custom-call | flops 256 | bytes 1024 | tf_op jit(solution)/shard_map/side_0/pallas_call | solution.py:341
  7.7 1.3 %collective-permute-done.1.refs_1_ = f32[4,64,128]{2,1,0:T(8,128)S(1)} collective-permute-done((f32[4,64,128]{2,1,0:T(8,128)S(1)}, f32[4,64,128]{2,1,0:T(8,128)S(1)}, u32[]{:S(2)}, u32[]{:S(2)}) %collective-permute-start.1) | collective-permute-done | bytes 131104 | tf_op jit(solution)/shard_map/ppermute | solution.py:296
  9.0 2.2 %collective-permute-start.2 = (f32[4,64,128]{2,1,0:T(8,128)S(1)}, f32[4,64,128]{2,1,0:T(8,128)S(1)}, u32[]{:S(2)}, u32[]{:S(2)}) collective-permute-start(f32[4,64,128]{2,1,0:T(8,128)S(1)} %merge_side_0.1), channel_id=1, source_target_pairs={{0,4},{1,3},{2,6},{3,1},{4,0},{5,7},{6,2},{7,5},{8,12},{9,11},{10,... | collective-permute-start | bytes 393224 | tf_op jit(solution)/shard_map/ppermute | solution.py:296
  11.2 0.8 %own_0.1.refs_0_ = f32[4,64,128]{2,1,0:T(8,128)S(1)} custom-call(f32[32,128]{1,0:T(8,128)S(1)} %get-tuple-element.13.base_ref, f32[2,32,128]{2,1,0:T(8,128)S(1)} %get-tuple-element.14.dirs_ref, s32[256,128]{1,0:T(8,128)S(1)} %get-tuple-element.15.labels_ref, f32[32,32768]{1,0:T(8,128)S(1)} %get-tuple-element.16.energies_ref), custom_call_target="tpu_custom_call" | custom-call | flops 256 | bytes 1024 | tf_op jit(solution)/shard_map/own_0/pallas_call | solution.py:341
  12.0 0.8 %collective-permute-done.refs_1_ = f32[4,64,128]{2,1,0:T(8,128)S(1)} collective-permute-done((f32[4,64,128]{2,1,0:T(8,128)S(1)}, f32[4,64,128]{2,1,0:T(8,128)S(1)}, u32[]{:S(2)}, u32[]{:S(2)}) %collective-permute-start) | collective-permute-done | bytes 131104 | tf_op jit(solution)/shard_map/ppermute | solution.py:296
  12.8 1.4 %collective-permute-done.2.refs_1_ = f32[4,64,128]{2,1,0:T(8,128)S(1)} collective-permute-done((f32[4,64,128]{2,1,0:T(8,128)S(1)}, f32[4,64,128]{2,1,0:T(8,128)S(1)}, u32[]{:S(2)}, u32[]{:S(2)}) %collective-permute-start.2) | collective-permute-done | bytes 131104 | tf_op jit(solution)/shard_map/ppermute | solution.py:296
  14.2 3.1 %collective-permute-start.3 = (f32[4,64,128]{2,1,0:T(8,128)S(1)}, f32[4,64,128]{2,1,0:T(8,128)S(1)}, u32[]{:S(2)}, u32[]{:S(2)}) collective-permute-start(f32[4,64,128]{2,1,0:T(8,128)S(1)} %merge_square_0.1.refs_0_), channel_id=1, source_target_pairs={{0,8},{1,9},{2,10},{3,11},{4,12},{5,13},{6,14},{7,15},{8,0},{9,1},... | collective-permute-start | bytes 393224 | tf_op jit(solution)/shard_map/ppermute | solution.py:296
  17.3 5.3 %collective-permute-done.3.refs_1_ = f32[4,64,128]{2,1,0:T(8,128)S(1)} collective-permute-done((f32[4,64,128]{2,1,0:T(8,128)S(1)}, f32[4,64,128]{2,1,0:T(8,128)S(1)}, u32[]{:S(2)}, u32[]{:S(2)}) %collective-permute-start.3) | collective-permute-done | bytes 131104 | tf_op jit(solution)/shard_map/ppermute | solution.py:296
  22.6 1.0 %collective-permute-start.4 = (f32[4,64,128]{2,1,0:T(8,128)S(1)}, f32[4,64,128]{2,1,0:T(8,128)S(1)}, u32[]{:S(2)}, u32[]{:S(2)}) collective-permute-start(f32[4,64,128]{2,1,0:T(8,128)S(1)} %merge_far_0.1.part_ref.refs_0_), channel_id=1, source_target_pairs={{0,6},{1,7},{2,4},{3,5},{4,2},{5,3},{6,0},{7,1},{8,14},{9,15},{10,... | collective-permute-start | bytes 393224 | tf_op jit(solution)/shard_map/ppermute | solution.py:296
  23.6 1.2 %collective-permute-start.5 = (f32[4,64,128]{2,1,0:T(8,128)S(1)}, f32[4,64,128]{2,1,0:T(8,128)S(1)}, u32[]{:S(2)}, u32[]{:S(2)}) collective-permute-start(f32[4,64,128]{2,1,0:T(8,128)S(1)} %merge_far_0.1.part_ref.refs_0_), channel_id=1, source_target_pairs={{0,2},{1,5},{2,0},{3,7},{4,6},{5,1},{6,4},{7,3},{8,10},{9,13},{10,... | collective-permute-start | bytes 393224 | tf_op jit(solution)/shard_map/ppermute | solution.py:296
  24.8 1.4 %collective-permute-start.6 = (f32[4,64,128]{2,1,0:T(8,128)S(1)}, f32[4,64,128]{2,1,0:T(8,128)S(1)}, u32[]{:S(2)}, u32[]{:S(2)}) collective-permute-start(f32[4,64,128]{2,1,0:T(8,128)S(1)} %merge_far_0.1.part_ref.refs_0_), channel_id=1, source_target_pairs={{0,4},{1,3},{2,6},{3,1},{4,0},{5,7},{6,2},{7,5},{8,12},{9,11},{10,... | collective-permute-start | bytes 393224 | tf_op jit(solution)/shard_map/ppermute | solution.py:296
  26.2 0.6 %tally.1.tally_ref = f32[32,128]{1,0:T(8,128)S(1)} custom-call(s32[256,128]{1,0:T(8,128)S(1)} %get-tuple-element.15.labels_ref), custom_call_target="tpu_custom_call" | custom-call | flops 256 | bytes 1024 | tf_op jit(solution)/shard_map/tally/pallas_call | solution.py:355
  26.7 0.4 %weigh0_0.1.refs_0_ = f32[3,32,128]{2,1,0:T(8,128)S(1)} custom-call(f32[4,64,128]{2,1,0:T(8,128)S(1)} %merge_far_0.1.part_ref.refs_0_, f32[32,128]{1,0:T(8,128)S(1)} %get-tuple-element.13.base_ref, f32[32,32768]{1,0:T(8,128)S(1)} %get-tuple-element.16.energies_ref), custom_call_target="tpu_custom_call" | custom-call | flops 256 | bytes 1024 | tf_op jit(solution)/shard_map/weigh0_0/pallas_call | solution.py:352
  27.1 1.5 %collective-permute-done.4.part_ref.refs_1_ = f32[4,64,128]{2,1,0:T(8,128)S(1)} collective-permute-done((f32[4,64,128]{2,1,0:T(8,128)S(1)}, f32[4,64,128]{2,1,0:T(8,128)S(1)}, u32[]{:S(2)}, u32[]{:S(2)}) %collective-permute-start.4) | collective-permute-done | bytes 131104 | tf_op jit(solution)/shard_map/ppermute | solution.py:296
  28.6 0.4 %weigh1_0.1.refs_0_ = f32[3,32,128]{2,1,0:T(8,128)S(1)} custom-call(f32[4,64,128]{2,1,0:T(8,128)S(1)} %collective-permute-done.4.part_ref.refs_1_, f32[32,128]{1,0:T(8,128)S(1)} %get-tuple-element.13.base_ref, f32[32,32768]{1,0:T(8,128)S(1)} %get-tuple-element.16.energies_ref, f32[3,32,128]{2,1,0:T(8,128)S(1)} %weigh0_0.1.refs_0_), custom_call_target="tpu_custom_call" | custom-call | flops 256 | bytes 1024 | tf_op jit(solution)/shard_map/weigh1_0/pallas_call | solution.py:352
  29.0 0.9 %collective-permute-done.5.part_ref.refs_2_ = f32[4,64,128]{2,1,0:T(8,128)S(1)} collective-permute-done((f32[4,64,128]{2,1,0:T(8,128)S(1)}, f32[4,64,128]{2,1,0:T(8,128)S(1)}, u32[]{:S(2)}, u32[]{:S(2)}) %collective-permute-start.5) | collective-permute-done | bytes 131104 | tf_op jit(solution)/shard_map/ppermute | solution.py:296
  29.9 0.4 %weigh2_0.1.refs_0_ = f32[3,32,128]{2,1,0:T(8,128)S(1)} custom-call(f32[4,64,128]{2,1,0:T(8,128)S(1)} %collective-permute-done.5.part_ref.refs_2_, f32[32,128]{1,0:T(8,128)S(1)} %get-tuple-element.13.base_ref, f32[32,32768]{1,0:T(8,128)S(1)} %get-tuple-element.16.energies_ref, f32[3,32,128]{2,1,0:T(8,128)S(1)} %weigh1_0.1.refs_0_), custom_call_target="tpu_custom_call" | custom-call | flops 256 | bytes 1024 | tf_op jit(solution)/shard_map/weigh2_0/pallas_call | solution.py:352
  30.3 0.0 collective-permute-done.6.part_ref.refs_3_
  30.3 0.5 %last_sums.1.refs_4_ = f32[3,32]{1,0:T(4,128)S(1)} custom-call(f32[4,64,128]{2,1,0:T(8,128)S(1)} %collective-permute-done.6.part_ref.refs_3_, f32[32,128]{1,0:T(8,128)S(1)} %get-tuple-element.13.base_ref, f32[32,32768]{1,0:T(8,128)S(1)} %get-tuple-element.16.energies_ref, f32[2,32,128]{2,1,0:T(8,128)S(1)} %get-tuple-element.14.dirs_ref, ...), custom_call_target="tpu_custom_call" | custom-call | flops 256 | bytes 1024 | tf_op jit(solution)/shard_map/last_sums/pallas_call | solution.py:383
  30.8 0.1 collective-permute-start.7
  30.9 1.1 %collective-permute-done.7.refs_5_ = f32[3,32]{1,0:T(4,128)S(1)} collective-permute-done((f32[3,32]{1,0:T(4,128)S(1)}, f32[3,32]{1,0:T(4,128)S(1)}, u32[]{:S(2)}, u32[]{:S(2)}) %collective-permute-start.7) | collective-permute-done | bytes 416 | tf_op jit(solution)/shard_map/ppermute | solution.py:386
  32.0 0.8 %totals.1 = (f32[256,128]{1,0:T(8,128)}, f32[256,128]{1,0:T(8,128)}, f32[1,32]{1,0:T(1,128)}, f32[2,32]{1,0:T(2,128)}) custom-call(f32[4,64,128]{2,1,0:T(8,128)S(1)} %merge_far_0.1.part_ref.refs_0_, f32[4,64,128]{2,1,0:T(8,128)S(1)} %collective-permute-done.4.part_ref.refs_1_, f32[4,64,128]{2,1,0:T(8,128)S(1)} %collective-permute-done.5.part_ref.refs_2_, ...), custom_call_target="tpu_custom_call" | custom-call | flops 1 | bytes 1024 | tf_op jit(solution)/shard_map/totals/pallas_call | solution.py:389
  (4 shorter events, 0.1 us)
Async XLA Ops:
  3.0 6.0 %collective-permute-start.1 = (f32[4,64,128]{2,1,0:T(8,128)S(1)}, f32[4,64,128]{2,1,0:T(8,128)S(1)}, u32[]{:S(2)}, u32[]{:S(2)}) collective-permute-start(f32[4,64,128]{2,1,0:T(8,128)S(1)} %get-tuple-element.17), channel_id=1, source_target_pairs={{0,2},{1,5},{2,0},{3,7},{4,6},{5,1},{6,4},{7,3},{8,10},{9,13},{10,... | collective-permute-start | bytes 393224 | tf_op jit(solution)/shard_map/ppermute | solution.py:296
  6.8 5.9 %collective-permute-start = (f32[4,64,128]{2,1,0:T(8,128)S(1)}, f32[4,64,128]{2,1,0:T(8,128)S(1)}, u32[]{:S(2)}, u32[]{:S(2)}) collective-permute-start(f32[4,64,128]{2,1,0:T(8,128)S(1)} %near_0.1), channel_id=1, source_target_pairs={{0,2},{1,5},{2,0},{3,7},{4,6},{5,1},{6,4},{7,3},{8,10},{9,13},{10,... | collective-permute-start | bytes 393224 | tf_op jit(solution)/shard_map/ppermute | solution.py:296
  9.0 5.1 %collective-permute-start.2 = (f32[4,64,128]{2,1,0:T(8,128)S(1)}, f32[4,64,128]{2,1,0:T(8,128)S(1)}, u32[]{:S(2)}, u32[]{:S(2)}) collective-permute-start(f32[4,64,128]{2,1,0:T(8,128)S(1)} %merge_side_0.1), channel_id=1, source_target_pairs={{0,4},{1,3},{2,6},{3,1},{4,0},{5,7},{6,2},{7,5},{8,12},{9,11},{10,... | collective-permute-start | bytes 393224 | tf_op jit(solution)/shard_map/ppermute | solution.py:296
  14.2 8.4 %collective-permute-start.3 = (f32[4,64,128]{2,1,0:T(8,128)S(1)}, f32[4,64,128]{2,1,0:T(8,128)S(1)}, u32[]{:S(2)}, u32[]{:S(2)}) collective-permute-start(f32[4,64,128]{2,1,0:T(8,128)S(1)} %merge_square_0.1.refs_0_), channel_id=1, source_target_pairs={{0,8},{1,9},{2,10},{3,11},{4,12},{5,13},{6,14},{7,15},{8,0},{9,1},... | collective-permute-start | bytes 393224 | tf_op jit(solution)/shard_map/ppermute | solution.py:296
  22.6 6.0 %collective-permute-start.4 = (f32[4,64,128]{2,1,0:T(8,128)S(1)}, f32[4,64,128]{2,1,0:T(8,128)S(1)}, u32[]{:S(2)}, u32[]{:S(2)}) collective-permute-start(f32[4,64,128]{2,1,0:T(8,128)S(1)} %merge_far_0.1.part_ref.refs_0_), channel_id=1, source_target_pairs={{0,6},{1,7},{2,4},{3,5},{4,2},{5,3},{6,0},{7,1},{8,14},{9,15},{10,... | collective-permute-start | bytes 393224 | tf_op jit(solution)/shard_map/ppermute | solution.py:296
  23.6 6.3 %collective-permute-start.5 = (f32[4,64,128]{2,1,0:T(8,128)S(1)}, f32[4,64,128]{2,1,0:T(8,128)S(1)}, u32[]{:S(2)}, u32[]{:S(2)}) collective-permute-start(f32[4,64,128]{2,1,0:T(8,128)S(1)} %merge_far_0.1.part_ref.refs_0_), channel_id=1, source_target_pairs={{0,2},{1,5},{2,0},{3,7},{4,6},{5,1},{6,4},{7,3},{8,10},{9,13},{10,... | collective-permute-start | bytes 393224 | tf_op jit(solution)/shard_map/ppermute | solution.py:296
  24.8 5.5 %collective-permute-start.6 = (f32[4,64,128]{2,1,0:T(8,128)S(1)}, f32[4,64,128]{2,1,0:T(8,128)S(1)}, u32[]{:S(2)}, u32[]{:S(2)}) collective-permute-start(f32[4,64,128]{2,1,0:T(8,128)S(1)} %merge_far_0.1.part_ref.refs_0_), channel_id=1, source_target_pairs={{0,4},{1,3},{2,6},{3,1},{4,0},{5,7},{6,2},{7,5},{8,12},{9,11},{10,... | collective-permute-start | bytes 393224 | tf_op jit(solution)/shard_map/ppermute | solution.py:296
  30.8 1.2 %collective-permute-start.7 = (f32[3,32]{1,0:T(4,128)S(1)}, f32[3,32]{1,0:T(4,128)S(1)}, u32[]{:S(2)}, u32[]{:S(2)}) collective-permute-start(f32[3,32]{1,0:T(4,128)S(1)} %last_sums.1.refs_4_), channel_id=1, source_target_pairs={{0,1},{1,0},{2,3},{3,2},{4,5},{5,4},{6,7},{7,6},{8,9},{9,8},{10,11... | collective-permute-start | bytes 1160 | tf_op jit(solution)/shard_map/ppermute | solution.py:386

commit v5 on v4

v5 whole, which is shorter than its diff:
```python
import functools
import math

import jax
import jax.numpy as jnp
from jax import lax
from jax.experimental import pallas as pl
from jax.experimental.pallas import tpu as pltpu
from jax.sharding import PartitionSpec as P

LANES = 128
ROWS = 8
TILE = LANES * ROWS
LOADS = (2, 2)


def plan(level, shift):
    if level == 0:
        return [0] * ROWS, 1
    half = ROWS >> level
    first, count = plan(level - 1, shift)
    second, _ = plan(level - 1, shift - half)
    owner = []
    for row in range(ROWS):
        keep = ((row - shift) // half) % 2 == 1
        owner.append(first[row] if keep else second[row] + count)
    return owner, 2 * count


PLACE, _ = plan(3, 0)


def fold(leaf, combine, rows, level=3, shift=0, first=0):
    if level == 0:
        return leaf(PLACE.index(first))
    half = ROWS >> level
    count = 1 << (level - 1)
    a = fold(leaf, combine, rows, level - 1, shift, first)
    b = fold(leaf, combine, rows, level - 1, shift - half, first + count)
    keep = (((rows - shift + 2 * ROWS) // half) % 2) == 1
    out = []
    for one, two, how in zip(a, b, combine, strict=True):
        mine = jnp.where(keep, one, two)
        other = jnp.where(keep, two, one)
        out.append(how(mine, pltpu.roll(other, half, 0)))
    return tuple(out)


def column(row, states):
    spread = jnp.broadcast_to(row, (states, states))
    eye = lax.broadcasted_iota(jnp.int32, (states, states), 0) == lax.broadcasted_iota(jnp.int32, (states, states), 1)
    picked = jnp.sum(jnp.where(eye, spread, 0.0), axis=1, keepdims=True)
    return jnp.broadcast_to(picked, (states, LANES))


def bases(counts_ref, free_ref, states):
    return column(jnp.log(counts_ref[...].astype(jnp.float32)) + free_ref[...], states)


def spot(flip):
    return jnp.bitwise_xor(jnp.bitwise_and(lax.axis_index("state"), 3), flip)


def over_tiles(x, how):
    parts = [x[i * ROWS : (i + 1) * ROWS] for i in range(x.shape[0] // ROWS)]
    return functools.reduce(how, parts)


def spread(x, g, states):
    return jnp.broadcast_to(x[g : g + 1, :], (states, LANES))


def sums_of(out_ref, energies_ref, offset, labels_ref, label_row, base, dirs, steps):
    states = energies_ref.shape[0]
    rows = lax.broadcasted_iota(jnp.int32, (ROWS, LANES), 0)
    ids = lax.broadcasted_iota(jnp.int32, (states, LANES), 0)
    first_state = lax.axis_index("state") * states

    def step(j, carry):
        at = pl.multiple_of(j * ROWS, ROWS)
        labels = labels_ref[pl.ds(pl.multiple_of(label_row + j * ROWS, ROWS), ROWS), :] - first_state

        def shifted(g):
            cols = pl.ds(pl.multiple_of(offset + j * TILE + g * LANES, LANES), LANES)
            return base[...] - energies_ref[:, cols]

        (peak,) = fold(lambda g: (over_tiles(shifted(g), jnp.maximum),), (jnp.maximum,), rows)

        def leaf(g):
            s = shifted(g)
            e = jnp.exp(s - spread(peak, g, states))
            return (
                over_tiles(e, jnp.add),
                over_tiles(e * dirs[0], jnp.add),
                over_tiles(e * dirs[1], jnp.add),
                over_tiles(jnp.where(ids == spread(labels, g, states), s, 0.0), jnp.add),
            )

        total, mix0, mix1, anchor = fold(leaf, (jnp.add,) * 4, rows)
        inverse = 1.0 / total
        out_ref[0, pl.ds(at, ROWS), :] = peak + jnp.log(total)
        out_ref[1, pl.ds(at, ROWS), :] = mix0 * inverse
        out_ref[2, pl.ds(at, ROWS), :] = mix1 * inverse
        out_ref[3, pl.ds(at, ROWS), :] = anchor
        return carry

    lax.fori_loop(0, steps, step, 0)


def quarter_copies(flips, energies_hbm, quarter_refs, sems, first=0):
    width = quarter_refs[0].shape[1]
    copies = []
    for k, (flip, ref) in enumerate(zip(flips, quarter_refs, strict=True)):
        at = pl.ds(pl.multiple_of(spot(flip) * width, width), width)
        copies.append(pltpu.make_async_copy(energies_hbm.at[:, at], ref, sems.at[first + k]))
    return copies


def first_body(flips, pieces, counts_hbm, free_hbm, dirs_hbm, labels_hbm, energies_hbm, *refs):
    out_ref, base_ref, dirs_ref, labels_ref, near_ref, *rest_refs = refs[:-4]
    counts_s, free_s, dirs_s, sems = refs[-4:]
    states, width = near_ref.shape
    piece = width // pieces
    quarter = spot(flips[0])
    near = []
    for i in range(pieces):
        source = energies_hbm.at[:, pl.ds(pl.multiple_of(quarter * width + i * piece, piece), piece)]
        near.append(pltpu.make_async_copy(source, near_ref.at[:, pl.ds(i * piece, piece)], sems.at[i]))
    small = [
        pltpu.make_async_copy(counts_hbm, counts_s, sems.at[pieces]),
        pltpu.make_async_copy(free_hbm, free_s, sems.at[pieces + 1]),
        pltpu.make_async_copy(dirs_hbm, dirs_s, sems.at[pieces + 2]),
        pltpu.make_async_copy(labels_hbm, labels_ref, sems.at[pieces + 3]),
    ]
    rest = quarter_copies(flips[1:], energies_hbm, rest_refs, sems, pieces + 4) if rest_refs else []
    for copy in near[:1] + small + near[1:] + rest:
        copy.start()
    for copy in small:
        copy.wait()
    base_ref[...] = bases(counts_s, free_s, states)
    dirs_ref[0] = column(dirs_s[0:1, :], states)
    dirs_ref[1] = column(dirs_s[1:2, :], states)
    rows = piece // LANES
    for i, copy in enumerate(near):
        copy.wait()
        part = out_ref.at[:, pl.ds(i * rows, rows), :]
        row = quarter * (width // LANES) + i * rows
        sums_of(part, near_ref, i * piece, labels_ref, row, base_ref, dirs_ref, piece // TILE)
    for copy in rest:
        copy.wait()


def later_body(flip, loads, base_ref, dirs_ref, labels_ref, energies_ref, *refs):
    copies = []
    if loads:
        energies_hbm, out_ref, *load_refs, sems = refs
        copies = quarter_copies(loads, energies_hbm, load_refs, sems)
    else:
        (out_ref,) = refs
    for copy in copies:
        copy.start()
    width = energies_ref.shape[1]
    row = spot(flip) * (width // LANES)
    sums_of(out_ref, energies_ref, 0, labels_ref, row, base_ref, dirs_ref, width // TILE)
    for copy in copies:
        copy.wait()


def tally_body(labels_ref, tally_ref):
    states = tally_ref.shape[0]
    first_state = lax.axis_index("state") * states
    ids = lax.broadcasted_iota(jnp.int32, (states, LANES), 0)

    def step(j, tally):
        labels = labels_ref[pl.ds(pl.multiple_of(j * ROWS, ROWS), ROWS), :] - first_state
        for g in range(ROWS):
            tally += jnp.where(ids == spread(labels, g, states), 1.0, 0.0)
        return tally

    tally_ref[...] = lax.fori_loop(0, labels_ref.shape[0] // ROWS, step, jnp.zeros((states, LANES), jnp.float32))


def weigh(part_ref, energies_ref, base_ref):
    states, size = energies_ref.shape

    def step(j, carry):
        occupancy, mix0, mix1 = carry
        at = pl.ds(pl.multiple_of(j * ROWS, ROWS), ROWS)
        norm, first, second = part_ref[0, at, :], part_ref[1, at, :], part_ref[2, at, :]
        for g in range(ROWS):
            cols = pl.ds(pl.multiple_of(j * TILE + g * LANES, LANES), LANES)
            w = jnp.exp((base_ref[...] - energies_ref[:, cols]) - spread(norm, g, states))
            occupancy += w
            mix0 += w * spread(first, g, states)
            mix1 += w * spread(second, g, states)
        return occupancy, mix0, mix1

    zero = jnp.zeros((states, LANES), jnp.float32)
    return lax.fori_loop(0, size // TILE, step, (zero, zero, zero))


def weigh_body(part_ref, base_ref, energies_ref, *refs):
    *before, sums_ref = refs
    for i, x in enumerate(weigh(part_ref, energies_ref, base_ref)):
        sums_ref[i] = x + before[0][i] if before else x


def last_body(part_ref, base_ref, energies_ref, dirs_ref, tally_ref, before_ref, out_ref):
    sums = [x + before_ref[i] for i, x in enumerate(weigh(part_ref, energies_ref, base_ref))]
    states = energies_ref.shape[0]
    eye = lax.broadcasted_iota(jnp.int32, (states, states), 0) == lax.broadcasted_iota(jnp.int32, (states, states), 1)

    def row(x):
        total = jnp.broadcast_to(jnp.sum(x, axis=1, keepdims=True), (states, states))
        return jnp.sum(jnp.where(eye, total, 0.0), axis=0, keepdims=True)

    out_ref[0:1, :] = row(sums[0] - tally_ref[...])
    for j in range(2):
        out_ref[j + 1 : j + 2, :] = row(dirs_ref[j] * sums[0] - sums[j + 1])


def total_body(flips, scale, *refs):
    *part_refs, mine_ref, other_ref, norm_hbm, anchor_hbm, gradient_hbm, products_hbm = refs[:-3]
    gradient_s, products_s, sems = refs[-3:]
    n = len(part_refs)
    rows = part_refs[0].shape[1]
    copies = []
    for k, part_ref in enumerate(part_refs):
        at = pl.ds(pl.multiple_of(spot(flips[k]) * rows, rows), rows)
        copies.append(pltpu.make_async_copy(part_ref.at[0], norm_hbm.at[at, :], sems.at[2 * k]))
        copies.append(pltpu.make_async_copy(part_ref.at[3], anchor_hbm.at[at, :], sems.at[2 * k + 1]))
    copies.append(pltpu.make_async_copy(gradient_s, gradient_hbm, sems.at[2 * n]))
    copies.append(pltpu.make_async_copy(products_s, products_hbm, sems.at[2 * n + 1]))
    for copy in copies[: 2 * n]:
        copy.start()
    total = scale * (mine_ref[...] + other_ref[...])
    gradient_s[...] = total[0:1]
    products_s[...] = total[1:3]
    for copy in copies[2 * n :]:
        copy.start()
    for copy in copies:
        copy.wait()


def unite(parts, out_ref, last=False):
    norms = [part[0] for part in parts]
    peak = functools.reduce(jnp.maximum, norms)
    scales = [jnp.exp(norm - peak) for norm in norms]
    total = functools.reduce(jnp.add, scales)
    inverse = 1.0 / total
    norm = peak + jnp.log(total)
    anchor = functools.reduce(jnp.add, [part[3] for part in parts])
    out_ref[0] = norm
    for j in (1, 2):
        out_ref[j] = functools.reduce(jnp.add, [s * part[j] for s, part in zip(scales, parts, strict=True)]) * inverse
    out_ref[3] = anchor - norm if last else anchor


def merge_body(last, *refs):
    unite(refs[:-1], refs[-1], last)


VMEM = pl.BlockSpec(memory_space=pltpu.VMEM)
HBM = pl.BlockSpec(memory_space=pltpu.HBM)
LIMIT = 16 * 1024 * 1024


def f32(*shape):
    return jax.ShapeDtypeStruct(shape, jnp.float32)


def kernel(body, in_specs, out_specs, out_shape, name, work, scratch=()):
    return pl.pallas_call(
        body,
        in_specs=in_specs,
        out_specs=out_specs,
        out_shape=out_shape,
        scratch_shapes=list(scratch),
        compiler_params=pltpu.CompilerParams(vmem_limit_bytes=LIMIT),
        cost_estimate=pl.CostEstimate(flops=work // 1024, bytes_accessed=1024, transcendentals=0),
        name=name,
    )


def local(energies, counts, labels, free_energy, directions):
    states, samples = energies.shape
    width, cores = lax.axis_size("state"), lax.axis_size("sample")
    near, side, across, stay = 2, 1, 3, 0
    order, loads = (across, near, side, stay), LOADS
    rows = samples // 4 // LANES
    work = states * rows * LANES
    labels_in = labels.reshape(samples // LANES, LANES)
    part = f32(4, rows, LANES)
    pieces = 8 if rows % (8 * ROWS) == 0 else 1
    quarter = f32(states, samples // 4)
    energies = pltpu.with_memory_space_constraint(energies, pltpu.HBM)

    first, base, dirs, labels, *quarters = kernel(
        functools.partial(first_body, order[: loads[0]], pieces),
        [HBM] * 5,
        [VMEM] * (4 + loads[0]),
        [
            part,
            f32(states, LANES),
            f32(2, states, LANES),
            jax.ShapeDtypeStruct(labels_in.shape, labels_in.dtype),
        ]
        + [quarter] * loads[0],
        "first_sums",
        work,
        [
            pltpu.VMEM((1, states), jnp.int32),
            pltpu.VMEM((1, states), jnp.float32),
            pltpu.VMEM((2, states), jnp.float32),
            pltpu.SemaphoreType.DMA((pieces + 3 + loads[0],)),
        ],
    )(
        *(
            pltpu.with_memory_space_constraint(x, pltpu.HBM)
            for x in (counts.reshape(1, states), free_energy.reshape(1, states), directions, labels_in)
        ),
        energies,
    )

    def sums_for(k, name):
        have = len(quarters)
        more = order[have : have + (loads[k] if k < len(loads) else 0)]
        out, *loaded = kernel(
            functools.partial(later_body, order[k], more),
            [VMEM] * 4 + [HBM] * bool(more),
            [VMEM] * (1 + len(more)),
            [part] + [quarter] * len(more),
            name,
            work,
            [pltpu.SemaphoreType.DMA((len(more),))] if more else [],
        )(base, dirs, labels, quarters[k], *([energies] if more else []))
        quarters.extend(loaded)
        return out

    def send(x, flip):
        return lax.ppermute(x, "state", [(place, place ^ flip) for place in range(width)])

    def weigh_part(k, x, before, name):
        args = [x, base, quarters[k], *before]
        return kernel(weigh_body, [VMEM] * len(args), VMEM, f32(3, states, LANES), name, work)(*args)

    def merge(parts, last, name):
        return kernel(functools.partial(merge_body, last), [VMEM] * len(parts), VMEM, part, name, work)(*parts)

    far = range(2, int(math.log2(width)))
    got_side = send(first, near)
    got_near = send(sums_for(1, "near_sums"), near)
    pair = merge([sums_for(2, "side_sums"), got_side], False, "merge_pair")
    got_pair = send(pair, side)
    union = merge([sums_for(3, "own_sums"), got_near], False, "merge_near")
    union = merge([union, got_pair], not far, "merge_square")
    tally = kernel(tally_body, [VMEM], VMEM, f32(states, LANES), "tally", work)(labels)
    for bit in far:
        union = merge([union, send(union, 1 << bit)], bit == far[-1], "merge_far")
    ends = [(3, union)] + [(k, send(union, order[k])) for k in range(3)]
    sums = []
    for k, x in ends[:-1]:
        sums = [weigh_part(k, x, sums, f"weigh{k}")]
    k, x = ends[-1]
    mine = kernel(last_body, [VMEM] * 6, VMEM, f32(3, states), "last_sums", work)(
        x, base, quarters[k], dirs, tally, *sums
    )
    other = lax.ppermute(mine, "sample", [(c, cores - 1 - c) for c in range(cores)])
    long = f32(samples // LANES, LANES)
    log_norm, anchor_logp, gradient, products = kernel(
        functools.partial(total_body, tuple(order[k] for k, _ in ends), states * width / (samples * cores)),
        [VMEM] * (len(ends) + 2),
        [HBM] * 4,
        [long, long, f32(1, states), f32(2, states)],
        "totals",
        1024,
        [
            pltpu.VMEM((1, states), jnp.float32),
            pltpu.VMEM((2, states), jnp.float32),
            pltpu.SemaphoreType.DMA((2 * len(ends) + 2,)),
        ],
    )(*(x for _, x in ends), mine, other)
    return log_norm.reshape(samples), anchor_logp.reshape(samples), gradient.reshape(states), products


def solution(mesh):
    return jax.shard_map(
        local,
        mesh=mesh,
        in_specs=(
            P(("group", "state"), "sample"),
            P(("group", "state")),
            P(("group", "sample")),
            P(("group", "state")),
            P(None, ("group", "state")),
        ),
        out_specs=(
            P(("group", "sample")),
            P(("group", "sample")),
            P(("group", "state")),
            P(None, ("group", "state")),
        ),
        check_vma=False,
    )
```

time: 33 us -> 32 us (0.970)
  starting transfers between devices: 12 us -> 11.3 us
  waiting for transfers between devices: 12.3 us -> 11.8 us
    ppermute x7, starting transfers between devices: 11.9 us -> 11.2 us  [send(): lax.ppermute(x, 'state', [(place, place ^ flip) for place in range(width)])]
    ppermute x7, waiting for transfers between devices: 11.2 us -> 10.6 us  [send(): lax.ppermute(x, 'state', [(place, place ^ flip) for place in range(width)])]
  transfers between devices with their start and end apart: 8 -> 8, of which waited for: 7 -> 7; matrix products, arithmetic and copies ran while one was open for 0% -> 0% of each run, Pallas kernels for 12% -> 15%
where the time goes in v5:
time: 32 us; the launch traced here: 31.8 us
  waiting for transfers between devices  11.8 us (37%)
  starting transfers between devices  11.3 us (35%)
  Pallas kernels  8.05 us (25%)
  between operations  0.71 us (2%)
    ppermute x7, starting transfers between devices, send(): lax.ppermute(x, 'state', [(place, place ^ flip) for place in range(width)])  11.2 us
    ppermute x7, waiting for transfers between devices, send(): lax.ppermute(x, 'state', [(place, place ^ flip) for place in range(width)])  10.6 us
    pallas_call x3, Pallas kernels, sums_for(): kernel(functools.partial(later_body, order[k], more), [VMEM] * 4 + [HBM]...  3.08 us
    pallas_call x1, Pallas kernels, local(): kernel(functools.partial(first_body, order[:loads[0]], pieces), [HBM] * 5...  1.93 us
    ppermute x1, waiting for transfers between devices, local(): lax.ppermute(mine, 'sample', [(c, cores - 1 - c) for c in range(cores)])  1.14 us
    pallas_call x3, Pallas kernels, weigh_part(): kernel(weigh_body, [VMEM] * len(args), VMEM, f32(3, states, LANES), name,...  1.09 us
    pallas_call x1, Pallas kernels, local(): kernel(functools.partial(total_body, tuple((order[k] for k, _ in ends)),...  0.78 us
  transfers between devices with their start and end apart: 8, of which 7 were waited for; matrix products, arithmetic and copies ran while one was open for 0% of the time, Pallas kernels for 15%

profile of v5, /device:TPU:0, one launch (start us, length us, event | category | flops | bytes accessed | tf_op | source)
XLA Modules:
  0.0 31.8 jit_solution(17552627851452074428)
XLA Ops:
  0.6 1.9 %first_sums.1 = (f32[4,64,128]{2,1,0:T(8,128)S(1)}, f32[32,128]{1,0:T(8,128)S(1)}, f32[2,32,128]{2,1,0:T(8,128)S(1)}, s32[256,128]{1,0:T(8,128)S(1)}, f32[32,8192]{1,0:T(8,128)S(1)}, /*index=5*/f32[32,8192]{1,0:T(8,128)S(1)}) custom-call(s32[1,32]{1,0:T(1,128)} %bitcast.7, f32[1,32]{1,0:T(1,128)} %bitcast.8, f32[2,32]{1,0:T(2,128)} %dirs_hbm.1, ...), custom_call_target="tpu_custom_call" | custom-call | flops 256 | bytes 1024 | tf_op jit(solution)/shard_map/first_sums/pallas_call | solution.py:298
  2.6 3.1 %collective-permute-start.1 = (f32[4,64,128]{2,1,0:T(8,128)S(1)}, f32[4,64,128]{2,1,0:T(8,128)S(1)}, u32[]{:S(2)}, u32[]{:S(2)}) collective-permute-start(f32[4,64,128]{2,1,0:T(8,128)S(1)} %get-tuple-element.24), channel_id=1, source_target_pairs={{0,4},{2,6},{4,0},{6,2},{8,12},{10,14},{12,8},{14,10},{1,5},{3,7},... | collective-permute-start | bytes 393224 | tf_op jit(solution)/shard_map/ppermute | solution.py:341
  5.7 1.6 %near_sums.1 = (f32[4,64,128]{2,1,0:T(8,128)S(1)}, f32[32,8192]{1,0:T(8,128)S(1)}, f32[32,8192]{1,0:T(8,128)S(1)}) custom-call(f32[32,128]{1,0:T(8,128)S(1)} %get-tuple-element.17.base_ref, f32[2,32,128]{2,1,0:T(8,128)S(1)} %get-tuple-element.18.dirs_ref, s32[256,128]{1,0:T(8,128)S(1)} %get-tuple-element.19.labels_ref, ...), custom_call_target="tpu_custom_call" | custom-call | flops 256 | bytes 1024 | tf_op jit(solution)/shard_map/near_sums/pallas_call | solution.py:328
  7.2 0.1 collective-permute-start
  7.3 0.8 %side_sums.1.refs_0_ = f32[4,64,128]{2,1,0:T(8,128)S(1)} custom-call(f32[32,128]{1,0:T(8,128)S(1)} %get-tuple-element.17.base_ref, f32[2,32,128]{2,1,0:T(8,128)S(1)} %get-tuple-element.18.dirs_ref, s32[256,128]{1,0:T(8,128)S(1)} %get-tuple-element.19.labels_ref, f32[32,8192]{1,0:T(8,128)S(1)} %get-tuple-element.23.energies_ref), custom_call_target="tpu_custom_call" | custom-call | flops 256 | bytes 1024 | tf_op jit(solution)/shard_map/side_sums/pallas_call | solution.py:328
  8.1 1.5 %collective-permute-done.1.refs_1_ = f32[4,64,128]{2,1,0:T(8,128)S(1)} collective-permute-done((f32[4,64,128]{2,1,0:T(8,128)S(1)}, f32[4,64,128]{2,1,0:T(8,128)S(1)}, u32[]{:S(2)}, u32[]{:S(2)}) %collective-permute-start.1) | collective-permute-done | bytes 131104 | tf_op jit(solution)/shard_map/ppermute | solution.py:341
  9.6 1.5 %collective-permute-start.2 = (f32[4,64,128]{2,1,0:T(8,128)S(1)}, f32[4,64,128]{2,1,0:T(8,128)S(1)}, u32[]{:S(2)}, u32[]{:S(2)}) collective-permute-start(f32[4,64,128]{2,1,0:T(8,128)S(1)} %merge_pair.1), channel_id=1, source_target_pairs={{0,2},{2,0},{4,6},{6,4},{8,10},{10,8},{12,14},{14,12},{1,3},{3,1},... | collective-permute-start | bytes 393224 | tf_op jit(solution)/shard_map/ppermute | solution.py:341
  11.1 0.8 %own_sums.1.refs_0_ = f32[4,64,128]{2,1,0:T(8,128)S(1)} custom-call(f32[32,128]{1,0:T(8,128)S(1)} %get-tuple-element.17.base_ref, f32[2,32,128]{2,1,0:T(8,128)S(1)} %get-tuple-element.18.dirs_ref, s32[256,128]{1,0:T(8,128)S(1)} %get-tuple-element.19.labels_ref, f32[32,8192]{1,0:T(8,128)S(1)} %get-tuple-element.21.energies_ref), custom_call_target="tpu_custom_call" | custom-call | flops 256 | bytes 1024 | tf_op jit(solution)/shard_map/own_sums/pallas_call | solution.py:328
  11.8 0.4 %collective-permute-done.refs_1_ = f32[4,64,128]{2,1,0:T(8,128)S(1)} collective-permute-done((f32[4,64,128]{2,1,0:T(8,128)S(1)}, f32[4,64,128]{2,1,0:T(8,128)S(1)}, u32[]{:S(2)}, u32[]{:S(2)}) %collective-permute-start) | collective-permute-done | bytes 131104 | tf_op jit(solution)/shard_map/ppermute | solution.py:341
  12.3 2.3 %collective-permute-done.2.refs_1_ = f32[4,64,128]{2,1,0:T(8,128)S(1)} collective-permute-done((f32[4,64,128]{2,1,0:T(8,128)S(1)}, f32[4,64,128]{2,1,0:T(8,128)S(1)}, u32[]{:S(2)}, u32[]{:S(2)}) %collective-permute-start.2) | collective-permute-done | bytes 131104 | tf_op jit(solution)/shard_map/ppermute | solution.py:341
  14.7 2.6 %collective-permute-start.3 = (f32[4,64,128]{2,1,0:T(8,128)S(1)}, f32[4,64,128]{2,1,0:T(8,128)S(1)}, u32[]{:S(2)}, u32[]{:S(2)}) collective-permute-start(f32[4,64,128]{2,1,0:T(8,128)S(1)} %merge_square.1.refs_0_), channel_id=1, source_target_pairs={{0,8},{2,10},{4,12},{6,14},{8,0},{10,2},{12,4},{14,6},{1,9},{3,11}... | collective-permute-start | bytes 393224 | tf_op jit(solution)/shard_map/ppermute | solution.py:341
  17.2 3.4 %collective-permute-done.3.refs_1_ = f32[4,64,128]{2,1,0:T(8,128)S(1)} collective-permute-done((f32[4,64,128]{2,1,0:T(8,128)S(1)}, f32[4,64,128]{2,1,0:T(8,128)S(1)}, u32[]{:S(2)}, u32[]{:S(2)}) %collective-permute-start.3) | collective-permute-done | bytes 131104 | tf_op jit(solution)/shard_map/ppermute | solution.py:341
  20.6 3.4 %collective-permute-start.4 = (f32[4,64,128]{2,1,0:T(8,128)S(1)}, f32[4,64,128]{2,1,0:T(8,128)S(1)}, u32[]{:S(2)}, u32[]{:S(2)}) collective-permute-start(f32[4,64,128]{2,1,0:T(8,128)S(1)} %merge_far.1.part_ref.refs_0_), channel_id=1, source_target_pairs={{0,6},{2,4},{4,2},{6,0},{8,14},{10,12},{12,10},{14,8},{1,7},{3,5},... | collective-permute-start | bytes 393224 | tf_op jit(solution)/shard_map/ppermute | solution.py:341
  24.0 0.0 collective-permute-start.5
  24.0 0.6 %collective-permute-start.6 = (f32[4,64,128]{2,1,0:T(8,128)S(1)}, f32[4,64,128]{2,1,0:T(8,128)S(1)}, u32[]{:S(2)}, u32[]{:S(2)}) collective-permute-start(f32[4,64,128]{2,1,0:T(8,128)S(1)} %merge_far.1.part_ref.refs_0_), channel_id=1, source_target_pairs={{0,2},{2,0},{4,6},{6,4},{8,10},{10,8},{12,14},{14,12},{1,3},{3,1},... | collective-permute-start | bytes 393224 | tf_op jit(solution)/shard_map/ppermute | solution.py:341
  24.7 0.6 %tally.1.tally_ref = f32[32,128]{1,0:T(8,128)S(1)} custom-call(s32[256,128]{1,0:T(8,128)S(1)} %get-tuple-element.19.labels_ref), custom_call_target="tpu_custom_call" | custom-call | flops 256 | bytes 1024 | tf_op jit(solution)/shard_map/tally/pallas_call | solution.py:357
  25.2 0.4 %weigh3.1.refs_0_ = f32[3,32,128]{2,1,0:T(8,128)S(1)} custom-call(f32[4,64,128]{2,1,0:T(8,128)S(1)} %merge_far.1.part_ref.refs_0_, f32[32,128]{1,0:T(8,128)S(1)} %get-tuple-element.17.base_ref, f32[32,8192]{1,0:T(8,128)S(1)} %get-tuple-element.21.energies_ref), custom_call_target="tpu_custom_call" | custom-call | flops 256 | bytes 1024 | tf_op jit(solution)/shard_map/weigh3/pallas_call | solution.py:345
  25.6 1.4 %collective-permute-done.4.part_ref.refs_1_ = f32[4,64,128]{2,1,0:T(8,128)S(1)} collective-permute-done((f32[4,64,128]{2,1,0:T(8,128)S(1)}, f32[4,64,128]{2,1,0:T(8,128)S(1)}, u32[]{:S(2)}, u32[]{:S(2)}) %collective-permute-start.4) | collective-permute-done | bytes 131104 | tf_op jit(solution)/shard_map/ppermute | solution.py:341
  27.0 0.4 %weigh0.1.refs_0_ = f32[3,32,128]{2,1,0:T(8,128)S(1)} custom-call(f32[4,64,128]{2,1,0:T(8,128)S(1)} %collective-permute-done.4.part_ref.refs_1_, f32[32,128]{1,0:T(8,128)S(1)} %get-tuple-element.17.base_ref, f32[32,8192]{1,0:T(8,128)S(1)} %get-tuple-element.25.energies_ref, f32[3,32,128]{2,1,0:T(8,128)S(1)} %weigh3.1.refs_0_), custom_call_target="tpu_custom_call" | custom-call | flops 256 | bytes 1024 | tf_op jit(solution)/shard_map/weigh0/pallas_call | solution.py:345
  27.3 1.7 %collective-permute-done.5.part_ref.refs_2_ = f32[4,64,128]{2,1,0:T(8,128)S(1)} collective-permute-done((f32[4,64,128]{2,1,0:T(8,128)S(1)}, f32[4,64,128]{2,1,0:T(8,128)S(1)}, u32[]{:S(2)}, u32[]{:S(2)}) %collective-permute-start.5) | collective-permute-done | bytes 131104 | tf_op jit(solution)/shard_map/ppermute | solution.py:341
  29.0 0.4 %weigh1.1.before_ref = f32[3,32,128]{2,1,0:T(8,128)S(1)} custom-call(f32[4,64,128]{2,1,0:T(8,128)S(1)} %collective-permute-done.5.part_ref.refs_2_, f32[32,128]{1,0:T(8,128)S(1)} %get-tuple-element.17.base_ref, f32[32,8192]{1,0:T(8,128)S(1)} %get-tuple-element.20.energies_ref, f32[3,32,128]{2,1,0:T(8,128)S(1)} %weigh0.1.refs_0_), custom_call_target="tpu_custom_call" | custom-call | flops 256 | bytes 1024 | tf_op jit(solution)/shard_map/weigh1/pallas_call | solution.py:345
  29.4 0.0 collective-permute-done.6.part_ref.refs_3_
  29.4 0.5 %last_sums.1.refs_4_ = f32[3,32]{1,0:T(4,128)S(1)} custom-call(f32[4,64,128]{2,1,0:T(8,128)S(1)} %collective-permute-done.6.part_ref.refs_3_, f32[32,128]{1,0:T(8,128)S(1)} %get-tuple-element.17.base_ref, f32[32,8192]{1,0:T(8,128)S(1)} %get-tuple-element.23.energies_ref, f32[2,32,128]{2,1,0:T(8,128)S(1)} %get-tuple-element.18.dirs_ref, ...), custom_call_target="tpu_custom_call" | custom-call | flops 256 | bytes 1024 | tf_op jit(solution)/shard_map/last_sums/pallas_call | solution.py:365
  29.8 0.1 collective-permute-start.7
  29.9 1.1 %collective-permute-done.7.refs_5_ = f32[3,32]{1,0:T(4,128)S(1)} collective-permute-done((f32[3,32]{1,0:T(4,128)S(1)}, f32[3,32]{1,0:T(4,128)S(1)}, u32[]{:S(2)}, u32[]{:S(2)}) %collective-permute-start.7) | collective-permute-done | bytes 416 | tf_op jit(solution)/shard_map/ppermute | solution.py:368
  31.1 0.8 %totals.1 = (f32[256,128]{1,0:T(8,128)}, f32[256,128]{1,0:T(8,128)}, f32[1,32]{1,0:T(1,128)}, f32[2,32]{1,0:T(2,128)}) custom-call(f32[4,64,128]{2,1,0:T(8,128)S(1)} %merge_far.1.part_ref.refs_0_, f32[4,64,128]{2,1,0:T(8,128)S(1)} %collective-permute-done.4.part_ref.refs_1_, f32[4,64,128]{2,1,0:T(8,128)S(1)} %collective-permute-done.5.part_ref.refs_2_, ...), custom_call_target="tpu_custom_call" | custom-call | flops 1 | bytes 1024 | tf_op jit(solution)/shard_map/totals/pallas_call | solution.py:370
  (4 shorter events, 0.1 us)
Async XLA Ops:
  2.6 7.0 %collective-permute-start.1 = (f32[4,64,128]{2,1,0:T(8,128)S(1)}, f32[4,64,128]{2,1,0:T(8,128)S(1)}, u32[]{:S(2)}, u32[]{:S(2)}) collective-permute-start(f32[4,64,128]{2,1,0:T(8,128)S(1)} %get-tuple-element.24), channel_id=1, source_target_pairs={{0,4},{2,6},{4,0},{6,2},{8,12},{10,14},{12,8},{14,10},{1,5},{3,7},... | collective-permute-start | bytes 393224 | tf_op jit(solution)/shard_map/ppermute | solution.py:341
  7.2 5.0 %collective-permute-start = (f32[4,64,128]{2,1,0:T(8,128)S(1)}, f32[4,64,128]{2,1,0:T(8,128)S(1)}, u32[]{:S(2)}, u32[]{:S(2)}) collective-permute-start(f32[4,64,128]{2,1,0:T(8,128)S(1)} %get-tuple-element.22), channel_id=1, source_target_pairs={{0,4},{2,6},{4,0},{6,2},{8,12},{10,14},{12,8},{14,10},{1,5},{3,7},... | collective-permute-start | bytes 393224 | tf_op jit(solution)/shard_map/ppermute | solution.py:341
  9.6 5.0 %collective-permute-start.2 = (f32[4,64,128]{2,1,0:T(8,128)S(1)}, f32[4,64,128]{2,1,0:T(8,128)S(1)}, u32[]{:S(2)}, u32[]{:S(2)}) collective-permute-start(f32[4,64,128]{2,1,0:T(8,128)S(1)} %merge_pair.1), channel_id=1, source_target_pairs={{0,2},{2,0},{4,6},{6,4},{8,10},{10,8},{12,14},{14,12},{1,3},{3,1},... | collective-permute-start | bytes 393224 | tf_op jit(solution)/shard_map/ppermute | solution.py:341
  14.7 5.9 %collective-permute-start.3 = (f32[4,64,128]{2,1,0:T(8,128)S(1)}, f32[4,64,128]{2,1,0:T(8,128)S(1)}, u32[]{:S(2)}, u32[]{:S(2)}) collective-permute-start(f32[4,64,128]{2,1,0:T(8,128)S(1)} %merge_square.1.refs_0_), channel_id=1, source_target_pairs={{0,8},{2,10},{4,12},{6,14},{8,0},{10,2},{12,4},{14,6},{1,9},{3,11}... | collective-permute-start | bytes 393224 | tf_op jit(solution)/shard_map/ppermute | solution.py:341
  20.6 6.3 %collective-permute-start.4 = (f32[4,64,128]{2,1,0:T(8,128)S(1)}, f32[4,64,128]{2,1,0:T(8,128)S(1)}, u32[]{:S(2)}, u32[]{:S(2)}) collective-permute-start(f32[4,64,128]{2,1,0:T(8,128)S(1)} %merge_far.1.part_ref.refs_0_), channel_id=1, source_target_pairs={{0,6},{2,4},{4,2},{6,0},{8,14},{10,12},{12,10},{14,8},{1,7},{3,5},... | collective-permute-start | bytes 393224 | tf_op jit(solution)/shard_map/ppermute | solution.py:341
  24.0 5.0 %collective-permute-start.5 = (f32[4,64,128]{2,1,0:T(8,128)S(1)}, f32[4,64,128]{2,1,0:T(8,128)S(1)}, u32[]{:S(2)}, u32[]{:S(2)}) collective-permute-start(f32[4,64,128]{2,1,0:T(8,128)S(1)} %merge_far.1.part_ref.refs_0_), channel_id=1, source_target_pairs={{0,4},{2,6},{4,0},{6,2},{8,12},{10,14},{12,8},{14,10},{1,5},{3,7},... | collective-permute-start | bytes 393224 | tf_op jit(solution)/shard_map/ppermute | solution.py:341
  24.0 5.3 %collective-permute-start.6 = (f32[4,64,128]{2,1,0:T(8,128)S(1)}, f32[4,64,128]{2,1,0:T(8,128)S(1)}, u32[]{:S(2)}, u32[]{:S(2)}) collective-permute-start(f32[4,64,128]{2,1,0:T(8,128)S(1)} %merge_far.1.part_ref.refs_0_), channel_id=1, source_target_pairs={{0,2},{2,0},{4,6},{6,4},{8,10},{10,8},{12,14},{14,12},{1,3},{3,1},... | collective-permute-start | bytes 393224 | tf_op jit(solution)/shard_map/ppermute | solution.py:341
  29.8 1.2 %collective-permute-start.7 = (f32[3,32]{1,0:T(4,128)S(1)}, f32[3,32]{1,0:T(4,128)S(1)}, u32[]{:S(2)}, u32[]{:S(2)}) collective-permute-start(f32[3,32]{1,0:T(4,128)S(1)} %last_sums.1.refs_4_), channel_id=1, source_target_pairs={{0,1},{1,0},{2,3},{3,2},{4,5},{5,4},{6,7},{7,6},{8,9},{9,8},{10,11... | collective-permute-start | bytes 1160 | tf_op jit(solution)/shard_map/ppermute | solution.py:368

commit v6 on v5

--- a/solution.py
+++ b/solution.py
@@ -11,7 +11,7 @@
 LANES = 128
 ROWS = 8
 TILE = LANES * ROWS
-LOADS = (2, 2)
+LOADS = (1, 3)
 
 
 def plan(level, shift):
@@ -107,62 +107,75 @@
     lax.fori_loop(0, steps, step, 0)
 
 
-def quarter_copies(flips, energies_hbm, quarter_refs, sems, first=0):
-    width = quarter_refs[0].shape[1]
+def quarter_copy(flip, energies_hbm, quarter_ref, pieces):
+    width = quarter_ref.shape[1]
+    size = width // len(pieces)
     copies = []
-    for k, (flip, ref) in enumerate(zip(flips, quarter_refs, strict=True)):
-        at = pl.ds(pl.multiple_of(spot(flip) * width, width), width)
-        copies.append(pltpu.make_async_copy(energies_hbm.at[:, at], ref, sems.at[first + k]))
+    for i, sem in enumerate(pieces):
+        source = energies_hbm.at[:, pl.ds(pl.multiple_of(spot(flip) * width + i * size, size), size)]
+        copies.append(pltpu.make_async_copy(source, quarter_ref.at[:, pl.ds(i * size, size)], sem))
     return copies
 
 
+def piecewise(flip, copies, out_ref, quarter_ref, labels_ref, base_ref, dirs_ref):
+    width = quarter_ref.shape[1]
+    n = max(len(copies), 1)
+    size, rows = width // n, width // LANES // n
+    for i in range(n):
+        if copies:
+            copies[i].wait()
+        part = out_ref.at[:, pl.ds(i * rows, rows), :]
+        row = spot(flip) * (width // LANES) + i * rows
+        sums_of(part, quarter_ref, i * size, labels_ref, row, base_ref, dirs_ref, size // TILE)
+
+
 def first_body(flips, pieces, counts_hbm, free_hbm, dirs_hbm, labels_hbm, energies_hbm, *refs):
-    out_ref, base_ref, dirs_ref, labels_ref, near_ref, *rest_refs = refs[:-4]
+    out_ref, base_ref, dirs_ref, labels_ref, *quarter_refs = refs[:-4]
     counts_s, free_s, dirs_s, sems = refs[-4:]
-    states, width = near_ref.shape
-    piece = width // pieces
-    quarter = spot(flips[0])
-    near = []
-    for i in range(pieces):
-        source = energies_hbm.at[:, pl.ds(pl.multiple_of(quarter * width + i * piece, piece), piece)]
-        near.append(pltpu.make_async_copy(source, near_ref.at[:, pl.ds(i * piece, piece)], sems.at[i]))
+    states = base_ref.shape[0]
+    own = quarter_copy(flips[0], energies_hbm, quarter_refs[0], [sems.at[i] for i in range(pieces)])
     small = [
         pltpu.make_async_copy(counts_hbm, counts_s, sems.at[pieces]),
         pltpu.make_async_copy(free_hbm, free_s, sems.at[pieces + 1]),
         pltpu.make_async_copy(dirs_hbm, dirs_s, sems.at[pieces + 2]),
-        pltpu.make_async_copy(labels_hbm, labels_ref, sems.at[pieces + 3]),
     ]
-    rest = quarter_copies(flips[1:], energies_hbm, rest_refs, sems, pieces + 4) if rest_refs else []
-    for copy in near[:1] + small + near[1:] + rest:
+    rows = labels_ref.shape[0] // 4
+    marks = []
+    for i in range(4):
+        at = pl.ds(pl.multiple_of(jnp.bitwise_xor(spot(flips[0]), i) * rows, rows), rows)
+        marks.append(pltpu.make_async_copy(labels_hbm.at[at, :], labels_ref.at[at, :], sems.at[pieces + 3 + i]))
+    rest = []
+    for k in range(1, len(flips)):
+        rest += quarter_copy(flips[k], energies_hbm, quarter_refs[k], [sems.at[pieces + 6 + k]])
+    for copy in small + own[:1] + marks[:1] + own[1:] + marks[1:] + rest:
         copy.start()
     for copy in small:
         copy.wait()
     base_ref[...] = bases(counts_s, free_s, states)
     dirs_ref[0] = column(dirs_s[0:1, :], states)
     dirs_ref[1] = column(dirs_s[1:2, :], states)
-    rows = piece // LANES
-    for i, copy in enumerate(near):
+    marks[0].wait()
+    piecewise(flips[0], own, out_ref, quarter_refs[0], labels_ref, base_ref, dirs_ref)
+    for copy in marks[1:] + rest:
         copy.wait()
-        part = out_ref.at[:, pl.ds(i * rows, rows), :]
-        row = quarter * (width // LANES) + i * rows
-        sums_of(part, near_ref, i * piece, labels_ref, row, base_ref, dirs_ref, piece // TILE)
+
+
+def later_body(flip, loads, pieces, base_ref, dirs_ref, labels_ref, *refs):
+    own, rest = [], []
+    if loads:
+        energies_hbm, out_ref, *load_refs, sems = refs[-3 - len(loads) :]
+        for k, (load, ref) in enumerate(zip(loads, load_refs, strict=True)):
+            if load == flip:
+                own = quarter_copy(load, energies_hbm, ref, [sems.at[len(loads) + i] for i in range(pieces)])
+            else:
+                rest += quarter_copy(load, energies_hbm, ref, [sems.at[k]])
+        quarter_ref = load_refs[0] if own else refs[0]
+    else:
+        quarter_ref, out_ref = refs
+    for copy in own + rest:
+        copy.start()
+    piecewise(flip, own, out_ref, quarter_ref, labels_ref, base_ref, dirs_ref)
     for copy in rest:
-        copy.wait()
-
-
-def later_body(flip, loads, base_ref, dirs_ref, labels_ref, energies_ref, *refs):
-    copies = []
-    if loads:
-        energies_hbm, out_ref, *load_refs, sems = refs
-        copies = quarter_copies(loads, energies_hbm, load_refs, sems)
-    else:
-        (out_ref,) = refs
-    for copy in copies:
-        copy.start()
-    width = energies_ref.shape[1]
-    row = spot(flip) * (width // LANES)
-    sums_of(out_ref, energies_ref, 0, labels_ref, row, base_ref, dirs_ref, width // TILE)
-    for copy in copies:
         copy.wait()
 
 
@@ -312,7 +325,7 @@
             pltpu.VMEM((1, states), jnp.int32),
             pltpu.VMEM((1, states), jnp.float32),
             pltpu.VMEM((2, states), jnp.float32),
-            pltpu.SemaphoreType.DMA((pieces + 3 + loads[0],)),
+            pltpu.SemaphoreType.DMA((pieces + 6 + loads[0],)),
         ],
     )(
         *(
@@ -325,15 +338,16 @@
     def sums_for(k, name):
         have = len(quarters)
         more = order[have : have + (loads[k] if k < len(loads) else 0)]
+        args = [base, dirs, labels] + ([quarters[k]] if k < have else []) + ([energies] if more else [])
         out, *loaded = kernel(
-            functools.partial(later_body, order[k], more),
-            [VMEM] * 4 + [HBM] * bool(more),
+            functools.partial(later_body, order[k], more, pieces),
+            [VMEM] * (len(args) - bool(more)) + [HBM] * bool(more),
             [VMEM] * (1 + len(more)),
             [part] + [quarter] * len(more),
             name,
             work,
-            [pltpu.SemaphoreType.DMA((len(more),))] if more else [],
-        )(base, dirs, labels, quarters[k], *([energies] if more else []))
+            [pltpu.SemaphoreType.DMA((len(more) + pieces,))] if more else [],
+        )(*args)
         quarters.extend(loaded)
         return out
 

time: 32 us -> 31.3 us (0.978)
  waiting for transfers between devices: 11.8 us -> 10.6 us
  Pallas kernels: 8.05 us -> 8.41 us
    ppermute x7, waiting for transfers between devices: 10.6 us -> 9.44 us  [send(): lax.ppermute(x, 'state', [(place, place ^ flip) for place in range(width)])]
    pallas_call x3, Pallas kernels: 3.08 us -> 3.59 us  [sums_for(): kernel(functools.partial(later_body, order[k], more, pieces), [VMEM] * (l...]
  transfers between devices with their start and end apart: 8 -> 8, of which waited for: 7 -> 7; matrix products, arithmetic and copies ran while one was open for 0% -> 0% of each run, Pallas kernels for 15% -> 17%
where the time goes in v6:
time: 31.3 us; the launch traced here: 31.1 us
  starting transfers between devices  11.4 us (36%)
  waiting for transfers between devices  10.6 us (34%)
  Pallas kernels  8.41 us (27%)
  between operations  0.71 us (2%)
    ppermute x7, starting transfers between devices, send(): lax.ppermute(x, 'state', [(place, place ^ flip) for place in range(width)])  11.4 us
    ppermute x7, waiting for transfers between devices, send(): lax.ppermute(x, 'state', [(place, place ^ flip) for place in range(width)])  9.44 us
    pallas_call x3, Pallas kernels, sums_for(): kernel(functools.partial(later_body, order[k], more, pieces), [VMEM] * (l...  3.59 us
    pallas_call x1, Pallas kernels, local(): kernel(functools.partial(first_body, order[:loads[0]], pieces), [HBM] * 5...  1.78 us
    ppermute x1, waiting for transfers between devices, local(): lax.ppermute(mine, 'sample', [(c, cores - 1 - c) for c in range(cores)])  1.14 us
    pallas_call x3, Pallas kernels, weigh_part(): kernel(weigh_body, [VMEM] * len(args), VMEM, f32(3, states, LANES), name,...  1.09 us
    pallas_call x1, Pallas kernels, local(): kernel(functools.partial(total_body, tuple((order[k] for k, _ in ends)),...  0.78 us
  transfers between devices with their start and end apart: 8, of which 7 were waited for; matrix products, arithmetic and copies ran while one was open for 0% of the time, Pallas kernels for 17%

profile of v6, /device:TPU:0, one launch (start us, length us, event | category | flops | bytes accessed | tf_op | source)
XLA Modules:
  0.0 31.1 jit_solution(7227433812813217415)
XLA Ops:
  0.6 1.8 %first_sums.1 = (f32[4,64,128]{2,1,0:T(8,128)S(1)}, f32[32,128]{1,0:T(8,128)S(1)}, f32[2,32,128]{2,1,0:T(8,128)S(1)}, s32[256,128]{1,0:T(8,128)S(1)}, f32[32,8192]{1,0:T(8,128)S(1)}) custom-call(s32[1,32]{1,0:T(1,128)} %bitcast.7, f32[1,32]{1,0:T(1,128)} %bitcast.8, f32[2,32]{1,0:T(2,128)} %dirs_hbm.1, s32[256,128]{1,0:T(8,128)} %bitcast.6, f32[32,32768]{1,0:T(8,128)} %refs_0_.1), custom_call_target="tpu_custom_call" | custom-call | flops 256 | bytes 1024 | tf_op jit(solution)/shard_map/first_sums/pallas_call | solution.py:311
  2.4 3.1 %collective-permute-start.1 = (f32[4,64,128]{2,1,0:T(8,128)S(1)}, f32[4,64,128]{2,1,0:T(8,128)S(1)}, u32[]{:S(2)}, u32[]{:S(2)}) collective-permute-start(f32[4,64,128]{2,1,0:T(8,128)S(1)} %get-tuple-element.23), channel_id=1, source_target_pairs={{0,4},{2,6},{4,0},{6,2},{8,12},{10,14},{12,8},{14,10},{1,5},{3,7},... | collective-permute-start | bytes 393224 | tf_op jit(solution)/shard_map/ppermute | solution.py:355
  5.5 2.1 %near_sums.1 = (f32[4,64,128]{2,1,0:T(8,128)S(1)}, f32[32,8192]{1,0:T(8,128)S(1)}, f32[32,8192]{1,0:T(8,128)S(1)}, f32[32,8192]{1,0:T(8,128)S(1)}) custom-call(f32[32,128]{1,0:T(8,128)S(1)} %get-tuple-element.17.base_ref, f32[2,32,128]{2,1,0:T(8,128)S(1)} %get-tuple-element.18.dirs_ref, s32[256,128]{1,0:T(8,128)S(1)} %get-tuple-element.19.labels_ref, ...), custom_call_target="tpu_custom_call" | custom-call | flops 256 | bytes 1024 | tf_op jit(solution)/shard_map/near_sums/pallas_call | solution.py:342
  7.6 0.1 collective-permute-start
  7.7 0.8 %side_sums.1.refs_0_ = f32[4,64,128]{2,1,0:T(8,128)S(1)} custom-call(f32[32,128]{1,0:T(8,128)S(1)} %get-tuple-element.17.base_ref, f32[2,32,128]{2,1,0:T(8,128)S(1)} %get-tuple-element.18.dirs_ref, s32[256,128]{1,0:T(8,128)S(1)} %get-tuple-element.19.labels_ref, f32[32,8192]{1,0:T(8,128)S(1)} %get-tuple-element.22.refs_0_.energies_ref), custom_call_target="tpu_custom_call" | custom-call | flops 256 | bytes 1024 | tf_op jit(solution)/shard_map/side_sums/pallas_call | solution.py:342
  8.4 0.6 %collective-permute-done.1.refs_1_ = f32[4,64,128]{2,1,0:T(8,128)S(1)} collective-permute-done((f32[4,64,128]{2,1,0:T(8,128)S(1)}, f32[4,64,128]{2,1,0:T(8,128)S(1)}, u32[]{:S(2)}, u32[]{:S(2)}) %collective-permute-start.1) | collective-permute-done | bytes 131104 | tf_op jit(solution)/shard_map/ppermute | solution.py:355
  9.0 1.7 %collective-permute-start.2 = (f32[4,64,128]{2,1,0:T(8,128)S(1)}, f32[4,64,128]{2,1,0:T(8,128)S(1)}, u32[]{:S(2)}, u32[]{:S(2)}) collective-permute-start(f32[4,64,128]{2,1,0:T(8,128)S(1)} %merge_pair.1), channel_id=1, source_target_pairs={{0,2},{2,0},{4,6},{6,4},{8,10},{10,8},{12,14},{14,12},{1,3},{3,1},... | collective-permute-start | bytes 393224 | tf_op jit(solution)/shard_map/ppermute | solution.py:355
  10.8 0.8 %own_sums.1.refs_0_ = f32[4,64,128]{2,1,0:T(8,128)S(1)} custom-call(f32[32,128]{1,0:T(8,128)S(1)} %get-tuple-element.17.base_ref, f32[2,32,128]{2,1,0:T(8,128)S(1)} %get-tuple-element.18.dirs_ref, s32[256,128]{1,0:T(8,128)S(1)} %get-tuple-element.19.labels_ref, f32[32,8192]{1,0:T(8,128)S(1)} %get-tuple-element.20.refs_0_.energies_ref), custom_call_target="tpu_custom_call" | custom-call | flops 256 | bytes 1024 | tf_op jit(solution)/shard_map/own_sums/pallas_call | solution.py:342
  11.5 1.1 %collective-permute-done.refs_1_ = f32[4,64,128]{2,1,0:T(8,128)S(1)} collective-permute-done((f32[4,64,128]{2,1,0:T(8,128)S(1)}, f32[4,64,128]{2,1,0:T(8,128)S(1)}, u32[]{:S(2)}, u32[]{:S(2)}) %collective-permute-start) | collective-permute-done | bytes 131104 | tf_op jit(solution)/shard_map/ppermute | solution.py:355
  12.7 1.4 %collective-permute-done.2.refs_1_ = f32[4,64,128]{2,1,0:T(8,128)S(1)} collective-permute-done((f32[4,64,128]{2,1,0:T(8,128)S(1)}, f32[4,64,128]{2,1,0:T(8,128)S(1)}, u32[]{:S(2)}, u32[]{:S(2)}) %collective-permute-start.2) | collective-permute-done | bytes 131104 | tf_op jit(solution)/shard_map/ppermute | solution.py:355
  14.1 2.8 %collective-permute-start.3 = (f32[4,64,128]{2,1,0:T(8,128)S(1)}, f32[4,64,128]{2,1,0:T(8,128)S(1)}, u32[]{:S(2)}, u32[]{:S(2)}) collective-permute-start(f32[4,64,128]{2,1,0:T(8,128)S(1)} %merge_square.1.refs_0_), channel_id=1, source_target_pairs={{0,8},{2,10},{4,12},{6,14},{8,0},{10,2},{12,4},{14,6},{1,9},{3,11}... | collective-permute-start | bytes 393224 | tf_op jit(solution)/shard_map/ppermute | solution.py:355
  16.9 3.4 %collective-permute-done.3.refs_1_ = f32[4,64,128]{2,1,0:T(8,128)S(1)} collective-permute-done((f32[4,64,128]{2,1,0:T(8,128)S(1)}, f32[4,64,128]{2,1,0:T(8,128)S(1)}, u32[]{:S(2)}, u32[]{:S(2)}) %collective-permute-start.3) | collective-permute-done | bytes 131104 | tf_op jit(solution)/shard_map/ppermute | solution.py:355
  20.3 3.0 %collective-permute-start.4 = (f32[4,64,128]{2,1,0:T(8,128)S(1)}, f32[4,64,128]{2,1,0:T(8,128)S(1)}, u32[]{:S(2)}, u32[]{:S(2)}) collective-permute-start(f32[4,64,128]{2,1,0:T(8,128)S(1)} %merge_far.1.part_ref.refs_0_), channel_id=1, source_target_pairs={{0,6},{2,4},{4,2},{6,0},{8,14},{10,12},{12,10},{14,8},{1,7},{3,5},... | collective-permute-start | bytes 393224 | tf_op jit(solution)/shard_map/ppermute | solution.py:355
  23.3 0.0 collective-permute-start.5
  23.3 0.7 %collective-permute-start.6 = (f32[4,64,128]{2,1,0:T(8,128)S(1)}, f32[4,64,128]{2,1,0:T(8,128)S(1)}, u32[]{:S(2)}, u32[]{:S(2)}) collective-permute-start(f32[4,64,128]{2,1,0:T(8,128)S(1)} %merge_far.1.part_ref.refs_0_), channel_id=1, source_target_pairs={{0,2},{2,0},{4,6},{6,4},{8,10},{10,8},{12,14},{14,12},{1,3},{3,1},... | collective-permute-start | bytes 393224 | tf_op jit(solution)/shard_map/ppermute | solution.py:355
  24.0 0.6 %tally.1.tally_ref = f32[32,128]{1,0:T(8,128)S(1)} custom-call(s32[256,128]{1,0:T(8,128)S(1)} %get-tuple-element.19.labels_ref), custom_call_target="tpu_custom_call" | custom-call | flops 256 | bytes 1024 | tf_op jit(solution)/shard_map/tally/pallas_call | solution.py:371
  24.6 0.4 %weigh3.1.refs_0_ = f32[3,32,128]{2,1,0:T(8,128)S(1)} custom-call(f32[4,64,128]{2,1,0:T(8,128)S(1)} %merge_far.1.part_ref.refs_0_, f32[32,128]{1,0:T(8,128)S(1)} %get-tuple-element.17.base_ref, f32[32,8192]{1,0:T(8,128)S(1)} %get-tuple-element.20.refs_0_.energies_ref), custom_call_target="tpu_custom_call" | custom-call | flops 256 | bytes 1024 | tf_op jit(solution)/shard_map/weigh3/pallas_call | solution.py:359
  24.9 2.1 %collective-permute-done.4.part_ref.refs_1_ = f32[4,64,128]{2,1,0:T(8,128)S(1)} collective-permute-done((f32[4,64,128]{2,1,0:T(8,128)S(1)}, f32[4,64,128]{2,1,0:T(8,128)S(1)}, u32[]{:S(2)}, u32[]{:S(2)}) %collective-permute-start.4) | collective-permute-done | bytes 131104 | tf_op jit(solution)/shard_map/ppermute | solution.py:355
  27.0 0.4 %weigh0.1.refs_0_ = f32[3,32,128]{2,1,0:T(8,128)S(1)} custom-call(f32[4,64,128]{2,1,0:T(8,128)S(1)} %collective-permute-done.4.part_ref.refs_1_, f32[32,128]{1,0:T(8,128)S(1)} %get-tuple-element.17.base_ref, f32[32,8192]{1,0:T(8,128)S(1)} %get-tuple-element.25.energies_ref, f32[3,32,128]{2,1,0:T(8,128)S(1)} %weigh3.1.refs_0_), custom_call_target="tpu_custom_call" | custom-call | flops 256 | bytes 1024 | tf_op jit(solution)/shard_map/weigh0/pallas_call | solution.py:359
  27.4 0.9 %collective-permute-done.5.part_ref.refs_2_ = f32[4,64,128]{2,1,0:T(8,128)S(1)} collective-permute-done((f32[4,64,128]{2,1,0:T(8,128)S(1)}, f32[4,64,128]{2,1,0:T(8,128)S(1)}, u32[]{:S(2)}, u32[]{:S(2)}) %collective-permute-start.5) | collective-permute-done | bytes 131104 | tf_op jit(solution)/shard_map/ppermute | solution.py:355
  28.3 0.4 %weigh1.1.before_ref = f32[3,32,128]{2,1,0:T(8,128)S(1)} custom-call(f32[4,64,128]{2,1,0:T(8,128)S(1)} %collective-permute-done.5.part_ref.refs_2_, f32[32,128]{1,0:T(8,128)S(1)} %get-tuple-element.17.base_ref, f32[32,8192]{1,0:T(8,128)S(1)} %get-tuple-element.24.energies_ref, f32[3,32,128]{2,1,0:T(8,128)S(1)} %weigh0.1.refs_0_), custom_call_target="tpu_custom_call" | custom-call | flops 256 | bytes 1024 | tf_op jit(solution)/shard_map/weigh1/pallas_call | solution.py:359
  28.6 0.0 collective-permute-done.6.part_ref.refs_3_
  28.7 0.5 %last_sums.1.refs_4_ = f32[3,32]{1,0:T(4,128)S(1)} custom-call(f32[4,64,128]{2,1,0:T(8,128)S(1)} %collective-permute-done.6.part_ref.refs_3_, f32[32,128]{1,0:T(8,128)S(1)} %get-tuple-element.17.base_ref, f32[32,8192]{1,0:T(8,128)S(1)} %get-tuple-element.22.refs_0_.energies_ref, f32[2,32,128]{2,1,0:T(8,128)S(1)} %get-tuple-element.18.dirs_ref, ...), custom_call_target="tpu_custom_call" | custom-call | flops 256 | bytes 1024 | tf_op jit(solution)/shard_map/last_sums/pallas_call | solution.py:379
  29.1 0.1 collective-permute-start.7
  29.2 1.1 %collective-permute-done.7.refs_5_ = f32[3,32]{1,0:T(4,128)S(1)} collective-permute-done((f32[3,32]{1,0:T(4,128)S(1)}, f32[3,32]{1,0:T(4,128)S(1)}, u32[]{:S(2)}, u32[]{:S(2)}) %collective-permute-start.7) | collective-permute-done | bytes 416 | tf_op jit(solution)/shard_map/ppermute | solution.py:382
  30.3 0.8 %totals.1 = (f32[256,128]{1,0:T(8,128)}, f32[256,128]{1,0:T(8,128)}, f32[1,32]{1,0:T(1,128)}, f32[2,32]{1,0:T(2,128)}) custom-call(f32[4,64,128]{2,1,0:T(8,128)S(1)} %merge_far.1.part_ref.refs_0_, f32[4,64,128]{2,1,0:T(8,128)S(1)} %collective-permute-done.4.part_ref.refs_1_, f32[4,64,128]{2,1,0:T(8,128)S(1)} %collective-permute-done.5.part_ref.refs_2_, ...), custom_call_target="tpu_custom_call" | custom-call | flops 1 | bytes 1024 | tf_op jit(solution)/shard_map/totals/pallas_call | solution.py:384
  (4 shorter events, 0.1 us)
Async XLA Ops:
  2.4 6.6 %collective-permute-start.1 = (f32[4,64,128]{2,1,0:T(8,128)S(1)}, f32[4,64,128]{2,1,0:T(8,128)S(1)}, u32[]{:S(2)}, u32[]{:S(2)}) collective-permute-start(f32[4,64,128]{2,1,0:T(8,128)S(1)} %get-tuple-element.23), channel_id=1, source_target_pairs={{0,4},{2,6},{4,0},{6,2},{8,12},{10,14},{12,8},{14,10},{1,5},{3,7},... | collective-permute-start | bytes 393224 | tf_op jit(solution)/shard_map/ppermute | solution.py:355
  7.6 5.0 %collective-permute-start = (f32[4,64,128]{2,1,0:T(8,128)S(1)}, f32[4,64,128]{2,1,0:T(8,128)S(1)}, u32[]{:S(2)}, u32[]{:S(2)}) collective-permute-start(f32[4,64,128]{2,1,0:T(8,128)S(1)} %get-tuple-element.21), channel_id=1, source_target_pairs={{0,4},{2,6},{4,0},{6,2},{8,12},{10,14},{12,8},{14,10},{1,5},{3,7},... | collective-permute-start | bytes 393224 | tf_op jit(solution)/shard_map/ppermute | solution.py:355
  9.0 5.0 %collective-permute-start.2 = (f32[4,64,128]{2,1,0:T(8,128)S(1)}, f32[4,64,128]{2,1,0:T(8,128)S(1)}, u32[]{:S(2)}, u32[]{:S(2)}) collective-permute-start(f32[4,64,128]{2,1,0:T(8,128)S(1)} %merge_pair.1), channel_id=1, source_target_pairs={{0,2},{2,0},{4,6},{6,4},{8,10},{10,8},{12,14},{14,12},{1,3},{3,1},... | collective-permute-start | bytes 393224 | tf_op jit(solution)/shard_map/ppermute | solution.py:355
  14.1 6.2 %collective-permute-start.3 = (f32[4,64,128]{2,1,0:T(8,128)S(1)}, f32[4,64,128]{2,1,0:T(8,128)S(1)}, u32[]{:S(2)}, u32[]{:S(2)}) collective-permute-start(f32[4,64,128]{2,1,0:T(8,128)S(1)} %merge_square.1.refs_0_), channel_id=1, source_target_pairs={{0,8},{2,10},{4,12},{6,14},{8,0},{10,2},{12,4},{14,6},{1,9},{3,11}... | collective-permute-start | bytes 393224 | tf_op jit(solution)/shard_map/ppermute | solution.py:355
  20.3 6.7 %collective-permute-start.4 = (f32[4,64,128]{2,1,0:T(8,128)S(1)}, f32[4,64,128]{2,1,0:T(8,128)S(1)}, u32[]{:S(2)}, u32[]{:S(2)}) collective-permute-start(f32[4,64,128]{2,1,0:T(8,128)S(1)} %merge_far.1.part_ref.refs_0_), channel_id=1, source_target_pairs={{0,6},{2,4},{4,2},{6,0},{8,14},{10,12},{12,10},{14,8},{1,7},{3,5},... | collective-permute-start | bytes 393224 | tf_op jit(solution)/shard_map/ppermute | solution.py:355
  23.3 5.0 %collective-permute-start.5 = (f32[4,64,128]{2,1,0:T(8,128)S(1)}, f32[4,64,128]{2,1,0:T(8,128)S(1)}, u32[]{:S(2)}, u32[]{:S(2)}) collective-permute-start(f32[4,64,128]{2,1,0:T(8,128)S(1)} %merge_far.1.part_ref.refs_0_), channel_id=1, source_target_pairs={{0,4},{2,6},{4,0},{6,2},{8,12},{10,14},{12,8},{14,10},{1,5},{3,7},... | collective-permute-start | bytes 393224 | tf_op jit(solution)/shard_map/ppermute | solution.py:355
  23.3 5.3 %collective-permute-start.6 = (f32[4,64,128]{2,1,0:T(8,128)S(1)}, f32[4,64,128]{2,1,0:T(8,128)S(1)}, u32[]{:S(2)}, u32[]{:S(2)}) collective-permute-start(f32[4,64,128]{2,1,0:T(8,128)S(1)} %merge_far.1.part_ref.refs_0_), channel_id=1, source_target_pairs={{0,2},{2,0},{4,6},{6,4},{8,10},{10,8},{12,14},{14,12},{1,3},{3,1},... | collective-permute-start | bytes 393224 | tf_op jit(solution)/shard_map/ppermute | solution.py:355
  29.1 1.2 %collective-permute-start.7 = (f32[3,32]{1,0:T(4,128)S(1)}, f32[3,32]{1,0:T(4,128)S(1)}, u32[]{:S(2)}, u32[]{:S(2)}) collective-permute-start(f32[3,32]{1,0:T(4,128)S(1)} %last_sums.1.refs_4_), channel_id=1, source_target_pairs={{0,1},{1,0},{2,3},{3,2},{4,5},{5,4},{6,7},{7,6},{8,9},{9,8},{10,11... | collective-permute-start | bytes 1160 | tf_op jit(solution)/shard_map/ppermute | solution.py:382

commit v7 on v6

--- a/solution.py
+++ b/solution.py
@@ -232,24 +232,29 @@
         out_ref[j + 1 : j + 2, :] = row(dirs_ref[j] * sums[0] - sums[j + 1])
 
 
-def total_body(flips, scale, *refs):
-    *part_refs, mine_ref, other_ref, norm_hbm, anchor_hbm, gradient_hbm, products_hbm = refs[:-3]
-    gradient_s, products_s, sems = refs[-3:]
-    n = len(part_refs)
+def place_body(flips, *refs):
+    *part_refs, _, norm_hbm, anchor_hbm, sems = refs
     rows = part_refs[0].shape[1]
     copies = []
     for k, part_ref in enumerate(part_refs):
         at = pl.ds(pl.multiple_of(spot(flips[k]) * rows, rows), rows)
         copies.append(pltpu.make_async_copy(part_ref.at[0], norm_hbm.at[at, :], sems.at[2 * k]))
         copies.append(pltpu.make_async_copy(part_ref.at[3], anchor_hbm.at[at, :], sems.at[2 * k + 1]))
-    copies.append(pltpu.make_async_copy(gradient_s, gradient_hbm, sems.at[2 * n]))
-    copies.append(pltpu.make_async_copy(products_s, products_hbm, sems.at[2 * n + 1]))
-    for copy in copies[: 2 * n]:
+    for copy in copies:
         copy.start()
+    for copy in copies:
+        copy.wait()
+
+
+def total_body(scale, mine_ref, other_ref, gradient_hbm, products_hbm, gradient_s, products_s, sems):
     total = scale * (mine_ref[...] + other_ref[...])
     gradient_s[...] = total[0:1]
     products_s[...] = total[1:3]
-    for copy in copies[2 * n :]:
+    copies = [
+        pltpu.make_async_copy(gradient_s, gradient_hbm, sems.at[0]),
+        pltpu.make_async_copy(products_s, products_hbm, sems.at[1]),
+    ]
+    for copy in copies:
         copy.start()
     for copy in copies:
         copy.wait()
@@ -381,19 +386,24 @@
     )
     other = lax.ppermute(mine, "sample", [(c, cores - 1 - c) for c in range(cores)])
     long = f32(samples // LANES, LANES)
-    log_norm, anchor_logp, gradient, products = kernel(
-        functools.partial(total_body, tuple(order[k] for k, _ in ends), states * width / (samples * cores)),
-        [VMEM] * (len(ends) + 2),
-        [HBM] * 4,
-        [long, long, f32(1, states), f32(2, states)],
+    log_norm, anchor_logp = kernel(
+        functools.partial(place_body, tuple(order[k] for k, _ in ends)),
+        [VMEM] * (len(ends) + 1),
+        [HBM] * 2,
+        [long, long],
+        "place",
+        1024,
+        [pltpu.SemaphoreType.DMA((2 * len(ends),))],
+    )(*(x for _, x in ends), mine)
+    gradient, products = kernel(
+        functools.partial(total_body, states * width / (samples * cores)),
+        [VMEM] * 2,
+        [HBM] * 2,
+        [f32(1, states), f32(2, states)],
         "totals",
         1024,
-        [
-            pltpu.VMEM((1, states), jnp.float32),
-            pltpu.VMEM((2, states), jnp.float32),
-            pltpu.SemaphoreType.DMA((2 * len(ends) + 2,)),
-        ],
-    )(*(x for _, x in ends), mine, other)
+        [pltpu.VMEM((1, states), jnp.float32), pltpu.VMEM((2, states), jnp.float32), pltpu.SemaphoreType.DMA((2,))],
+    )(mine, other)
     return log_norm.reshape(samples), anchor_logp.reshape(samples), gradient.reshape(states), products
 
 

time: 31.3 us -> 31.1 us (level)
  waiting for transfers between devices: 10.6 us -> 9.8 us
  Pallas kernels: 8.41 us -> 8.99 us
    ppermute x1, waiting for transfers between devices: 1.14 us -> 0.36 us  [local(): lax.ppermute(mine, 'sample', [(c, cores - 1 - c) for c in range(cores)])]
    pallas_call x1 -> x2, Pallas kernels: 0.78 us -> 1.36 us  [the longest x1 0.77 us: local(): kernel(functools.partial(place_body, tuple((order[k] for k, _ in ends))),...]
  transfers between devices with their start and end apart: 8 -> 8, of which waited for: 7 -> 7; matrix products, arithmetic and copies ran while one was open for 0% -> 0% of each run, Pallas kernels for 17% -> 20%
where the time goes in v7:
time: 31.1 us; the launch traced here: 30.9 us
  starting transfers between devices  11.4 us (37%)
  waiting for transfers between devices  9.8 us (32%)
  Pallas kernels  8.99 us (29%)
  between operations  0.72 us (2%)
    ppermute x7, starting transfers between devices, send(): lax.ppermute(x, 'state', [(place, place ^ flip) for place in range(width)])  11.4 us
    ppermute x7, waiting for transfers between devices, send(): lax.ppermute(x, 'state', [(place, place ^ flip) for place in range(width)])  9.44 us
    pallas_call x3, Pallas kernels, sums_for(): kernel(functools.partial(later_body, order[k], more, pieces), [VMEM] * (l...  3.59 us
    pallas_call x1, Pallas kernels, local(): kernel(functools.partial(first_body, order[:loads[0]], pieces), [HBM] * 5...  1.78 us
    pallas_call x3, Pallas kernels, weigh_part(): kernel(weigh_body, [VMEM] * len(args), VMEM, f32(3, states, LANES), name,...  1.09 us
    pallas_call x1, Pallas kernels, local(): kernel(functools.partial(place_body, tuple((order[k] for k, _ in ends))),...  0.77 us
  transfers between devices with their start and end apart: 8, of which 7 were waited for; matrix products, arithmetic and copies ran while one was open for 0% of the time, Pallas kernels for 20%

profile of v7, /device:TPU:0, one launch (start us, length us, event | category | flops | bytes accessed | tf_op | source)
XLA Modules:
  0.0 30.9 jit_solution(3278938414105594917)
XLA Ops:
  0.6 1.8 %first_sums.1 = (f32[4,64,128]{2,1,0:T(8,128)S(1)}, f32[32,128]{1,0:T(8,128)S(1)}, f32[2,32,128]{2,1,0:T(8,128)S(1)}, s32[256,128]{1,0:T(8,128)S(1)}, f32[32,8192]{1,0:T(8,128)S(1)}) custom-call(s32[1,32]{1,0:T(1,128)} %bitcast.7, f32[1,32]{1,0:T(1,128)} %bitcast.8, f32[2,32]{1,0:T(2,128)} %dirs_hbm.1, s32[256,128]{1,0:T(8,128)} %bitcast.6, f32[32,32768]{1,0:T(8,128)} %refs_0_.1), custom_call_target="tpu_custom_call" | custom-call | flops 256 | bytes 1024 | tf_op jit(solution)/shard_map/first_sums/pallas_call | solution.py:316
  2.4 3.1 %collective-permute-start.1 = (f32[4,64,128]{2,1,0:T(8,128)S(1)}, f32[4,64,128]{2,1,0:T(8,128)S(1)}, u32[]{:S(2)}, u32[]{:S(2)}) collective-permute-start(f32[4,64,128]{2,1,0:T(8,128)S(1)} %get-tuple-element.23), channel_id=1, source_target_pairs={{0,4},{2,6},{4,0},{6,2},{8,12},{10,14},{12,8},{14,10},{1,5},{3,7},... | collective-permute-start | bytes 393224 | tf_op jit(solution)/shard_map/ppermute | solution.py:360
  5.5 2.1 %near_sums.1 = (f32[4,64,128]{2,1,0:T(8,128)S(1)}, f32[32,8192]{1,0:T(8,128)S(1)}, f32[32,8192]{1,0:T(8,128)S(1)}, f32[32,8192]{1,0:T(8,128)S(1)}) custom-call(f32[32,128]{1,0:T(8,128)S(1)} %get-tuple-element.17.base_ref, f32[2,32,128]{2,1,0:T(8,128)S(1)} %get-tuple-element.18.dirs_ref, s32[256,128]{1,0:T(8,128)S(1)} %get-tuple-element.19.labels_ref, ...), custom_call_target="tpu_custom_call" | custom-call | flops 256 | bytes 1024 | tf_op jit(solution)/shard_map/near_sums/pallas_call | solution.py:347
  7.6 0.1 collective-permute-start
  7.7 0.8 %side_sums.1.refs_0_ = f32[4,64,128]{2,1,0:T(8,128)S(1)} custom-call(f32[32,128]{1,0:T(8,128)S(1)} %get-tuple-element.17.base_ref, f32[2,32,128]{2,1,0:T(8,128)S(1)} %get-tuple-element.18.dirs_ref, s32[256,128]{1,0:T(8,128)S(1)} %get-tuple-element.19.labels_ref, f32[32,8192]{1,0:T(8,128)S(1)} %get-tuple-element.22.refs_0_.energies_ref), custom_call_target="tpu_custom_call" | custom-call | flops 256 | bytes 1024 | tf_op jit(solution)/shard_map/side_sums/pallas_call | solution.py:347
  8.4 0.6 %collective-permute-done.1.refs_1_ = f32[4,64,128]{2,1,0:T(8,128)S(1)} collective-permute-done((f32[4,64,128]{2,1,0:T(8,128)S(1)}, f32[4,64,128]{2,1,0:T(8,128)S(1)}, u32[]{:S(2)}, u32[]{:S(2)}) %collective-permute-start.1) | collective-permute-done | bytes 131104 | tf_op jit(solution)/shard_map/ppermute | solution.py:360
  9.0 1.7 %collective-permute-start.2 = (f32[4,64,128]{2,1,0:T(8,128)S(1)}, f32[4,64,128]{2,1,0:T(8,128)S(1)}, u32[]{:S(2)}, u32[]{:S(2)}) collective-permute-start(f32[4,64,128]{2,1,0:T(8,128)S(1)} %merge_pair.1), channel_id=1, source_target_pairs={{0,2},{2,0},{4,6},{6,4},{8,10},{10,8},{12,14},{14,12},{1,3},{3,1},... | collective-permute-start | bytes 393224 | tf_op jit(solution)/shard_map/ppermute | solution.py:360
  10.8 0.8 %own_sums.1.refs_0_ = f32[4,64,128]{2,1,0:T(8,128)S(1)} custom-call(f32[32,128]{1,0:T(8,128)S(1)} %get-tuple-element.17.base_ref, f32[2,32,128]{2,1,0:T(8,128)S(1)} %get-tuple-element.18.dirs_ref, s32[256,128]{1,0:T(8,128)S(1)} %get-tuple-element.19.labels_ref, f32[32,8192]{1,0:T(8,128)S(1)} %get-tuple-element.20.refs_0_.energies_ref), custom_call_target="tpu_custom_call" | custom-call | flops 256 | bytes 1024 | tf_op jit(solution)/shard_map/own_sums/pallas_call | solution.py:347
  11.5 1.1 %collective-permute-done.refs_1_ = f32[4,64,128]{2,1,0:T(8,128)S(1)} collective-permute-done((f32[4,64,128]{2,1,0:T(8,128)S(1)}, f32[4,64,128]{2,1,0:T(8,128)S(1)}, u32[]{:S(2)}, u32[]{:S(2)}) %collective-permute-start) | collective-permute-done | bytes 131104 | tf_op jit(solution)/shard_map/ppermute | solution.py:360
  12.7 1.4 %collective-permute-done.2.refs_1_ = f32[4,64,128]{2,1,0:T(8,128)S(1)} collective-permute-done((f32[4,64,128]{2,1,0:T(8,128)S(1)}, f32[4,64,128]{2,1,0:T(8,128)S(1)}, u32[]{:S(2)}, u32[]{:S(2)}) %collective-permute-start.2) | collective-permute-done | bytes 131104 | tf_op jit(solution)/shard_map/ppermute | solution.py:360
  14.1 2.8 %collective-permute-start.3 = (f32[4,64,128]{2,1,0:T(8,128)S(1)}, f32[4,64,128]{2,1,0:T(8,128)S(1)}, u32[]{:S(2)}, u32[]{:S(2)}) collective-permute-start(f32[4,64,128]{2,1,0:T(8,128)S(1)} %merge_square.1.refs_0_), channel_id=1, source_target_pairs={{0,8},{2,10},{4,12},{6,14},{8,0},{10,2},{12,4},{14,6},{1,9},{3,11}... | collective-permute-start | bytes 393224 | tf_op jit(solution)/shard_map/ppermute | solution.py:360
  16.9 3.4 %collective-permute-done.3.refs_1_ = f32[4,64,128]{2,1,0:T(8,128)S(1)} collective-permute-done((f32[4,64,128]{2,1,0:T(8,128)S(1)}, f32[4,64,128]{2,1,0:T(8,128)S(1)}, u32[]{:S(2)}, u32[]{:S(2)}) %collective-permute-start.3) | collective-permute-done | bytes 131104 | tf_op jit(solution)/shard_map/ppermute | solution.py:360
  20.3 3.0 %collective-permute-start.4 = (f32[4,64,128]{2,1,0:T(8,128)S(1)}, f32[4,64,128]{2,1,0:T(8,128)S(1)}, u32[]{:S(2)}, u32[]{:S(2)}) collective-permute-start(f32[4,64,128]{2,1,0:T(8,128)S(1)} %merge_far.1.part_ref.refs_0_), channel_id=1, source_target_pairs={{0,6},{2,4},{4,2},{6,0},{8,14},{10,12},{12,10},{14,8},{1,7},{3,5},... | collective-permute-start | bytes 393224 | tf_op jit(solution)/shard_map/ppermute | solution.py:360
  23.3 0.0 collective-permute-start.5
  23.3 0.7 %collective-permute-start.6 = (f32[4,64,128]{2,1,0:T(8,128)S(1)}, f32[4,64,128]{2,1,0:T(8,128)S(1)}, u32[]{:S(2)}, u32[]{:S(2)}) collective-permute-start(f32[4,64,128]{2,1,0:T(8,128)S(1)} %merge_far.1.part_ref.refs_0_), channel_id=1, source_target_pairs={{0,2},{2,0},{4,6},{6,4},{8,10},{10,8},{12,14},{14,12},{1,3},{3,1},... | collective-permute-start | bytes 393224 | tf_op jit(solution)/shard_map/ppermute | solution.py:360
  24.0 0.6 %tally.1.tally_ref = f32[32,128]{1,0:T(8,128)S(1)} custom-call(s32[256,128]{1,0:T(8,128)S(1)} %get-tuple-element.19.labels_ref), custom_call_target="tpu_custom_call" | custom-call | flops 256 | bytes 1024 | tf_op jit(solution)/shard_map/tally/pallas_call | solution.py:376
  24.6 0.4 %weigh3.1.refs_0_ = f32[3,32,128]{2,1,0:T(8,128)S(1)} custom-call(f32[4,64,128]{2,1,0:T(8,128)S(1)} %merge_far.1.part_ref.refs_0_, f32[32,128]{1,0:T(8,128)S(1)} %get-tuple-element.17.base_ref, f32[32,8192]{1,0:T(8,128)S(1)} %get-tuple-element.20.refs_0_.energies_ref), custom_call_target="tpu_custom_call" | custom-call | flops 256 | bytes 1024 | tf_op jit(solution)/shard_map/weigh3/pallas_call | solution.py:364
  24.9 2.1 %collective-permute-done.4.part_ref.refs_1_ = f32[4,64,128]{2,1,0:T(8,128)S(1)} collective-permute-done((f32[4,64,128]{2,1,0:T(8,128)S(1)}, f32[4,64,128]{2,1,0:T(8,128)S(1)}, u32[]{:S(2)}, u32[]{:S(2)}) %collective-permute-start.4) | collective-permute-done | bytes 131104 | tf_op jit(solution)/shard_map/ppermute | solution.py:360
  27.0 0.4 %weigh0.1.refs_0_ = f32[3,32,128]{2,1,0:T(8,128)S(1)} custom-call(f32[4,64,128]{2,1,0:T(8,128)S(1)} %collective-permute-done.4.part_ref.refs_1_, f32[32,128]{1,0:T(8,128)S(1)} %get-tuple-element.17.base_ref, f32[32,8192]{1,0:T(8,128)S(1)} %get-tuple-element.25.energies_ref, f32[3,32,128]{2,1,0:T(8,128)S(1)} %weigh3.1.refs_0_), custom_call_target="tpu_custom_call" | custom-call | flops 256 | bytes 1024 | tf_op jit(solution)/shard_map/weigh0/pallas_call | solution.py:364
  27.4 0.9 %collective-permute-done.5.part_ref.refs_2_ = f32[4,64,128]{2,1,0:T(8,128)S(1)} collective-permute-done((f32[4,64,128]{2,1,0:T(8,128)S(1)}, f32[4,64,128]{2,1,0:T(8,128)S(1)}, u32[]{:S(2)}, u32[]{:S(2)}) %collective-permute-start.5) | collective-permute-done | bytes 131104 | tf_op jit(solution)/shard_map/ppermute | solution.py:360
  28.3 0.4 %weigh1.1.before_ref = f32[3,32,128]{2,1,0:T(8,128)S(1)} custom-call(f32[4,64,128]{2,1,0:T(8,128)S(1)} %collective-permute-done.5.part_ref.refs_2_, f32[32,128]{1,0:T(8,128)S(1)} %get-tuple-element.17.base_ref, f32[32,8192]{1,0:T(8,128)S(1)} %get-tuple-element.24.energies_ref, f32[3,32,128]{2,1,0:T(8,128)S(1)} %weigh0.1.refs_0_), custom_call_target="tpu_custom_call" | custom-call | flops 256 | bytes 1024 | tf_op jit(solution)/shard_map/weigh1/pallas_call | solution.py:364
  28.6 0.0 collective-permute-done.6.part_ref.refs_3_
  28.7 0.5 %last_sums.1.refs_4_.mine_ref = f32[3,32]{1,0:T(4,128)S(1)} custom-call(f32[4,64,128]{2,1,0:T(8,128)S(1)} %collective-permute-done.6.part_ref.refs_3_, f32[32,128]{1,0:T(8,128)S(1)} %get-tuple-element.17.base_ref, f32[32,8192]{1,0:T(8,128)S(1)} %get-tuple-element.22.refs_0_.energies_ref, f32[2,32,128]{2,1,0:T(8,128)S(1)} %get-tuple-element.18.dirs_ref, ...), custom_call_target="tpu_custom_call" | custom-call | flops 256 | bytes 1024 | tf_op jit(solution)/shard_map/last_sums/pallas_call | solution.py:384
  29.1 0.1 collective-permute-start.7
  29.2 0.8 %place.1 = (f32[256,128]{1,0:T(8,128)}, f32[256,128]{1,0:T(8,128)}) custom-call(f32[4,64,128]{2,1,0:T(8,128)S(1)} %merge_far.1.part_ref.refs_0_, f32[4,64,128]{2,1,0:T(8,128)S(1)} %collective-permute-done.4.part_ref.refs_1_, f32[4,64,128]{2,1,0:T(8,128)S(1)} %collective-permute-done.5.part_ref.refs_2_, ...), custom_call_target="tpu_custom_call" | custom-call | flops 1 | bytes 1024 | tf_op jit(solution)/shard_map/place/pallas_call | solution.py:389
  30.0 0.4 %collective-permute-done.7.other_ref = f32[3,32]{1,0:T(4,128)S(1)} collective-permute-done((f32[3,32]{1,0:T(4,128)S(1)}, f32[3,32]{1,0:T(4,128)S(1)}, u32[]{:S(2)}, u32[]{:S(2)}) %collective-permute-start.7) | collective-permute-done | bytes 416 | tf_op jit(solution)/shard_map/ppermute | solution.py:387
  30.3 0.6 %totals.1 = (f32[1,32]{1,0:T(1,128)}, f32[2,32]{1,0:T(2,128)}) custom-call(f32[3,32]{1,0:T(4,128)S(1)} %last_sums.1.refs_4_.mine_ref, f32[3,32]{1,0:T(4,128)S(1)} %collective-permute-done.7.other_ref), custom_call_target="tpu_custom_call" | custom-call | flops 1 | bytes 1024 | tf_op jit(solution)/shard_map/totals/pallas_call | solution.py:398
  (4 shorter events, 0.1 us)
Async XLA Ops:
  2.4 6.6 %collective-permute-start.1 = (f32[4,64,128]{2,1,0:T(8,128)S(1)}, f32[4,64,128]{2,1,0:T(8,128)S(1)}, u32[]{:S(2)}, u32[]{:S(2)}) collective-permute-start(f32[4,64,128]{2,1,0:T(8,128)S(1)} %get-tuple-element.23), channel_id=1, source_target_pairs={{0,4},{2,6},{4,0},{6,2},{8,12},{10,14},{12,8},{14,10},{1,5},{3,7},... | collective-permute-start | bytes 393224 | tf_op jit(solution)/shard_map/ppermute | solution.py:360
  7.6 5.0 %collective-permute-start = (f32[4,64,128]{2,1,0:T(8,128)S(1)}, f32[4,64,128]{2,1,0:T(8,128)S(1)}, u32[]{:S(2)}, u32[]{:S(2)}) collective-permute-start(f32[4,64,128]{2,1,0:T(8,128)S(1)} %get-tuple-element.21), channel_id=1, source_target_pairs={{0,4},{2,6},{4,0},{6,2},{8,12},{10,14},{12,8},{14,10},{1,5},{3,7},... | collective-permute-start | bytes 393224 | tf_op jit(solution)/shard_map/ppermute | solution.py:360
  9.0 5.0 %collective-permute-start.2 = (f32[4,64,128]{2,1,0:T(8,128)S(1)}, f32[4,64,128]{2,1,0:T(8,128)S(1)}, u32[]{:S(2)}, u32[]{:S(2)}) collective-permute-start(f32[4,64,128]{2,1,0:T(8,128)S(1)} %merge_pair.1), channel_id=1, source_target_pairs={{0,2},{2,0},{4,6},{6,4},{8,10},{10,8},{12,14},{14,12},{1,3},{3,1},... | collective-permute-start | bytes 393224 | tf_op jit(solution)/shard_map/ppermute | solution.py:360
  14.1 6.2 %collective-permute-start.3 = (f32[4,64,128]{2,1,0:T(8,128)S(1)}, f32[4,64,128]{2,1,0:T(8,128)S(1)}, u32[]{:S(2)}, u32[]{:S(2)}) collective-permute-start(f32[4,64,128]{2,1,0:T(8,128)S(1)} %merge_square.1.refs_0_), channel_id=1, source_target_pairs={{0,8},{2,10},{4,12},{6,14},{8,0},{10,2},{12,4},{14,6},{1,9},{3,11}... | collective-permute-start | bytes 393224 | tf_op jit(solution)/shard_map/ppermute | solution.py:360
  20.3 6.7 %collective-permute-start.4 = (f32[4,64,128]{2,1,0:T(8,128)S(1)}, f32[4,64,128]{2,1,0:T(8,128)S(1)}, u32[]{:S(2)}, u32[]{:S(2)}) collective-permute-start(f32[4,64,128]{2,1,0:T(8,128)S(1)} %merge_far.1.part_ref.refs_0_), channel_id=1, source_target_pairs={{0,6},{2,4},{4,2},{6,0},{8,14},{10,12},{12,10},{14,8},{1,7},{3,5},... | collective-permute-start | bytes 393224 | tf_op jit(solution)/shard_map/ppermute | solution.py:360
  23.3 5.0 %collective-permute-start.5 = (f32[4,64,128]{2,1,0:T(8,128)S(1)}, f32[4,64,128]{2,1,0:T(8,128)S(1)}, u32[]{:S(2)}, u32[]{:S(2)}) collective-permute-start(f32[4,64,128]{2,1,0:T(8,128)S(1)} %merge_far.1.part_ref.refs_0_), channel_id=1, source_target_pairs={{0,4},{2,6},{4,0},{6,2},{8,12},{10,14},{12,8},{14,10},{1,5},{3,7},... | collective-permute-start | bytes 393224 | tf_op jit(solution)/shard_map/ppermute | solution.py:360
  23.3 5.3 %collective-permute-start.6 = (f32[4,64,128]{2,1,0:T(8,128)S(1)}, f32[4,64,128]{2,1,0:T(8,128)S(1)}, u32[]{:S(2)}, u32[]{:S(2)}) collective-permute-start(f32[4,64,128]{2,1,0:T(8,128)S(1)} %merge_far.1.part_ref.refs_0_), channel_id=1, source_target_pairs={{0,2},{2,0},{4,6},{6,4},{8,10},{10,8},{12,14},{14,12},{1,3},{3,1},... | collective-permute-start | bytes 393224 | tf_op jit(solution)/shard_map/ppermute | solution.py:360
  29.1 1.2 %collective-permute-start.7 = (f32[3,32]{1,0:T(4,128)S(1)}, f32[3,32]{1,0:T(4,128)S(1)}, u32[]{:S(2)}, u32[]{:S(2)}) collective-permute-start(f32[3,32]{1,0:T(4,128)S(1)} %last_sums.1.refs_4_.mine_ref), channel_id=1, source_target_pairs={{0,1},{1,0},{2,3},{3,2},{4,5},{5,4},{6,7},{7,6},{8,9},{9,8},{10,11... | collective-permute-start | bytes 1160 | tf_op jit(solution)/shard_map/ppermute | solution.py:387

commit v8 on v7

--- a/solution.py
+++ b/solution.py
@@ -12,6 +12,8 @@
 ROWS = 8
 TILE = LANES * ROWS
 LOADS = (1, 3)
+NEAR = (2, 2)
+GATHER = ((3, 2), (2, 1), (1, 3))
 
 
 def plan(level, shift):
@@ -57,7 +59,12 @@
     return column(jnp.log(counts_ref[...].astype(jnp.float32)) + free_ref[...], states)
 
 
-def spot(flip):
+def odd_core():
+    return lax.axis_index("sample") % 2 == 1
+
+
+def spot(flips):
+    flip = jnp.where(odd_core(), flips[1], flips[0]) if flips[0] != flips[1] else flips[0]
     return jnp.bitwise_xor(jnp.bitwise_and(lax.axis_index("state"), 3), flip)
 
 
@@ -209,18 +216,32 @@
         return occupancy, mix0, mix1
 
     zero = jnp.zeros((states, LANES), jnp.float32)
-    return lax.fori_loop(0, size // TILE, step, (zero, zero, zero))
-
-
-def weigh_body(part_ref, base_ref, energies_ref, *refs):
-    *before, sums_ref = refs
-    for i, x in enumerate(weigh(part_ref, energies_ref, base_ref)):
-        sums_ref[i] = x + before[0][i] if before else x
-
-
-def last_body(part_ref, base_ref, energies_ref, dirs_ref, tally_ref, before_ref, out_ref):
-    sums = [x + before_ref[i] for i, x in enumerate(weigh(part_ref, energies_ref, base_ref))]
-    states = energies_ref.shape[0]
+    return lax.fori_loop(0, size // TILE, step, (zero, zero, zero), unroll=4)
+
+
+def weigh_either(part_ref, base_ref, even_ref, odd_ref, sums_ref, before_ref=None):
+    def weigh_in(energies_ref):
+        for i, x in enumerate(weigh(part_ref, energies_ref, base_ref)):
+            sums_ref[i] = x + before_ref[i] if before_ref is not None else x
+
+    if even_ref is odd_ref:
+        weigh_in(even_ref)
+    else:
+        pl.when(odd_core())(lambda: weigh_in(odd_ref))
+        pl.when(jnp.logical_not(odd_core()))(lambda: weigh_in(even_ref))
+
+
+def weigh_body(same, *refs):
+    *refs, sums_ref = refs
+    part_ref, base_ref, *refs = refs
+    even_ref, odd_ref, *before = [refs[0], *refs] if same else refs
+    weigh_either(part_ref, base_ref, even_ref, odd_ref, sums_ref, *before)
+
+
+def last_body(part_ref, base_ref, even_ref, odd_ref, dirs_ref, tally_ref, before_ref, out_ref, sums_s):
+    weigh_either(part_ref, base_ref, even_ref, odd_ref, sums_s, before_ref)
+    sums = sums_s[0], sums_s[1], sums_s[2]
+    states = even_ref.shape[0]
     eye = lax.broadcasted_iota(jnp.int32, (states, states), 0) == lax.broadcasted_iota(jnp.int32, (states, states), 1)
 
     def row(x):
@@ -303,7 +324,7 @@
 def local(energies, counts, labels, free_energy, directions):
     states, samples = energies.shape
     width, cores = lax.axis_size("state"), lax.axis_size("sample")
-    near, side, across, stay = 2, 1, 3, 0
+    near, side, across, stay = NEAR, (3 - NEAR[0], 3 - NEAR[1]), (3, 3), (0, 0)
     order, loads = (across, near, side, stay), LOADS
     rows = samples // 4 // LANES
     work = states * rows * LANES
@@ -356,15 +377,22 @@
         quarters.extend(loaded)
         return out
 
-    def send(x, flip):
-        return lax.ppermute(x, "state", [(place, place ^ flip) for place in range(width)])
-
-    def weigh_part(k, x, before, name):
-        args = [x, base, quarters[k], *before]
-        return kernel(weigh_body, [VMEM] * len(args), VMEM, f32(3, states, LANES), name, work)(*args)
-
     def merge(parts, last, name):
         return kernel(functools.partial(merge_body, last), [VMEM] * len(parts), VMEM, part, name, work)(*parts)
+
+    def send(x, flips):
+        pairs = [(p * cores + c, (p ^ flips[c % 2]) * cores + c) for p in range(width) for c in range(cores)]
+        return lax.ppermute(x, ("state", "sample"), pairs)
+
+    def quarters_of(flips):
+        picked = [quarters[[f[c] for f in order].index(flips[c])] for c in range(2)]
+        return picked[:1] if picked[0] is picked[1] else picked
+
+    def weigh_part(flips, x, before, name):
+        energies = quarters_of(flips)
+        args = [x, base, *energies, *before]
+        body = functools.partial(weigh_body, len(energies) == 1)
+        return kernel(body, [VMEM] * len(args), VMEM, f32(3, states, LANES), name, work)(*args)
 
     far = range(2, int(math.log2(width)))
     got_side = send(first, near)
@@ -375,19 +403,26 @@
     union = merge([union, got_pair], not far, "merge_square")
     tally = kernel(tally_body, [VMEM], VMEM, f32(states, LANES), "tally", work)(labels)
     for bit in far:
-        union = merge([union, send(union, 1 << bit)], bit == far[-1], "merge_far")
-    ends = [(3, union)] + [(k, send(union, order[k])) for k in range(3)]
+        union = merge([union, send(union, (1 << bit,) * 2)], bit == far[-1], "merge_far")
+    ends = [(stay, union)] + [(flips, send(union, flips)) for flips in GATHER]
     sums = []
-    for k, x in ends[:-1]:
-        sums = [weigh_part(k, x, sums, f"weigh{k}")]
-    k, x = ends[-1]
-    mine = kernel(last_body, [VMEM] * 6, VMEM, f32(3, states), "last_sums", work)(
-        x, base, quarters[k], dirs, tally, *sums
-    )
+    for k, (flips, x) in enumerate(ends[:-1]):
+        sums = [weigh_part(flips, x, sums, f"weigh{k}")]
+    flips, x = ends[-1]
+    last = quarters_of(flips)
+    mine = kernel(
+        last_body,
+        [VMEM] * 7,
+        VMEM,
+        f32(3, states),
+        "last_sums",
+        work,
+        [pltpu.VMEM((3, states, LANES), jnp.float32)],
+    )(x, base, last[0], last[-1], dirs, tally, *sums)
     other = lax.ppermute(mine, "sample", [(c, cores - 1 - c) for c in range(cores)])
     long = f32(samples // LANES, LANES)
     log_norm, anchor_logp = kernel(
-        functools.partial(place_body, tuple(order[k] for k, _ in ends)),
+        functools.partial(place_body, tuple(flips for flips, _ in ends)),
         [VMEM] * (len(ends) + 1),
         [HBM] * 2,
         [long, long],

time: 31.1 us -> 31.1 us (level)
  transfers between devices with their start and end apart: 8 -> 8, of which waited for: 7 -> 7; matrix products, arithmetic and copies ran while one was open for 0% -> 0% of each run, Pallas kernels for 20% -> 19%
where the time goes in v8:
time: 31.1 us; the launch traced here: 30.9 us
  starting transfers between devices  11.4 us (37%)
  waiting for transfers between devices  9.87 us (32%)
  Pallas kernels  8.88 us (29%)
  between operations  0.72 us (2%)
    ppermute x7, starting transfers between devices, send(): return lax.ppermute(x, ('state', 'sample'), pairs)  11.4 us
    ppermute x7, waiting for transfers between devices, send(): return lax.ppermute(x, ('state', 'sample'), pairs)  9.5 us
    pallas_call x3, Pallas kernels, sums_for(): kernel(functools.partial(later_body, order[k], more, pieces), [VMEM] * (l...  3.59 us
    pallas_call x1, Pallas kernels, local(): kernel(functools.partial(first_body, order[:loads[0]], pieces), [HBM] * 5...  1.78 us
    pallas_call x3, Pallas kernels, weigh_part(): kernel(body, [VMEM] * len(args), VMEM, f32(3, states, LANES), name, work)  0.99 us
    pallas_call x1, Pallas kernels, local(): kernel(functools.partial(place_body, tuple((flips for flips, _ in ends)))...  0.77 us
  transfers between devices with their start and end apart: 8, of which 7 were waited for; matrix products, arithmetic and copies ran while one was open for 0% of the time, Pallas kernels for 19%

profile of v8, /device:TPU:0, one launch (start us, length us, event | category | flops | bytes accessed | tf_op | source)
XLA Modules:
  0.0 30.9 jit_solution(4715796066307852038)
XLA Ops:
  0.6 1.8 %first_sums.1 = (f32[4,64,128]{2,1,0:T(8,128)S(1)}, f32[32,128]{1,0:T(8,128)S(1)}, f32[2,32,128]{2,1,0:T(8,128)S(1)}, s32[256,128]{1,0:T(8,128)S(1)}, f32[32,8192]{1,0:T(8,128)S(1)}) custom-call(s32[1,32]{1,0:T(1,128)} %bitcast.7, f32[1,32]{1,0:T(1,128)} %bitcast.8, f32[2,32]{1,0:T(2,128)} %dirs_hbm.1, s32[256,128]{1,0:T(8,128)} %bitcast.6, f32[32,32768]{1,0:T(8,128)} %refs_0_.1), custom_call_target="tpu_custom_call" | custom-call | flops 256 | bytes 1024 | tf_op jit(solution)/shard_map/first_sums/pallas_call | solution.py:337
  2.4 3.1 %collective-permute-start.1 = (f32[4,64,128]{2,1,0:T(8,128)S(1)}, f32[4,64,128]{2,1,0:T(8,128)S(1)}, u32[]{:S(2)}, u32[]{:S(2)}) collective-permute-start(f32[4,64,128]{2,1,0:T(8,128)S(1)} %get-tuple-element.23), channel_id=1, source_target_pairs={{0,4},{1,5},{2,6},{3,7},{4,0},{5,1},{6,2},{7,3},{8,12},{9,13},{10,... | collective-permute-start | bytes 393224 | tf_op jit(solution)/shard_map/ppermute | solution.py:385
  5.5 2.1 %near_sums.1 = (f32[4,64,128]{2,1,0:T(8,128)S(1)}, f32[32,8192]{1,0:T(8,128)S(1)}, f32[32,8192]{1,0:T(8,128)S(1)}, f32[32,8192]{1,0:T(8,128)S(1)}) custom-call(f32[32,128]{1,0:T(8,128)S(1)} %get-tuple-element.17.base_ref.refs_1_, f32[2,32,128]{2,1,0:T(8,128)S(1)} %get-tuple-element.18.dirs_ref, s32[256,128]{1,0:T(8,128)S(1)} %get-tuple-element.19.labels_ref, ...), custom_call_target="tpu_custom_call" | custom-call | flops 256 | bytes 1024 | tf_op jit(solution)/shard_map/near_sums/pallas_call | solution.py:368
  7.6 0.1 collective-permute-start
  7.7 0.8 %side_sums.1.refs_0_ = f32[4,64,128]{2,1,0:T(8,128)S(1)} custom-call(f32[32,128]{1,0:T(8,128)S(1)} %get-tuple-element.17.base_ref.refs_1_, f32[2,32,128]{2,1,0:T(8,128)S(1)} %get-tuple-element.18.dirs_ref, s32[256,128]{1,0:T(8,128)S(1)} %get-tuple-element.19.labels_ref, f32[32,8192]{1,0:T(8,128)S(1)} %get-tuple-element.22.refs_0_.refs_3_.even_ref), custom_call_target="tpu_custom_call" | custom-call | flops 256 | bytes 1024 | tf_op jit(solution)/shard_map/side_sums/pallas_call | solution.py:368
  8.4 0.6 %collective-permute-done.1.refs_1_ = f32[4,64,128]{2,1,0:T(8,128)S(1)} collective-permute-done((f32[4,64,128]{2,1,0:T(8,128)S(1)}, f32[4,64,128]{2,1,0:T(8,128)S(1)}, u32[]{:S(2)}, u32[]{:S(2)}) %collective-permute-start.1) | collective-permute-done | bytes 131104 | tf_op jit(solution)/shard_map/ppermute | solution.py:385
  9.0 1.7 %collective-permute-start.2 = (f32[4,64,128]{2,1,0:T(8,128)S(1)}, f32[4,64,128]{2,1,0:T(8,128)S(1)}, u32[]{:S(2)}, u32[]{:S(2)}) collective-permute-start(f32[4,64,128]{2,1,0:T(8,128)S(1)} %merge_pair.1), channel_id=1, source_target_pairs={{0,2},{1,3},{2,0},{3,1},{4,6},{5,7},{6,4},{7,5},{8,10},{9,11},{10,... | collective-permute-start | bytes 393224 | tf_op jit(solution)/shard_map/ppermute | solution.py:385
  10.8 0.8 %own_sums.1.refs_0_ = f32[4,64,128]{2,1,0:T(8,128)S(1)} custom-call(f32[32,128]{1,0:T(8,128)S(1)} %get-tuple-element.17.base_ref.refs_1_, f32[2,32,128]{2,1,0:T(8,128)S(1)} %get-tuple-element.18.dirs_ref, s32[256,128]{1,0:T(8,128)S(1)} %get-tuple-element.19.labels_ref, f32[32,8192]{1,0:T(8,128)S(1)} %get-tuple-element.20.refs_0_.refs_2_), custom_call_target="tpu_custom_call" | custom-call | flops 256 | bytes 1024 | tf_op jit(solution)/shard_map/own_sums/pallas_call | solution.py:368
  11.5 1.1 %collective-permute-done.refs_1_ = f32[4,64,128]{2,1,0:T(8,128)S(1)} collective-permute-done((f32[4,64,128]{2,1,0:T(8,128)S(1)}, f32[4,64,128]{2,1,0:T(8,128)S(1)}, u32[]{:S(2)}, u32[]{:S(2)}) %collective-permute-start) | collective-permute-done | bytes 131104 | tf_op jit(solution)/shard_map/ppermute | solution.py:385
  12.7 1.4 %collective-permute-done.2.refs_1_ = f32[4,64,128]{2,1,0:T(8,128)S(1)} collective-permute-done((f32[4,64,128]{2,1,0:T(8,128)S(1)}, f32[4,64,128]{2,1,0:T(8,128)S(1)}, u32[]{:S(2)}, u32[]{:S(2)}) %collective-permute-start.2) | collective-permute-done | bytes 131104 | tf_op jit(solution)/shard_map/ppermute | solution.py:385
  14.1 2.8 %collective-permute-start.3 = (f32[4,64,128]{2,1,0:T(8,128)S(1)}, f32[4,64,128]{2,1,0:T(8,128)S(1)}, u32[]{:S(2)}, u32[]{:S(2)}) collective-permute-start(f32[4,64,128]{2,1,0:T(8,128)S(1)} %merge_square.1.refs_0_), channel_id=1, source_target_pairs={{0,8},{1,9},{2,10},{3,11},{4,12},{5,13},{6,14},{7,15},{8,0},{9,1},... | collective-permute-start | bytes 393224 | tf_op jit(solution)/shard_map/ppermute | solution.py:385
  16.9 3.4 %collective-permute-done.3.refs_1_ = f32[4,64,128]{2,1,0:T(8,128)S(1)} collective-permute-done((f32[4,64,128]{2,1,0:T(8,128)S(1)}, f32[4,64,128]{2,1,0:T(8,128)S(1)}, u32[]{:S(2)}, u32[]{:S(2)}) %collective-permute-start.3) | collective-permute-done | bytes 131104 | tf_op jit(solution)/shard_map/ppermute | solution.py:385
  20.4 3.0 %collective-permute-start.4 = (f32[4,64,128]{2,1,0:T(8,128)S(1)}, f32[4,64,128]{2,1,0:T(8,128)S(1)}, u32[]{:S(2)}, u32[]{:S(2)}) collective-permute-start(f32[4,64,128]{2,1,0:T(8,128)S(1)} %merge_far.1.refs_0_), channel_id=1, source_target_pairs={{0,6},{1,5},{2,4},{3,7},{4,2},{5,1},{6,0},{7,3},{8,14},{9,13},{10,... | collective-permute-start | bytes 393224 | tf_op jit(solution)/shard_map/ppermute | solution.py:385
  23.3 0.0 collective-permute-start.5
  23.3 0.7 %collective-permute-start.6 = (f32[4,64,128]{2,1,0:T(8,128)S(1)}, f32[4,64,128]{2,1,0:T(8,128)S(1)}, u32[]{:S(2)}, u32[]{:S(2)}) collective-permute-start(f32[4,64,128]{2,1,0:T(8,128)S(1)} %merge_far.1.refs_0_), channel_id=1, source_target_pairs={{0,2},{1,7},{2,0},{3,5},{4,6},{5,3},{6,4},{7,1},{8,10},{9,15},{10,... | collective-permute-start | bytes 393224 | tf_op jit(solution)/shard_map/ppermute | solution.py:385
  24.0 0.6 %tally.1.tally_ref = f32[32,128]{1,0:T(8,128)S(1)} custom-call(s32[256,128]{1,0:T(8,128)S(1)} %get-tuple-element.19.labels_ref), custom_call_target="tpu_custom_call" | custom-call | flops 256 | bytes 1024 | tf_op jit(solution)/shard_map/tally/pallas_call | solution.py:404
  24.6 0.3 %weigh0.1.refs_4_ = f32[3,32,128]{2,1,0:T(8,128)S(1)} custom-call(f32[4,64,128]{2,1,0:T(8,128)S(1)} %merge_far.1.refs_0_, f32[32,128]{1,0:T(8,128)S(1)} %get-tuple-element.17.base_ref.refs_1_, f32[32,8192]{1,0:T(8,128)S(1)} %get-tuple-element.20.refs_0_.refs_2_), custom_call_target="tpu_custom_call" | custom-call | flops 256 | bytes 1024 | tf_op jit(solution)/shard_map/weigh0/pallas_call | solution.py:395
  24.9 1.8 %collective-permute-done.4.refs_0_.refs_1_ = f32[4,64,128]{2,1,0:T(8,128)S(1)} collective-permute-done((f32[4,64,128]{2,1,0:T(8,128)S(1)}, f32[4,64,128]{2,1,0:T(8,128)S(1)}, u32[]{:S(2)}, u32[]{:S(2)}) %collective-permute-start.4) | collective-permute-done | bytes 131104 | tf_op jit(solution)/shard_map/ppermute | solution.py:385
  26.7 0.3 %weigh1.1.refs_4_ = f32[3,32,128]{2,1,0:T(8,128)S(1)} custom-call(f32[4,64,128]{2,1,0:T(8,128)S(1)} %collective-permute-done.4.refs_0_.refs_1_, f32[32,128]{1,0:T(8,128)S(1)} %get-tuple-element.17.base_ref.refs_1_, f32[32,8192]{1,0:T(8,128)S(1)} %get-tuple-element.24.refs_2_.odd_ref, f32[32,8192]{1,0:T(8,128)S(1)} %get-tuple-element.25.refs_3_.refs_2_, ...), custom_call_target="tpu_custom_call" | custom-call | flops 256 | bytes 1024 | tf_op jit(solution)/shard_map/weigh1/pallas_call | solution.py:395
  27.1 1.2 %collective-permute-done.5.refs_0_.refs_2_ = f32[4,64,128]{2,1,0:T(8,128)S(1)} collective-permute-done((f32[4,64,128]{2,1,0:T(8,128)S(1)}, f32[4,64,128]{2,1,0:T(8,128)S(1)}, u32[]{:S(2)}, u32[]{:S(2)}) %collective-permute-start.5) | collective-permute-done | bytes 131104 | tf_op jit(solution)/shard_map/ppermute | solution.py:385
  28.3 0.3 %weigh2.1.before_ref = f32[3,32,128]{2,1,0:T(8,128)S(1)} custom-call(f32[4,64,128]{2,1,0:T(8,128)S(1)} %collective-permute-done.5.refs_0_.refs_2_, f32[32,128]{1,0:T(8,128)S(1)} %get-tuple-element.17.base_ref.refs_1_, f32[32,8192]{1,0:T(8,128)S(1)} %get-tuple-element.25.refs_3_.refs_2_, f32[32,8192]{1,0:T(8,128)S(1)} %get-tuple-element.22.refs_0_.refs_3_.even_ref, ...), custom_call_target="tpu_custom_call" | custom-call | flops 256 | bytes 1024 | tf_op jit(solution)/shard_map/weigh2/pallas_call | solution.py:395
  28.6 0.0 collective-permute-done.6.part_ref.refs_3_
  28.6 0.4 %last_sums.1.refs_4_.mine_ref = f32[3,32]{1,0:T(4,128)S(1)} custom-call(f32[4,64,128]{2,1,0:T(8,128)S(1)} %collective-permute-done.6.part_ref.refs_3_, f32[32,128]{1,0:T(8,128)S(1)} %get-tuple-element.17.base_ref.refs_1_, f32[32,8192]{1,0:T(8,128)S(1)} %get-tuple-element.22.refs_0_.refs_3_.even_ref, f32[32,8192]{1,0:T(8,128)S(1)} %get-tuple-element.24.refs_2_.odd_ref, ...), custom_call_target="tpu_custom_call" | custom-call | flops 256 | bytes 1024 | tf_op jit(solution)/shard_map/last_sums/pallas_call | solution.py:413
  29.1 0.1 collective-permute-start.7
  29.2 0.8 %place.1 = (f32[256,128]{1,0:T(8,128)}, f32[256,128]{1,0:T(8,128)}) custom-call(f32[4,64,128]{2,1,0:T(8,128)S(1)} %merge_far.1.refs_0_, f32[4,64,128]{2,1,0:T(8,128)S(1)} %collective-permute-done.4.refs_0_.refs_1_, f32[4,64,128]{2,1,0:T(8,128)S(1)} %collective-permute-done.5.refs_0_.refs_2_, f32[4,64,128]{2,1,0:T(8,128)S(1)} %collective-permute-done.6.part_ref.refs_3_, ...), custom_call_target="tpu_custom_call" | custom-call | flops 1 | bytes 1024 | tf_op jit(solution)/shard_map/place/pallas_call | solution.py:424
  29.9 0.4 %collective-permute-done.7.other_ref = f32[3,32]{1,0:T(4,128)S(1)} collective-permute-done((f32[3,32]{1,0:T(4,128)S(1)}, f32[3,32]{1,0:T(4,128)S(1)}, u32[]{:S(2)}, u32[]{:S(2)}) %collective-permute-start.7) | collective-permute-done | bytes 416 | tf_op jit(solution)/shard_map/ppermute | solution.py:422
  30.3 0.6 %totals.1 = (f32[1,32]{1,0:T(1,128)}, f32[2,32]{1,0:T(2,128)}) custom-call(f32[3,32]{1,0:T(4,128)S(1)} %last_sums.1.refs_4_.mine_ref, f32[3,32]{1,0:T(4,128)S(1)} %collective-permute-done.7.other_ref), custom_call_target="tpu_custom_call" | custom-call | flops 1 | bytes 1024 | tf_op jit(solution)/shard_map/totals/pallas_call | solution.py:433
  (4 shorter events, 0.1 us)
Async XLA Ops:
  2.4 6.6 %collective-permute-start.1 = (f32[4,64,128]{2,1,0:T(8,128)S(1)}, f32[4,64,128]{2,1,0:T(8,128)S(1)}, u32[]{:S(2)}, u32[]{:S(2)}) collective-permute-start(f32[4,64,128]{2,1,0:T(8,128)S(1)} %get-tuple-element.23), channel_id=1, source_target_pairs={{0,4},{1,5},{2,6},{3,7},{4,0},{5,1},{6,2},{7,3},{8,12},{9,13},{10,... | collective-permute-start | bytes 393224 | tf_op jit(solution)/shard_map/ppermute | solution.py:385
  7.6 5.0 %collective-permute-start = (f32[4,64,128]{2,1,0:T(8,128)S(1)}, f32[4,64,128]{2,1,0:T(8,128)S(1)}, u32[]{:S(2)}, u32[]{:S(2)}) collective-permute-start(f32[4,64,128]{2,1,0:T(8,128)S(1)} %get-tuple-element.21), channel_id=1, source_target_pairs={{0,4},{1,5},{2,6},{3,7},{4,0},{5,1},{6,2},{7,3},{8,12},{9,13},{10,... | collective-permute-start | bytes 393224 | tf_op jit(solution)/shard_map/ppermute | solution.py:385
  9.0 5.0 %collective-permute-start.2 = (f32[4,64,128]{2,1,0:T(8,128)S(1)}, f32[4,64,128]{2,1,0:T(8,128)S(1)}, u32[]{:S(2)}, u32[]{:S(2)}) collective-permute-start(f32[4,64,128]{2,1,0:T(8,128)S(1)} %merge_pair.1), channel_id=1, source_target_pairs={{0,2},{1,3},{2,0},{3,1},{4,6},{5,7},{6,4},{7,5},{8,10},{9,11},{10,... | collective-permute-start | bytes 393224 | tf_op jit(solution)/shard_map/ppermute | solution.py:385
  14.1 6.2 %collective-permute-start.3 = (f32[4,64,128]{2,1,0:T(8,128)S(1)}, f32[4,64,128]{2,1,0:T(8,128)S(1)}, u32[]{:S(2)}, u32[]{:S(2)}) collective-permute-start(f32[4,64,128]{2,1,0:T(8,128)S(1)} %merge_square.1.refs_0_), channel_id=1, source_target_pairs={{0,8},{1,9},{2,10},{3,11},{4,12},{5,13},{6,14},{7,15},{8,0},{9,1},... | collective-permute-start | bytes 393224 | tf_op jit(solution)/shard_map/ppermute | solution.py:385
  20.4 6.4 %collective-permute-start.4 = (f32[4,64,128]{2,1,0:T(8,128)S(1)}, f32[4,64,128]{2,1,0:T(8,128)S(1)}, u32[]{:S(2)}, u32[]{:S(2)}) collective-permute-start(f32[4,64,128]{2,1,0:T(8,128)S(1)} %merge_far.1.refs_0_), channel_id=1, source_target_pairs={{0,6},{1,5},{2,4},{3,7},{4,2},{5,1},{6,0},{7,3},{8,14},{9,13},{10,... | collective-permute-start | bytes 393224 | tf_op jit(solution)/shard_map/ppermute | solution.py:385
  23.3 5.0 %collective-permute-start.5 = (f32[4,64,128]{2,1,0:T(8,128)S(1)}, f32[4,64,128]{2,1,0:T(8,128)S(1)}, u32[]{:S(2)}, u32[]{:S(2)}) collective-permute-start(f32[4,64,128]{2,1,0:T(8,128)S(1)} %merge_far.1.refs_0_), channel_id=1, source_target_pairs={{0,4},{1,3},{2,6},{3,1},{4,0},{5,7},{6,2},{7,5},{8,12},{9,11},{10,... | collective-permute-start | bytes 393224 | tf_op jit(solution)/shard_map/ppermute | solution.py:385
  23.3 5.3 %collective-permute-start.6 = (f32[4,64,128]{2,1,0:T(8,128)S(1)}, f32[4,64,128]{2,1,0:T(8,128)S(1)}, u32[]{:S(2)}, u32[]{:S(2)}) collective-permute-start(f32[4,64,128]{2,1,0:T(8,128)S(1)} %merge_far.1.refs_0_), channel_id=1, source_target_pairs={{0,2},{1,7},{2,0},{3,5},{4,6},{5,3},{6,4},{7,1},{8,10},{9,15},{10,... | collective-permute-start | bytes 393224 | tf_op jit(solution)/shard_map/ppermute | solution.py:385
  29.1 1.2 %collective-permute-start.7 = (f32[3,32]{1,0:T(4,128)S(1)}, f32[3,32]{1,0:T(4,128)S(1)}, u32[]{:S(2)}, u32[]{:S(2)}) collective-permute-start(f32[3,32]{1,0:T(4,128)S(1)} %last_sums.1.refs_4_.mine_ref), channel_id=1, source_target_pairs={{0,1},{1,0},{2,3},{3,2},{4,5},{5,4},{6,7},{7,6},{8,9},{9,8},{10,11... | collective-permute-start | bytes 1160 | tf_op jit(solution)/shard_map/ppermute | solution.py:422

commit v9 on v7

--- a/solution.py
+++ b/solution.py
@@ -304,7 +304,7 @@
     states, samples = energies.shape
     width, cores = lax.axis_size("state"), lax.axis_size("sample")
     near, side, across, stay = 2, 1, 3, 0
-    order, loads = (across, near, side, stay), LOADS
+    order, loads = (across, near, stay, side), LOADS
     rows = samples // 4 // LANES
     work = states * rows * LANES
     labels_in = labels.reshape(samples // LANES, LANES)
@@ -369,14 +369,14 @@
     far = range(2, int(math.log2(width)))
     got_side = send(first, near)
     got_near = send(sums_for(1, "near_sums"), near)
-    pair = merge([sums_for(2, "side_sums"), got_side], False, "merge_pair")
+    pair = merge([sums_for(3, "side_sums"), got_side], False, "merge_pair")
     got_pair = send(pair, side)
-    union = merge([sums_for(3, "own_sums"), got_near], False, "merge_near")
+    union = merge([sums_for(2, "own_sums"), got_near], False, "merge_near")
     union = merge([union, got_pair], not far, "merge_square")
     tally = kernel(tally_body, [VMEM], VMEM, f32(states, LANES), "tally", work)(labels)
     for bit in far:
         union = merge([union, send(union, 1 << bit)], bit == far[-1], "merge_far")
-    ends = [(3, union)] + [(k, send(union, order[k])) for k in range(3)]
+    ends = [(2, union)] + [(k, send(union, order[k])) for k in (0, 1, 3)]
     sums = []
     for k, x in ends[:-1]:
         sums = [weigh_part(k, x, sums, f"weigh{k}")]

time: 31.1 us -> 31.1 us (level)
  no operation moved by 1% of the time
where the time goes in v9:
time: 31.1 us; the launch traced here: 30.9 us
  starting transfers between devices  11.4 us (37%)
  waiting for transfers between devices  9.8 us (32%)
  Pallas kernels  8.98 us (29%)
  between operations  0.72 us (2%)
    ppermute x7, starting transfers between devices, send(): lax.ppermute(x, 'state', [(place, place ^ flip) for place in range(width)])  11.4 us
    ppermute x7, waiting for transfers between devices, send(): lax.ppermute(x, 'state', [(place, place ^ flip) for place in range(width)])  9.44 us
    pallas_call x3, Pallas kernels, sums_for(): kernel(functools.partial(later_body, order[k], more, pieces), [VMEM] * (l...  3.59 us
    pallas_call x1, Pallas kernels, local(): kernel(functools.partial(first_body, order[:loads[0]], pieces), [HBM] * 5...  1.78 us
    pallas_call x3, Pallas kernels, weigh_part(): kernel(weigh_body, [VMEM] * len(args), VMEM, f32(3, states, LANES), name,...  1.09 us
    pallas_call x1, Pallas kernels, local(): kernel(functools.partial(place_body, tuple((order[k] for k, _ in ends))),...  0.77 us
  transfers between devices with their start and end apart: 8, of which 7 were waited for; matrix products, arithmetic and copies ran while one was open for 0% of the time, Pallas kernels for 20%

profile of v9, /device:TPU:0, one launch (start us, length us, event | category | flops | bytes accessed | tf_op | source)
XLA Modules:
  0.0 30.9 jit_solution(16234859644694214955)
XLA Ops:
  0.6 1.8 %first_sums.1 = (f32[4,64,128]{2,1,0:T(8,128)S(1)}, f32[32,128]{1,0:T(8,128)S(1)}, f32[2,32,128]{2,1,0:T(8,128)S(1)}, s32[256,128]{1,0:T(8,128)S(1)}, f32[32,8192]{1,0:T(8,128)S(1)}) custom-call(s32[1,32]{1,0:T(1,128)} %bitcast.7, f32[1,32]{1,0:T(1,128)} %bitcast.8, f32[2,32]{1,0:T(2,128)} %dirs_hbm.1, s32[256,128]{1,0:T(8,128)} %bitcast.6, f32[32,32768]{1,0:T(8,128)} %refs_0_.1), custom_call_target="tpu_custom_call" | custom-call | flops 256 | bytes 1024 | tf_op jit(solution)/shard_map/first_sums/pallas_call | solution.py:316
  2.4 3.1 %collective-permute-start.1 = (f32[4,64,128]{2,1,0:T(8,128)S(1)}, f32[4,64,128]{2,1,0:T(8,128)S(1)}, u32[]{:S(2)}, u32[]{:S(2)}) collective-permute-start(f32[4,64,128]{2,1,0:T(8,128)S(1)} %get-tuple-element.23), channel_id=1, source_target_pairs={{0,4},{2,6},{4,0},{6,2},{8,12},{10,14},{12,8},{14,10},{1,5},{3,7},... | collective-permute-start | bytes 393224 | tf_op jit(solution)/shard_map/ppermute | solution.py:360
  5.5 2.1 %near_sums.1 = (f32[4,64,128]{2,1,0:T(8,128)S(1)}, f32[32,8192]{1,0:T(8,128)S(1)}, f32[32,8192]{1,0:T(8,128)S(1)}, f32[32,8192]{1,0:T(8,128)S(1)}) custom-call(f32[32,128]{1,0:T(8,128)S(1)} %get-tuple-element.17.base_ref, f32[2,32,128]{2,1,0:T(8,128)S(1)} %get-tuple-element.18.dirs_ref, s32[256,128]{1,0:T(8,128)S(1)} %get-tuple-element.19.labels_ref, ...), custom_call_target="tpu_custom_call" | custom-call | flops 256 | bytes 1024 | tf_op jit(solution)/shard_map/near_sums/pallas_call | solution.py:347
  7.6 0.1 collective-permute-start
  7.7 0.8 %side_sums.1.refs_0_ = f32[4,64,128]{2,1,0:T(8,128)S(1)} custom-call(f32[32,128]{1,0:T(8,128)S(1)} %get-tuple-element.17.base_ref, f32[2,32,128]{2,1,0:T(8,128)S(1)} %get-tuple-element.18.dirs_ref, s32[256,128]{1,0:T(8,128)S(1)} %get-tuple-element.19.labels_ref, f32[32,8192]{1,0:T(8,128)S(1)} %get-tuple-element.22.refs_0_.energies_ref), custom_call_target="tpu_custom_call" | custom-call | flops 256 | bytes 1024 | tf_op jit(solution)/shard_map/side_sums/pallas_call | solution.py:347
  8.4 0.6 %collective-permute-done.1.refs_1_ = f32[4,64,128]{2,1,0:T(8,128)S(1)} collective-permute-done((f32[4,64,128]{2,1,0:T(8,128)S(1)}, f32[4,64,128]{2,1,0:T(8,128)S(1)}, u32[]{:S(2)}, u32[]{:S(2)}) %collective-permute-start.1) | collective-permute-done | bytes 131104 | tf_op jit(solution)/shard_map/ppermute | solution.py:360
  9.0 1.7 %collective-permute-start.2 = (f32[4,64,128]{2,1,0:T(8,128)S(1)}, f32[4,64,128]{2,1,0:T(8,128)S(1)}, u32[]{:S(2)}, u32[]{:S(2)}) collective-permute-start(f32[4,64,128]{2,1,0:T(8,128)S(1)} %merge_pair.1), channel_id=1, source_target_pairs={{0,2},{2,0},{4,6},{6,4},{8,10},{10,8},{12,14},{14,12},{1,3},{3,1},... | collective-permute-start | bytes 393224 | tf_op jit(solution)/shard_map/ppermute | solution.py:360
  10.8 0.8 %own_sums.1.refs_0_ = f32[4,64,128]{2,1,0:T(8,128)S(1)} custom-call(f32[32,128]{1,0:T(8,128)S(1)} %get-tuple-element.17.base_ref, f32[2,32,128]{2,1,0:T(8,128)S(1)} %get-tuple-element.18.dirs_ref, s32[256,128]{1,0:T(8,128)S(1)} %get-tuple-element.19.labels_ref, f32[32,8192]{1,0:T(8,128)S(1)} %get-tuple-element.20.refs_0_.energies_ref), custom_call_target="tpu_custom_call" | custom-call | flops 256 | bytes 1024 | tf_op jit(solution)/shard_map/own_sums/pallas_call | solution.py:347
  11.5 1.1 %collective-permute-done.refs_1_ = f32[4,64,128]{2,1,0:T(8,128)S(1)} collective-permute-done((f32[4,64,128]{2,1,0:T(8,128)S(1)}, f32[4,64,128]{2,1,0:T(8,128)S(1)}, u32[]{:S(2)}, u32[]{:S(2)}) %collective-permute-start) | collective-permute-done | bytes 131104 | tf_op jit(solution)/shard_map/ppermute | solution.py:360
  12.7 1.4 %collective-permute-done.2.refs_1_ = f32[4,64,128]{2,1,0:T(8,128)S(1)} collective-permute-done((f32[4,64,128]{2,1,0:T(8,128)S(1)}, f32[4,64,128]{2,1,0:T(8,128)S(1)}, u32[]{:S(2)}, u32[]{:S(2)}) %collective-permute-start.2) | collective-permute-done | bytes 131104 | tf_op jit(solution)/shard_map/ppermute | solution.py:360
  14.1 2.8 %collective-permute-start.3 = (f32[4,64,128]{2,1,0:T(8,128)S(1)}, f32[4,64,128]{2,1,0:T(8,128)S(1)}, u32[]{:S(2)}, u32[]{:S(2)}) collective-permute-start(f32[4,64,128]{2,1,0:T(8,128)S(1)} %merge_square.1.refs_0_), channel_id=1, source_target_pairs={{0,8},{2,10},{4,12},{6,14},{8,0},{10,2},{12,4},{14,6},{1,9},{3,11}... | collective-permute-start | bytes 393224 | tf_op jit(solution)/shard_map/ppermute | solution.py:360
  16.9 3.4 %collective-permute-done.3.refs_1_ = f32[4,64,128]{2,1,0:T(8,128)S(1)} collective-permute-done((f32[4,64,128]{2,1,0:T(8,128)S(1)}, f32[4,64,128]{2,1,0:T(8,128)S(1)}, u32[]{:S(2)}, u32[]{:S(2)}) %collective-permute-start.3) | collective-permute-done | bytes 131104 | tf_op jit(solution)/shard_map/ppermute | solution.py:360
  20.3 3.0 %collective-permute-start.4 = (f32[4,64,128]{2,1,0:T(8,128)S(1)}, f32[4,64,128]{2,1,0:T(8,128)S(1)}, u32[]{:S(2)}, u32[]{:S(2)}) collective-permute-start(f32[4,64,128]{2,1,0:T(8,128)S(1)} %merge_far.1.part_ref.refs_0_), channel_id=1, source_target_pairs={{0,6},{2,4},{4,2},{6,0},{8,14},{10,12},{12,10},{14,8},{1,7},{3,5},... | collective-permute-start | bytes 393224 | tf_op jit(solution)/shard_map/ppermute | solution.py:360
  23.3 0.0 collective-permute-start.5
  23.3 0.7 %collective-permute-start.6 = (f32[4,64,128]{2,1,0:T(8,128)S(1)}, f32[4,64,128]{2,1,0:T(8,128)S(1)}, u32[]{:S(2)}, u32[]{:S(2)}) collective-permute-start(f32[4,64,128]{2,1,0:T(8,128)S(1)} %merge_far.1.part_ref.refs_0_), channel_id=1, source_target_pairs={{0,2},{2,0},{4,6},{6,4},{8,10},{10,8},{12,14},{14,12},{1,3},{3,1},... | collective-permute-start | bytes 393224 | tf_op jit(solution)/shard_map/ppermute | solution.py:360
  24.0 0.6 %tally.1.tally_ref = f32[32,128]{1,0:T(8,128)S(1)} custom-call(s32[256,128]{1,0:T(8,128)S(1)} %get-tuple-element.19.labels_ref), custom_call_target="tpu_custom_call" | custom-call | flops 256 | bytes 1024 | tf_op jit(solution)/shard_map/tally/pallas_call | solution.py:376
  24.6 0.4 %weigh2.1.refs_0_ = f32[3,32,128]{2,1,0:T(8,128)S(1)} custom-call(f32[4,64,128]{2,1,0:T(8,128)S(1)} %merge_far.1.part_ref.refs_0_, f32[32,128]{1,0:T(8,128)S(1)} %get-tuple-element.17.base_ref, f32[32,8192]{1,0:T(8,128)S(1)} %get-tuple-element.20.refs_0_.energies_ref), custom_call_target="tpu_custom_call" | custom-call | flops 256 | bytes 1024 | tf_op jit(solution)/shard_map/weigh2/pallas_call | solution.py:364
  24.9 2.1 %collective-permute-done.4.part_ref.refs_1_ = f32[4,64,128]{2,1,0:T(8,128)S(1)} collective-permute-done((f32[4,64,128]{2,1,0:T(8,128)S(1)}, f32[4,64,128]{2,1,0:T(8,128)S(1)}, u32[]{:S(2)}, u32[]{:S(2)}) %collective-permute-start.4) | collective-permute-done | bytes 131104 | tf_op jit(solution)/shard_map/ppermute | solution.py:360
  27.0 0.4 %weigh0.1.refs_0_ = f32[3,32,128]{2,1,0:T(8,128)S(1)} custom-call(f32[4,64,128]{2,1,0:T(8,128)S(1)} %collective-permute-done.4.part_ref.refs_1_, f32[32,128]{1,0:T(8,128)S(1)} %get-tuple-element.17.base_ref, f32[32,8192]{1,0:T(8,128)S(1)} %get-tuple-element.25.energies_ref, f32[3,32,128]{2,1,0:T(8,128)S(1)} %weigh2.1.refs_0_), custom_call_target="tpu_custom_call" | custom-call | flops 256 | bytes 1024 | tf_op jit(solution)/shard_map/weigh0/pallas_call | solution.py:364
  27.4 0.9 %collective-permute-done.5.part_ref.refs_2_ = f32[4,64,128]{2,1,0:T(8,128)S(1)} collective-permute-done((f32[4,64,128]{2,1,0:T(8,128)S(1)}, f32[4,64,128]{2,1,0:T(8,128)S(1)}, u32[]{:S(2)}, u32[]{:S(2)}) %collective-permute-start.5) | collective-permute-done | bytes 131104 | tf_op jit(solution)/shard_map/ppermute | solution.py:360
  28.3 0.4 %weigh1.1.before_ref = f32[3,32,128]{2,1,0:T(8,128)S(1)} custom-call(f32[4,64,128]{2,1,0:T(8,128)S(1)} %collective-permute-done.5.part_ref.refs_2_, f32[32,128]{1,0:T(8,128)S(1)} %get-tuple-element.17.base_ref, f32[32,8192]{1,0:T(8,128)S(1)} %get-tuple-element.24.energies_ref, f32[3,32,128]{2,1,0:T(8,128)S(1)} %weigh0.1.refs_0_), custom_call_target="tpu_custom_call" | custom-call | flops 256 | bytes 1024 | tf_op jit(solution)/shard_map/weigh1/pallas_call | solution.py:364
  28.6 0.0 collective-permute-done.6.part_ref.refs_3_
  28.7 0.5 %last_sums.1.refs_4_.mine_ref = f32[3,32]{1,0:T(4,128)S(1)} custom-call(f32[4,64,128]{2,1,0:T(8,128)S(1)} %collective-permute-done.6.part_ref.refs_3_, f32[32,128]{1,0:T(8,128)S(1)} %get-tuple-element.17.base_ref, f32[32,8192]{1,0:T(8,128)S(1)} %get-tuple-element.22.refs_0_.energies_ref, f32[2,32,128]{2,1,0:T(8,128)S(1)} %get-tuple-element.18.dirs_ref, ...), custom_call_target="tpu_custom_call" | custom-call | flops 256 | bytes 1024 | tf_op jit(solution)/shard_map/last_sums/pallas_call | solution.py:384
  29.1 0.1 collective-permute-start.7
  29.2 0.8 %place.1 = (f32[256,128]{1,0:T(8,128)}, f32[256,128]{1,0:T(8,128)}) custom-call(f32[4,64,128]{2,1,0:T(8,128)S(1)} %merge_far.1.part_ref.refs_0_, f32[4,64,128]{2,1,0:T(8,128)S(1)} %collective-permute-done.4.part_ref.refs_1_, f32[4,64,128]{2,1,0:T(8,128)S(1)} %collective-permute-done.5.part_ref.refs_2_, ...), custom_call_target="tpu_custom_call" | custom-call | flops 1 | bytes 1024 | tf_op jit(solution)/shard_map/place/pallas_call | solution.py:389
  30.0 0.4 %collective-permute-done.7.other_ref = f32[3,32]{1,0:T(4,128)S(1)} collective-permute-done((f32[3,32]{1,0:T(4,128)S(1)}, f32[3,32]{1,0:T(4,128)S(1)}, u32[]{:S(2)}, u32[]{:S(2)}) %collective-permute-start.7) | collective-permute-done | bytes 416 | tf_op jit(solution)/shard_map/ppermute | solution.py:387
  30.3 0.6 %totals.1 = (f32[1,32]{1,0:T(1,128)}, f32[2,32]{1,0:T(2,128)}) custom-call(f32[3,32]{1,0:T(4,128)S(1)} %last_sums.1.refs_4_.mine_ref, f32[3,32]{1,0:T(4,128)S(1)} %collective-permute-done.7.other_ref), custom_call_target="tpu_custom_call" | custom-call | flops 1 | bytes 1024 | tf_op jit(solution)/shard_map/totals/pallas_call | solution.py:398
  (4 shorter events, 0.1 us)
Async XLA Ops:
  2.4 6.6 %collective-permute-start.1 = (f32[4,64,128]{2,1,0:T(8,128)S(1)}, f32[4,64,128]{2,1,0:T(8,128)S(1)}, u32[]{:S(2)}, u32[]{:S(2)}) collective-permute-start(f32[4,64,128]{2,1,0:T(8,128)S(1)} %get-tuple-element.23), channel_id=1, source_target_pairs={{0,4},{2,6},{4,0},{6,2},{8,12},{10,14},{12,8},{14,10},{1,5},{3,7},... | collective-permute-start | bytes 393224 | tf_op jit(solution)/shard_map/ppermute | solution.py:360
  7.6 5.0 %collective-permute-start = (f32[4,64,128]{2,1,0:T(8,128)S(1)}, f32[4,64,128]{2,1,0:T(8,128)S(1)}, u32[]{:S(2)}, u32[]{:S(2)}) collective-permute-start(f32[4,64,128]{2,1,0:T(8,128)S(1)} %get-tuple-element.21), channel_id=1, source_target_pairs={{0,4},{2,6},{4,0},{6,2},{8,12},{10,14},{12,8},{14,10},{1,5},{3,7},... | collective-permute-start | bytes 393224 | tf_op jit(solution)/shard_map/ppermute | solution.py:360
  9.0 5.0 %collective-permute-start.2 = (f32[4,64,128]{2,1,0:T(8,128)S(1)}, f32[4,64,128]{2,1,0:T(8,128)S(1)}, u32[]{:S(2)}, u32[]{:S(2)}) collective-permute-start(f32[4,64,128]{2,1,0:T(8,128)S(1)} %merge_pair.1), channel_id=1, source_target_pairs={{0,2},{2,0},{4,6},{6,4},{8,10},{10,8},{12,14},{14,12},{1,3},{3,1},... | collective-permute-start | bytes 393224 | tf_op jit(solution)/shard_map/ppermute | solution.py:360
  14.1 6.2 %collective-permute-start.3 = (f32[4,64,128]{2,1,0:T(8,128)S(1)}, f32[4,64,128]{2,1,0:T(8,128)S(1)}, u32[]{:S(2)}, u32[]{:S(2)}) collective-permute-start(f32[4,64,128]{2,1,0:T(8,128)S(1)} %merge_square.1.refs_0_), channel_id=1, source_target_pairs={{0,8},{2,10},{4,12},{6,14},{8,0},{10,2},{12,4},{14,6},{1,9},{3,11}... | collective-permute-start | bytes 393224 | tf_op jit(solution)/shard_map/ppermute | solution.py:360
  20.3 6.7 %collective-permute-start.4 = (f32[4,64,128]{2,1,0:T(8,128)S(1)}, f32[4,64,128]{2,1,0:T(8,128)S(1)}, u32[]{:S(2)}, u32[]{:S(2)}) collective-permute-start(f32[4,64,128]{2,1,0:T(8,128)S(1)} %merge_far.1.part_ref.refs_0_), channel_id=1, source_target_pairs={{0,6},{2,4},{4,2},{6,0},{8,14},{10,12},{12,10},{14,8},{1,7},{3,5},... | collective-permute-start | bytes 393224 | tf_op jit(solution)/shard_map/ppermute | solution.py:360
  23.3 5.0 %collective-permute-start.5 = (f32[4,64,128]{2,1,0:T(8,128)S(1)}, f32[4,64,128]{2,1,0:T(8,128)S(1)}, u32[]{:S(2)}, u32[]{:S(2)}) collective-permute-start(f32[4,64,128]{2,1,0:T(8,128)S(1)} %merge_far.1.part_ref.refs_0_), channel_id=1, source_target_pairs={{0,4},{2,6},{4,0},{6,2},{8,12},{10,14},{12,8},{14,10},{1,5},{3,7},... | collective-permute-start | bytes 393224 | tf_op jit(solution)/shard_map/ppermute | solution.py:360
  23.3 5.3 %collective-permute-start.6 = (f32[4,64,128]{2,1,0:T(8,128)S(1)}, f32[4,64,128]{2,1,0:T(8,128)S(1)}, u32[]{:S(2)}, u32[]{:S(2)}) collective-permute-start(f32[4,64,128]{2,1,0:T(8,128)S(1)} %merge_far.1.part_ref.refs_0_), channel_id=1, source_target_pairs={{0,2},{2,0},{4,6},{6,4},{8,10},{10,8},{12,14},{14,12},{1,3},{3,1},... | collective-permute-start | bytes 393224 | tf_op jit(solution)/shard_map/ppermute | solution.py:360
  29.1 1.2 %collective-permute-start.7 = (f32[3,32]{1,0:T(4,128)S(1)}, f32[3,32]{1,0:T(4,128)S(1)}, u32[]{:S(2)}, u32[]{:S(2)}) collective-permute-start(f32[3,32]{1,0:T(4,128)S(1)} %last_sums.1.refs_4_.mine_ref), channel_id=1, source_target_pairs={{0,1},{1,0},{2,3},{3,2},{4,5},{5,4},{6,7},{7,6},{8,9},{9,8},{10,11... | collective-permute-start | bytes 1160 | tf_op jit(solution)/shard_map/ppermute | solution.py:387
